TPU v7x, 256 devices: a whole 4x4x8 slice. The times are simulated.
256 devices in a mesh: dp: 8 (over x, core), seq: 32 (over y, z).
Axes of the slice: x: 4, y: 4, z: 8, core: 2. Of those that a mesh axis runs over, the one named last changes fastest.
Arguments:
- hidden: bfloat16 [8, 4096, 2560], P('dp', 'seq'), may hold values from -6 to 6
- b_proj: bfloat16 [8, 4096, 128], P('dp', 'seq'), may hold values from -2 to 2
- c_proj: bfloat16 [8, 4096, 128], P('dp', 'seq'), may hold values from -2 to 2
- dt_raw: float32 [8, 4096, 40], P('dp', 'seq'), may hold values from -3 to 3
- base_ids: int32 [8, 4096], P('dp', 'seq'), may hold values from 0 to 11
- complement: int32 [12], replicated, may hold values from 0 to 11, each once
- a_log: float32 [40], replicated, may hold values from -20 to 0
- d_skip: float32 [40], replicated, may hold values from 0.5 to 1.5
- dt_bias: float32 [40], replicated, may hold values from -1 to 0.5
- base_shift: float32 [12, 40], replicated, may hold values from -2.5 to 2.5
- conv_w: float32 [4, 2560], replicated, may hold values from -3 to 3
- conv_b: float32 [2560], replicated, may hold values from -2 to 2
- grad_out: bfloat16 [8, 4096, 2560], P('dp', 'seq'), may hold values from -6 to 6
Outputs:
- layer_out: bfloat16 [8, 4096, 2560], P('dp', 'seq')
- d_hidden: bfloat16 [8, 4096, 2560], P('dp', 'seq')
- d_b_proj: float32 [8, 4096, 128], P('dp', 'seq')
- d_c_proj: float32 [8, 4096, 128], P('dp', 'seq')
- d_dt_raw: float32 [8, 4096, 40], P('dp', 'seq')
- d_a_log: float32 [40], replicated
- d_d_skip: float32 [40], replicated
- d_dt_bias: float32 [40], replicated
- d_base_shift: float32 [12, 40], replicated
- d_conv_w: float32 [4, 2560], replicated
- d_conv_b: float32 [2560], replicated
Inputs may be any that keep to these rules, and one draw needn't show every extreme that they name: `complement`: every id appears once.
All inputs are finite; a program needn't handle non-finite values.
Results may differ from a plain program's by a relative error of at most 0.0015.
Values may be sent and summed in bfloat16 or wider, within the bound.
No kernel may reach another device: no remote copies, remote signals or barrier semaphores. Data moves between devices by JAX's collectives and lax.ppermute only.
A program may use at most 384 MiB of HBM per device.

v0:
```python
import jax
import jax.numpy as jnp
from jax import lax
from jax.sharding import PartitionSpec as P

exact_prec = lax.Precision.HIGHEST


def with_halo(array, sides, width):
    for axis, dim in sides:
        devices, length = (lax.axis_size(axis), array.shape[dim])
        up = [(i, (i + 1) % devices) for i in range(devices - 1)]
        down = [(j, i) for i, j in up]
        last = lax.slice_in_dim(array, length - width, length, axis=dim)
        leading = lax.slice_in_dim(array, 0, width, axis=dim)
        before = lax.ppermute(last, axis, up)
        after = lax.ppermute(leading, axis, down)
        array = jnp.concatenate([before, array, after], axis=dim)
    return array


def prefix(value, axis, join, neutral, backward):
    count, mine = (lax.axis_size(axis), lax.axis_index(axis))
    pieces = jax.tree.map(lambda part: lax.all_gather(part, axis), value)
    if backward:
        pieces = jax.tree.map(lambda part: part[::-1], pieces)
        mine = count - 1 - mine
    running = jax.tree.map(
        lambda part, zero: jnp.full_like(part, 0) + jnp.asarray(zero, part.dtype), value, neutral
    )

    def hop(position, running):
        longer = join(running, jax.tree.map(lambda part: part[position], pieces))
        return jax.tree.map(lambda new, old: jnp.where(position < mine, new, old), longer, running)

    return lax.fori_loop(0, count - 1, hop, running)


def shifted_2(array, axis, by):
    devices = lax.axis_size(axis)
    pairs = [(i, i + by) for i in range(devices) if 0 <= i + by < devices]
    return lax.ppermute(array, axis, pairs)


def section_one(
    window, b_part, c_part, dt_part, onehot, a_log, d_skip, dt_bias, base_shift, conv_w, conv_b
):
    rows_here = b_part.shape[0]
    head_count = a_log.shape[0]
    pre_act = (
        conv_b
        + conv_w[0] * window[3 : 3 + rows_here]
        + conv_w[1] * window[2 : 2 + rows_here]
        + conv_w[2] * window[1 : 1 + rows_here]
        + conv_w[3] * window[0:rows_here]
    )
    conv_out = jax.nn.silu(pre_act)
    shifted = jnp.dot(onehot, base_shift, precision=exact_prec)
    step_size = jax.nn.softplus(dt_part + dt_bias + shifted)
    log_decay = -jnp.exp(a_log) * step_size
    cumul = jnp.cumsum(log_decay, axis=0)
    values = conv_out.reshape(rows_here, head_count, -1)
    scores = jnp.dot(c_part, b_part.T, precision=exact_prec)
    lower_mask = jnp.arange(rows_here)[:, None] >= jnp.arange(rows_here)[None, :]
    gap_logs = jnp.where(lower_mask[:, :, None], cumul[:, None, :] - cumul[None, :, :], -jnp.inf)
    weights = scores[:, :, None] * jnp.exp(gap_logs) * step_size[None, :, :]
    inner_out = jnp.einsum("tsh,shp->thp", weights, values, precision=exact_prec)
    local_out = (inner_out + d_skip[None, :, None] * values).reshape(rows_here, -1)
    tail_weight = jnp.exp(cumul[-1][None, :] - cumul) * step_size
    scaled_values = values * tail_weight[:, :, None]
    state_out = jnp.einsum("shp,sn->hpn", scaled_values, b_part, precision=exact_prec)
    return (local_out, state_out, jnp.exp(cumul[-1]), cumul)


def incoming(cumul, c_part, start_state):
    rows_here = c_part.shape[0]
    reached = jnp.einsum("tn,hpn->thp", c_part, start_state, precision=exact_prec)
    return (jnp.exp(cumul)[:, :, None] * reached).reshape(rows_here, -1)


def chain_link(earlier, later):
    return (later[1][:, None, None] * earlier[0] + later[0], earlier[1] * later[1])


def state_pull(cumul, c_part, grad_rows):
    rows_here, head_count = cumul.shape
    grad_heads = grad_rows.reshape(rows_here, head_count, -1) * jnp.exp(cumul)[:, :, None]
    return jnp.einsum("thp,tn->hpn", grad_heads, c_part, precision=exact_prec)


def finish(pullback, cumul, c_part, grad_rows, start_state, later_grad):
    rows_here, head_count = cumul.shape
    grad_heads = grad_rows.reshape(rows_here, head_count, -1)
    growth = jnp.exp(cumul)
    d_total = jnp.einsum("hpn,hpn->h", later_grad, start_state, precision=exact_prec)
    reached = jnp.einsum("thp,hpn->thn", grad_heads, start_state, precision=exact_prec)
    d_cumul = growth * jnp.einsum("thn,tn->th", reached, c_part, precision=exact_prec)
    extra_c = jnp.einsum("th,thn->tn", growth, reached, precision=exact_prec)
    gradients = pullback((grad_rows, later_grad, d_total, d_cumul))
    return (gradients, extra_c)


def per_device(
    hidden,
    b_proj,
    c_proj,
    dt_raw,
    base_ids,
    complement,
    a_log,
    d_skip,
    dt_bias,
    base_shift,
    conv_w,
    conv_b,
    grad_out,
):
    rows_here = hidden.shape[1]
    padded = with_halo(hidden, (("seq", 1),), 3)[0].astype(jnp.float32)
    b_rows = b_proj[0].astype(jnp.float32)
    c_rows = c_proj[0].astype(jnp.float32)
    dt_rows = dt_raw[0]
    code_ids = jnp.arange(base_shift.shape[0], dtype=jnp.int32)
    matches = base_ids[0][:, None] == code_ids[None, :]
    onehot_fwd = matches.astype(jnp.float32)
    partner = jnp.sum(jnp.where(matches, complement[None, :], 0), axis=1)
    onehot_rev = (partner[:, None] == code_ids[None, :]).astype(jnp.float32)[::-1]
    param_set = (a_log, d_skip, dt_bias, base_shift, conv_w, conv_b)

    def local_forward(window, b_in, c_in, dt_in, params_in):
        return section_one(window, b_in, c_in, dt_in, onehot_fwd, *params_in)

    def local_reverse(window, b_in, c_in, dt_in, params_in):
        return section_one(window, b_in, c_in, dt_in, onehot_rev, *params_in)

    c_flip = c_rows[::-1]
    out_fwd, pull_fwd = jax.vjp(
        local_forward, padded[: rows_here + 3], b_rows, c_rows, dt_rows, param_set
    )
    out_rev, pull_rev = jax.vjp(
        local_reverse, padded[3:][::-1], b_rows[::-1], c_flip, dt_rows[::-1], param_set
    )
    neutral = (jnp.zeros_like(out_fwd[1]), jnp.ones_like(out_fwd[2]))
    grad_rows = grad_out[0].astype(jnp.float32)
    grad_flip = grad_rows[::-1]
    pulled_fwd = state_pull(out_fwd[3], c_rows, grad_rows)
    pulled_rev = state_pull(out_rev[3], c_flip, grad_flip)
    start_fwd = prefix((out_fwd[1], out_fwd[2]), "seq", chain_link, neutral, False)[0]
    start_rev = prefix((out_rev[1], out_rev[2]), "seq", chain_link, neutral, True)[0]
    later_fwd = prefix((pulled_fwd, out_fwd[2]), "seq", chain_link, neutral, True)[0]
    later_rev = prefix((pulled_rev, out_rev[2]), "seq", chain_link, neutral, False)[0]
    mixed_fwd = out_fwd[0] + incoming(out_fwd[3], c_rows, start_fwd)
    mixed_rev = out_rev[0] + incoming(out_rev[3], c_flip, start_rev)
    layer_out = (mixed_fwd + mixed_rev[::-1]).astype(jnp.bfloat16)
    grads_fwd, extra_fwd = finish(pull_fwd, out_fwd[3], c_rows, grad_rows, start_fwd, later_fwd)
    grads_rev, extra_rev = finish(pull_rev, out_rev[3], c_flip, grad_flip, start_rev, later_rev)
    spread = jnp.pad(grads_fwd[0], ((0, 3), (0, 0))) + jnp.pad(grads_rev[0][::-1], ((3, 0), (0, 0)))
    from_next = shifted_2(spread[:3], "seq", -1)
    from_prev = shifted_2(spread[rows_here + 3 :], "seq", 1)
    own_rows = (
        spread[3 : rows_here + 3]
        + jnp.pad(from_next, ((rows_here - 3, 0), (0, 0)))
        + jnp.pad(from_prev, ((0, rows_here - 3), (0, 0)))
    )
    d_b_proj = grads_fwd[1] + grads_rev[1][::-1]
    d_c_proj = grads_fwd[2] + extra_fwd + (grads_rev[2] + extra_rev)[::-1]
    d_dt_raw = grads_fwd[3] + grads_rev[3][::-1]
    params_fwd = grads_fwd[4]
    params_rev = grads_rev[4]
    summed = lax.psum(
        (
            params_fwd[0] + params_rev[0],
            params_fwd[1] + params_rev[1],
            params_fwd[2] + params_rev[2],
            params_fwd[3] + params_rev[3],
            params_fwd[4] + params_rev[4],
            params_fwd[5] + params_rev[5],
        ),
        ("dp", "seq"),
    )
    return (
        layer_out[None],
        own_rows.astype(jnp.bfloat16)[None],
        d_b_proj[None],
        d_c_proj[None],
        d_dt_raw[None],
        summed[0],
        summed[1],
        summed[2],
        summed[3],
        summed[4],
        summed[5],
    )


def solution(mesh):
    placed = (
        P("dp", "seq", None),
        P("dp", "seq", None),
        P("dp", "seq", None),
        P("dp", "seq", None),
        P("dp", "seq"),
        P(),
        P(),
        P(),
        P(),
        P(),
        P(),
        P(),
        P("dp", "seq", None),
    )
    return jax.shard_map(
        per_device,
        mesh=mesh,
        in_specs=placed,
        out_specs=(
            P("dp", "seq", None),
            P("dp", "seq", None),
            P("dp", "seq", None),
            P("dp", "seq", None),
            P("dp", "seq", None),
            P(),
            P(),
            P(),
            P(),
            P(),
            P(),
        ),
        check_vma=False,
    )
```

profile of v0, /device:TPU:6, one launch (start us, length us, event | category | flops | bytes accessed | tf_op | source)
XLA Modules:
  0.0 1495.3 jit_solution(14055351527248711225)
XLA Ops:
  24.7 4.4 collective-permute-start
  35.7 45.7 %all-gather.4 = f32[32,1,40]{2,1,0:T(1,128)} all-gather(f32[1,1,40]{2,1,0:T(1,128)} %get-tuple-element.607), channel_id=1, replica_groups=mesh['dp'=8,'seq'=32] {'seq'}, dimensions={0}, use_global_device_ids=true | all-gather | bytes 5280 | tf_op jit(solution)/shard_map/all_gather | solution.py:24
  82.8 39.4 %all-gather.5 = f32[32,1,40]{2,1,0:T(1,128)} all-gather(f32[1,1,40]{2,1,0:T(1,128)S(1)} %get-tuple-element.605), channel_id=1, replica_groups=mesh['dp'=8,'seq'=32] {'seq'}, dimensions={0}, use_global_device_ids=true | all-gather | bytes 5280 | tf_op jit(solution)/shard_map/all_gather | solution.py:24
  128.1 3.7 slice_bitcast_fusion
  131.9 11.4 slice.119
  143.2 11.2 slice.122
  154.5 11.3 slice.125
  165.7 11.2 slice.128
  176.9 128.0 %all-gather.17.cloned.1.call-done = f32[1280,64,128]{2,1,0:T(8,128)} async-done(((f32[40,64,128]{2,1,0:T(8,128)}), f32[1280,64,128]{2,1,0:T(8,128)}) %all-gather.17.cloned.1.call-update) | async-done | bytes 41943056 | tf_op jit(solution)/shard_map/all_gather | solution.py:24
  304.9 72.4 %while.59 = (s32[]{:T(128)}, f32[40,64,128]{2,1,0:T(8,128)S(1)}, s32[]{:T(128)}, f32[32,40]{1,0:T(8,128)}, f32[32,40,64,128]{3,2,1,0:T(8,128)}, /*index=5*/s32[]{:T(128)}, s32[]{:T(128)}) while((s32[]{:T(128)}, f32[40,64,128]{2,1,0:T(8,128)S(1)}, s32[]{:T(128)}, f32[32,40]{1,0:T(8,128)}, f32[32,40,64,128]{3,2,1,0:T(8,128)}, ...), condition=%wide.region_10.12_spmd.clone, body=%wide.region_9.11_spmd.clone.sunk | while | flops 1310724 | bytes 3932745 | solution.py:36
  379.6 207.8 %all-gather.15.cloned.1.call-done = f32[1280,64,128]{2,1,0:T(8,128)} async-done(((f32[40,64,128]{2,1,0:T(8,128)}), f32[1280,64,128]{2,1,0:T(8,128)}) %all-gather.15.cloned.1.call-update) | async-done | bytes 41943056 | tf_op jit(solution)/shard_map/all_gather | solution.py:24
  587.4 29.2 %rev.51 = f32[32,40,64,128]{3,2,1,0:T(8,128)} reverse(f32[32,40,64,128]{3,2,1,0:T(8,128)} %bitcast.303), dimensions={0} | reverse | bytes 83886080 | tf_op jit(solution)/shard_map/rev | solution.py:26
  616.6 71.8 %while.58 = (s32[]{:T(128)}, f32[40,64,128]{2,1,0:T(8,128)S(1)}, s32[]{:T(128)}, f32[32,40]{1,0:T(8,128)}, f32[32,40,64,128]{3,2,1,0:T(8,128)}, /*index=5*/s32[]{:T(128)}, s32[]{:T(128)}) while((s32[]{:T(128)}, f32[40,64,128]{2,1,0:T(8,128)S(1)}, s32[]{:T(128)}, f32[32,40]{1,0:T(8,128)}, f32[32,40,64,128]{3,2,1,0:T(8,128)}, ...), condition=%wide.region_8.10_spmd.clone, body=%wide.region_7.9_spmd.clone.sunk | while | flops 1310724 | bytes 3932745 | solution.py:36
  691.2 4.1 fusion.42
  697.8 8.4 fusion.146
  729.8 3.7 fusion.97
  735.3 9.2 fusion.25
  747.5 4.2 broadcast_multiply_fusion
  751.7 6.5 pad_add_fusion
  758.2 21.9 %reverse.4 = f32[256,2560]{0,1:T(8,128)} reverse(f32[256,2560]{0,1:T(8,128)} %bitcast.322), dimensions={0} | reverse | bytes 5242880
  791.4 5.6 collective-permute-start.3
  797.0 4.0 fusion.100
  805.4 6.4 fusion.45
  811.9 6.4 fusion.48
  835.0 5.1 fusion.112
  842.3 148.1 %all-gather.11.cloned.1.call-done = f32[1280,64,128]{2,1,0:T(8,128)} async-done(((f32[40,64,128]{2,1,0:T(8,128)}), f32[1280,64,128]{2,1,0:T(8,128)}) %all-gather.11.cloned.1.call-update) | async-done | bytes 41943056 | tf_op jit(solution)/shard_map/all_gather | solution.py:24
  990.3 130.5 %while.56 = (s32[]{:T(128)}, f32[40,64,128]{2,1,0:T(8,128)}, s32[]{:T(128)}, f32[32,40]{1,0:T(8,128)}, f32[32,40,64,128]{3,2,1,0:T(8,128)}, /*index=5*/s32[]{:T(128)}, s32[]{:T(128)}) while((s32[]{:T(128)}, f32[40,64,128]{2,1,0:T(8,128)}, s32[]{:T(128)}, f32[32,40]{1,0:T(8,128)}, f32[32,40,64,128]{3,2,1,0:T(8,128)}, ...), condition=%wide.region_2.4_spmd.clone, body=%wide.region_1.3_spmd.clone.sunk | while | flops 1310724 | bytes 3932745 | solution.py:36
  995.3 3.0 fusion.195
  999.4 3.0 fusion.195
  1003.6 3.2 fusion.195
  1008.0 3.0 fusion.195
  1012.2 3.0 fusion.195
  1016.4 3.0 fusion.195
  1020.6 3.0 fusion.195
  1024.8 3.1 fusion.195
  1029.0 3.0 fusion.195
  1033.2 3.0 fusion.195
  1037.4 3.0 fusion.195
  1041.6 3.0 fusion.195
  1045.8 3.0 fusion.195
  1050.0 3.0 fusion.195
  1054.1 3.0 fusion.195
  1058.3 3.0 fusion.195
  1062.5 3.0 fusion.195
  1066.6 3.4 fusion.195
  1071.2 3.2 fusion.195
  1075.6 3.0 fusion.195
  1079.8 3.0 fusion.195
  1084.0 3.0 fusion.195
  1088.2 3.1 fusion.195
  1092.5 3.0 fusion.195
  1096.7 3.0 fusion.195
  1100.8 3.1 fusion.195
  1105.1 3.0 fusion.195
  1113.5 3.1 fusion.195
  1117.8 3.0 fusion.195
  1123.5 4.4 fusion.7
  1128.0 144.7 %all-gather.13.cloned.1.call-done = f32[1280,64,128]{2,1,0:T(8,128)} async-done(((f32[40,64,128]{2,1,0:T(8,128)}), f32[1280,64,128]{2,1,0:T(8,128)}) %all-gather.13.cloned.1.call-update) | async-done | bytes 41943056 | tf_op jit(solution)/shard_map/all_gather | solution.py:24
  1272.7 29.2 %rev.48 = f32[32,40,64,128]{3,2,1,0:T(8,128)} reverse(f32[32,40,64,128]{3,2,1,0:T(8,128)} %bitcast.302), dimensions={0} | reverse | bytes 83886080 | tf_op jit(solution)/shard_map/rev | solution.py:26
  1301.9 72.1 %while.57 = (s32[]{:T(128)}, f32[40,64,128]{2,1,0:T(8,128)S(1)}, s32[]{:T(128)}, f32[32,40]{1,0:T(8,128)}, f32[32,40,64,128]{3,2,1,0:T(8,128)}, /*index=5*/s32[]{:T(128)}, s32[]{:T(128)}) while((s32[]{:T(128)}, f32[40,64,128]{2,1,0:T(8,128)S(1)}, s32[]{:T(128)}, f32[32,40]{1,0:T(8,128)}, f32[32,40,64,128]{3,2,1,0:T(8,128)}, ...), condition=%wide.region_6.8_spmd.clone, body=%wide.region_5.7_spmd.clone.sunk | while | flops 1310724 | bytes 3932745 | solution.py:36
  1375.3 5.8 fusion.6
  1395.8 8.6 rev.49
  1404.4 3.1 fusion.38
  1413.5 75.1 %all-reduce.24 = (f32[40]{0:T(128)}, f32[40]{0:T(128)}, f32[40]{0:T(128)}, f32[12,40]{1,0:T(8,128)}, f32[4,2560]{1,0:T(4,128)}, /*index=5*/f32[2560]{0:T(1024)}) all-reduce(f32[40]{0:T(128)S(1)} %add_multiply_fusion, f32[40]{0:T(128)S(1)} %copy-done.112, f32[40]{0:T(128)S(1)} %add.334, ...), channel_id=1, replica_groups=mesh['dp'=8,'seq'=32] {'dp','seq'}, use_global_device_ids=true, to_apply=%region_27.29 | all-reduce | flops 13400 | bytes 107200 | tf_op jit(solution)/shard_map/psum | solution.py:170
  (582 shorter events, 382.4 us)
Async XLA Ops:
  7.2 297.7 %all-gather.17.cloned.1.call-start = ((), (), s32[]{:S(2)}) async-start(), calls=%async_computation.3 | async-start | bytes 43253760 | tf_op jit(solution)/shard_map/all_gather | solution.py:24
  8.1 5.7 copy-start.30
  8.8 3.3 copy-start.109
  10.6 10.0 copy-start.38
  12.1 3.8 copy-start.40
  12.4 3.4 copy-start.32
  12.4 3.4 copy-start.103
  15.8 3.2 copy-start.12
  19.0 568.4 %all-gather.15.cloned.1.call-start = ((), (), s32[]{:S(2)}) async-start(), calls=%async_computation.2 | async-start | bytes 43253760 | tf_op jit(solution)/shard_map/all_gather | solution.py:24
  23.2 7.2 copy-start.29
  23.2 7.3 copy-start.79
  23.2 967.1 %all-gather.11.cloned.1.call-start = ((), (), s32[]{:S(2)}) async-start(), calls=%async_computation | async-start | bytes 43253760 | tf_op jit(solution)/shard_map/all_gather | solution.py:24
  24.7 97.5 %collective-permute-start = (bf16[1,3,2560]{2,1,0:T(4,128)(2,1)}, bf16[1,3,2560]{2,1,0:T(4,128)(2,1)}, u32[]{:S(2)}, u32[]{:S(2)}) collective-permute-start(bf16[1,3,2560]{2,1,0:T(4,128)(2,1)} %get-tuple-element.602), channel_id=1, source_target_pairs={{0,1},{1,2},{2,3},{3,4},{4,5},{5,6},{6,7},{7,8},{8,9},{9,10},{10,1... | collective-permute-start | bytes 46088 | tf_op jit(solution)/shard_map/ppermute | solution.py:16
  29.1 94.9 %collective-permute-start.1 = (bf16[1,3,2560]{2,1,0:T(4,128)(2,1)}, bf16[1,3,2560]{2,1,0:T(4,128)(2,1)}, u32[]{:S(2)}, u32[]{:S(2)}) collective-permute-start(bf16[1,3,2560]{2,1,0:T(4,128)(2,1)} %get-tuple-element.603), channel_id=1, source_target_pairs={{1,0},{2,1},{3,2},{4,3},{5,4},{6,5},{7,6},{8,7},{9,8},{10,9},{11,1... | collective-permute-start | bytes 46088 | tf_op jit(solution)/shard_map/ppermute | solution.py:17
  128.1 3.7 copy-start.5
  689.5 5.8 copy-start.26
  691.1 4.2 copy-start.36
  691.1 4.2 copy-start.60
  691.1 4.2 copy-start.74
  691.2 4.2 copy-start.90
  691.2 6.3 copy-start.22
  691.2 6.3 copy-start.23
  710.3 562.4 %all-gather.13.cloned.1.call-start = ((), (), s32[]{:S(2)}) async-start(), calls=%async_computation.1 | async-start | bytes 43253760 | tf_op jit(solution)/shard_map/all_gather | solution.py:24
  711.6 3.4 copy-start.62
  729.8 3.7 copy-start.8
  735.3 12.2 copy-start.65
  735.3 12.2 copy-start.67
  784.9 12.1 copy-start.61
  787.7 42.7 %collective-permute-start.2 = (f32[3,2560]{1,0:T(4,128)}, f32[3,2560]{1,0:T(4,128)}, u32[]{:S(2)}, u32[]{:S(2)}) collective-permute-start(f32[3,2560]{1,0:T(4,128)} %copy.135), channel_id=1, source_target_pairs={{1,0},{2,1},{3,2},{4,3},{5,4},{6,5},{7,6},{8,7},{9,8},{10,9},{11,1... | collective-permute-start | bytes 92168 | tf_op jit(solution)/shard_map/ppermute | solution.py:42
  791.4 9.6 copy-start.54
  791.4 11.3 copy-start.9
  791.4 11.3 copy-start.27
  791.4 41.3 %collective-permute-start.3 = (f32[3,2560]{1,0:T(4,128)}, f32[3,2560]{1,0:T(4,128)}, u32[]{:S(2)}, u32[]{:S(2)}) collective-permute-start(f32[3,2560]{1,0:T(4,128)} %copy.137), channel_id=1, source_target_pairs={{0,1},{1,2},{2,3},{3,4},{4,5},{5,6},{6,7},{7,8},{8,9},{9,10},{10,1... | collective-permute-start | bytes 92168 | tf_op jit(solution)/shard_map/ppermute | solution.py:42
  804.5 14.5 copy-start.44
  805.4 13.6 copy-start.46
  805.4 6.4 copy-start.76
  805.4 6.4 copy-start.92
  805.4 6.4 copy-start.116
  811.8 6.5 copy-start.80
  811.8 6.5 copy-start.81
  811.8 6.5 copy-start.82
  811.8 6.5 copy-start.83
  811.8 6.4 copy-start.84
  811.8 6.4 copy-start.85
  811.8 6.4 copy-start.86
  811.8 6.4 copy-start.87
  811.8 7.1 copy-start.39
  811.9 7.1 copy-start.41
  811.9 7.1 copy-start.104
  811.9 7.1 copy-start.107
  1375.3 5.8 copy-start.114
  1375.3 6.6 copy-start.59
  1382.0 4.3 copy-start.58
  1386.3 3.6 copy-start.93
  1386.3 3.6 copy-start.94
  1386.4 3.6 copy-start.110
  1386.4 3.8 copy-start.111
  1386.4 4.0 copy-start.31
  1386.4 5.0 copy-start.57
  1388.5 3.1 copy-start.51
  1395.7 8.6 copy-start.3
  1395.7 8.7 copy-start.50
  1407.5 2.9 copy-start.55
  1410.4 78.2 %copy-start.1 = (f32[12,40]{1,0:T(8,128)S(1)}, f32[12,40]{1,0:T(8,128)}, u32[]{:S(2)}) copy-start(f32[12,40]{1,0:T(8,128)} %param.31) | copy-start | bytes 5764
  (61 other events, 114.3 us)
Sparse Core Ops, SparseCore 0:
  19.1 285.7 all-gather.16
  307.5 279.8 all-gather.14
  710.4 279.8 all-gather.10
  992.7 279.8 all-gather.12
where the time goes:
time: 1520 us; the launch traced here: 1500 us
  waiting for transfers between devices  629 us (41%)
  local copies, waits for them, and re-layouts  302 us (20%)
  other arithmetic  302 us (20%)
  blocking collectives  160 us (11%)
  matrix products  72.2 us (5%)
  between operations  15.3 us (1%)
    all_gather x4, waiting for transfers between devices, prefix(): pieces = jax.tree.map(lambda part: lax.all_gather(part, axis), value)  629 us
    select_n x124, other arithmetic, hop(): jnp.where(position < mine, new, old)  244 us
    mul x124, local copies, waits for them, and re-layouts, chain_link(): later[1][:, None, None] * earlier[0] + later[0]  101 us
    all_gather x2, blocking collectives, prefix(): pieces = jax.tree.map(lambda part: lax.all_gather(part, axis), value)  85.2 us
    psum x1, blocking collectives, per_device(): lax.psum((params_fwd[0] + params_rev[0], params_fwd[1] + params_rev[1], p...  75.1 us
    rev x4, local copies, waits for them, and re-layouts, prefix(): pieces = jax.tree.map(lambda part: part[::-1], pieces)  60.4 us
    unnamed x241, local copies, waits for them, and re-layouts  41.7 us
  transfers between devices with their start and end apart: 8, of which 4 were waited for; matrix products, arithmetic and copies ran while one was open for 27% of the time, Pallas kernels for 0%

commit v1 on v0

v1 whole, which is shorter than its diff:
```python
import functools

import jax
import jax.numpy as jnp
from jax import lax
from jax.experimental import pallas as pl
from jax.experimental.pallas import tpu as pltpu
from jax.sharding import PartitionSpec as P

bf16 = jnp.bfloat16
f32 = jnp.float32

GROUP = 8
ROWS = 4
LANES = 128
HEADS = 5
WIDTH = 64
CH = HEADS * WIDTH
PACK = 928
VMEM = 58 * 1024 * 1024

Z_GROUPS = [[y * GROUP + z for z in range(GROUP)] for y in range(ROWS)]

NN = (((1,), (0,)), ((), ()))
NT = (((1,), (1,)), ((), ()))
TN = (((0,), (0,)), ((), ()))


def dot(a, b, dims):
    return lax.dot_general(a, b, dims, preferred_element_type=f32)


def split2(a):
    hi = a.astype(bf16)
    return hi, (a - hi.astype(f32)).astype(bf16)


def split3(a):
    hi = a.astype(bf16)
    rest = a - hi.astype(f32)
    mid = rest.astype(bf16)
    return hi, mid, (rest - mid.astype(f32)).astype(bf16)


def exact_dot(a, table, dims):
    hi, mid, lo = split3(a)
    return dot(hi, table, dims) + dot(mid, table, dims) + dot(lo, table, dims)


def iota(shape, axis):
    return lax.broadcasted_iota(jnp.int32, shape, axis)


def zero_one(condition):
    return jnp.where(condition, 1.0, 0.0).astype(bf16)


def square_masks():
    row, col = iota((LANES, LANES), 0), iota((LANES, LANES), 1)
    return row, col


def pack_kernel(comp_ref, hid_ref, grad_ref, b_ref, c_ref, dt_ref, ids_ref, out_ref):
    row, col = square_masks()
    eye = zero_one(row == col)
    for source, base in ((hid_ref, 0), (grad_ref, CH)):
        for block in range(GROUP * CH // LANES):
            piece = source[:, block * LANES : (block + 1) * LANES]
            flipped = dot(eye, piece, NT).astype(bf16)
            for half in range(2):
                channel = block * LANES + half * WIDTH
                target, at = channel // CH, channel % CH
                out_ref[target, base + at : base + at + WIDTH, :] = flipped[
                    half * WIDTH : (half + 1) * WIDTH
                ]
    pick_row, pick_col = iota((GROUP * 8, 40), 0), iota((GROUP * 8, 40), 1)
    pick = zero_one(
        ((pick_row % 8) < HEADS) & ((pick_row // 8) * HEADS + (pick_row % 8) == pick_col)
    )
    parts = [dot(pick, part, NT) for part in split3(dt_ref[...])]
    ids = ids_ref[...]
    partner = jnp.zeros_like(ids)
    for code in range(12):
        partner = jnp.where(ids == code, comp_ref[code], partner)
    both = jnp.concatenate([ids, partner, jnp.zeros((6, LANES), jnp.int32)], axis=0).astype(f32)
    b_rows, c_rows = b_ref[...], c_ref[...]
    for target in range(GROUP):
        out_ref[target, 2 * CH : 2 * CH + LANES, :] = b_rows
        out_ref[target, 2 * CH + LANES : 2 * CH + 2 * LANES, :] = c_rows
        tail = jnp.concatenate(
            [part[target * 8 : target * 8 + 8] for part in parts] + [both], axis=0
        )
        out_ref[target, 2 * CH + 2 * LANES : PACK, :] = tail.astype(bf16)


def pack(complement, hidden, grad, b_rows, c_rows, dt_rows, ids):
    whole = pl.BlockSpec(memory_space=pltpu.VMEM)
    return pl.pallas_call(
        pack_kernel,
        name="pack",
        out_shape=jax.ShapeDtypeStruct((GROUP, PACK, LANES), bf16),
        in_specs=[pl.BlockSpec(memory_space=pltpu.SMEM)] + [whole] * 6,
        out_specs=whole,
        compiler_params=pltpu.CompilerParams(vmem_limit_bytes=VMEM),
    )(complement, hidden, grad, b_rows, c_rows, dt_rows, ids)


(R_STEP_F, R_STEP_R, R_CUM_F, R_CUM_R, R_SIG_F, R_SIG_R, R_TOT_F, R_TOT_R,
 R_PRE_F, R_POST_F, R_PRE_R, R_POST_R) = range(12)


def code_tables(tail):
    code = iota((LANES, LANES), 0)
    tables = []
    for line in (24, 25):
        ids = (tail[line : line + 1] + 3.0).astype(jnp.int32)
        tables.append(zero_one((code == ids) | (code == 2)))
    return tables


def rows_at(slot):
    return slice(slot * 8, slot * 8 + 8)


def heads_at(head, offset=0):
    return slice(offset + head * WIDTH, offset + (head + 1) * WIDTH)


def phase_one_kernel(
    pk, before, after, cw, shift_table, rate,
    x_f, x_r, slope_f, slope_r, u_f, u_r, v_f, v_r, rows, ends_up, ends_down,
    ext, left_x, left_g, run,
):
    row, col = square_masks()
    upper = zero_one(row <= col)
    lower = zero_one(row >= col)
    ones = jnp.ones((LANES, LANES), bf16)
    lane = iota((WIDTH, LANES), 1)
    ext[0] = before[...]
    ext[GROUP + 1] = after[...]

    def chunk(k, _):
        ext[k + 1] = pk[k, :CH, :]
        tail = pk[k, 2 * CH + 2 * LANES : PACK, :].astype(f32)
        dt = tail[0:8] + tail[8:16] + tail[16:24]
        for index, table in enumerate(code_tables(tail)):
            arg = dt + exact_dot(shift_table[...], table, NN)
            decay = jnp.exp(-jnp.abs(arg))
            step = jnp.maximum(arg, 0.0) + jnp.log1p(decay)
            log_decay = rate[...] * step
            rows[k, rows_at(R_STEP_F + index), :] = step
            rows[k, rows_at(R_SIG_F + index), :] = (
                jnp.where(arg >= 0, 1.0, decay) / (1.0 + decay)
            )
            rows[k, rows_at(R_CUM_F + index), :] = exact_dot(log_decay, (upper, lower)[index], NN)
            rows[k, rows_at(R_TOT_F + index), :] = exact_dot(log_decay, ones, NN)
        return 0

    lax.fori_loop(0, GROUP, chunk, 0)

    def body(k, _):
        cums = (rows[k, rows_at(R_CUM_F), :], rows[k, rows_at(R_CUM_R), :])
        growth = [jnp.exp(c) for c in cums]
        tails = [
            jnp.exp(rows[k, rows_at(R_TOT_F + i), :] - cums[i]) * rows[k, rows_at(R_STEP_F + i), :]
            for i in range(2)
        ]
        for head in range(HEADS):
            at = heads_at(head)
            cur = ext[k + 1, at, :].astype(f32)
            prv = ext[k, at, :].astype(f32)
            nxt = ext[k + 2, at, :].astype(f32)
            base = cw[4, at, :] + cw[0, at, :] * cur
            pre_f, pre_r = base, base
            for tap in range(1, 4):
                weight = cw[tap, at, :]
                pre_f += weight * pltpu.roll(jnp.where(lane < LANES - tap, cur, prv), tap, 1)
                pre_r += weight * pltpu.roll(jnp.where(lane >= tap, cur, nxt), LANES - tap, 1)
            grads = pk[k, CH + head * WIDTH : CH + (head + 1) * WIDTH, :].astype(f32)
            for index, (pre, x_ref, slope_ref) in enumerate(
                ((pre_f, x_f, slope_f), (pre_r, x_r, slope_r))
            ):
                gate = 1.0 / (1.0 + jnp.exp(-pre))
                x = pre * gate
                x_ref[k, at, :] = x
                slope_ref[k, at, :] = gate + x * (1.0 - gate)
                hi, lo = split2(x * tails[index][head : head + 1])
                out_at = heads_at(head, index * CH)
                left_x[out_at, :LANES] = hi
                left_x[out_at, LANES:] = lo
                hi, lo = split2(grads * growth[index][head : head + 1])
                left_g[out_at, :LANES] = hi
                left_g[out_at, LANES:] = lo
        b_rows = pk[k, 2 * CH : 2 * CH + LANES, :]
        c_rows = pk[k, 2 * CH + LANES : 2 * CH + 2 * LANES, :]
        states = dot(left_x[...], jnp.concatenate([b_rows, b_rows], axis=0), NN)
        u_f[k] = states[:CH]
        u_r[k] = states[CH:]
        pulls = dot(left_g[...], jnp.concatenate([c_rows, c_rows], axis=0), NN)
        v_f[k] = pulls[:CH]
        v_r[k] = pulls[CH:]
        return 0

    lax.fori_loop(0, GROUP, body, 0)

    run[...] = jnp.zeros_like(run)

    def scan(step, logs):
        up, down = step, GROUP - 1 - step
        pre_f, pre_r, post_f, post_r = logs
        rows[up, rows_at(R_PRE_F), :] = jnp.exp(pre_f)
        rows[up, rows_at(R_PRE_R), :] = jnp.exp(pre_r)
        rows[down, rows_at(R_POST_F), :] = jnp.exp(post_f)
        rows[down, rows_at(R_POST_R), :] = jnp.exp(post_r)
        moves = ((u_f, up, R_TOT_F), (v_r, up, R_TOT_R), (u_r, down, R_TOT_R), (v_f, down, R_TOT_F))
        for slot, (ref, at_chunk, total) in enumerate(moves):
            factor = jnp.exp(rows[at_chunk, rows_at(total), :])
            for head in range(HEADS):
                at = heads_at(head)
                held = run[slot, at, :]
                own = ref[at_chunk, at, :]
                ref[at_chunk, at, :] = held
                run[slot, at, :] = factor[head : head + 1] * held + own
        return (
            pre_f + rows[up, rows_at(R_TOT_F), :],
            pre_r + rows[up, rows_at(R_TOT_R), :],
            post_f + rows[down, rows_at(R_TOT_F), :],
            post_r + rows[down, rows_at(R_TOT_R), :],
        )

    zero = jnp.zeros((8, LANES), f32)
    all_f, all_r, _, _ = lax.fori_loop(0, GROUP, scan, (zero, zero, zero, zero))
    for ends, pair in ((ends_up, (0, 1)), (ends_down, (2, 3))):
        ends[0:CH, :] = run[pair[0]]
        ends[CH : 2 * CH, :] = run[pair[1]]
        ends[2 * CH : 2 * CH + 8, :] = jnp.exp(all_f)
        ends[2 * CH + 8 : 2 * CH + 16, :] = jnp.exp(all_r)


def phase_one(pk, before, after, cw, shift_table, rate):
    whole = pl.BlockSpec(memory_space=pltpu.VMEM)
    block = jax.ShapeDtypeStruct((GROUP, CH, LANES), f32)
    ends = jax.ShapeDtypeStruct((2 * CH + 16, LANES), f32)
    return pl.pallas_call(
        phase_one_kernel,
        name="phase_one",
        out_shape=[block] * 8 + [jax.ShapeDtypeStruct((GROUP, 96, LANES), f32), ends, ends],
        in_specs=[whole] * 6,
        out_specs=[whole] * 11,
        scratch_shapes=[
            pltpu.VMEM((GROUP + 2, CH, LANES), bf16),
            pltpu.VMEM((2 * CH, 2 * LANES), bf16),
            pltpu.VMEM((2 * CH, 2 * LANES), bf16),
            pltpu.VMEM((4, CH, LANES), f32),
        ],
        compiler_params=pltpu.CompilerParams(vmem_limit_bytes=VMEM),
    )(pk, before, after, cw, shift_table, rate)


def phase_two_kernel(
    pk, before, after, cw, rate, skip,
    x_f, x_r, slope_f, slope_r, u_f, u_r, v_f, v_r, rows,
    up_1, up_2, up_3, down_1, down_2, down_3,
    layer, d_hid, spill, wide, conv_out, head_out,
    entry, states, d_states, state_bits, d_state_bits, reach, pulled, gd, xt,
    d_pre_f, d_pre_r, acc, line, acc_rows, d_g, a_hi, a_lo,
):
    row, col = square_masks()
    is_low = row >= col
    is_up = row <= col
    low_one, up_one = zero_one(is_low), zero_one(is_up)
    ones = jnp.ones((LANES, LANES), bf16)
    lane = iota((WIDTH, LANES), 1)

    for slot, (chain, part, total) in enumerate(
        (
            ((up_1, up_2, up_3), 0, 0),
            ((up_1, up_2, up_3), 1, 1),
            ((down_1, down_2, down_3), 0, 1),
            ((down_1, down_2, down_3), 1, 0),
        )
    ):
        near, middle, far = chain
        factor_at = slice(2 * CH + total * 8, 2 * CH + total * 8 + 8)
        near_total, middle_total = near[factor_at, :], middle[factor_at, :]
        for head in range(HEADS):
            at = heads_at(head, part * CH)
            inner = middle[at, :] + middle_total[head : head + 1] * far[at, :]
            entry[slot, heads_at(head), :] = near[at, :] + near_total[head : head + 1] * inner

    line[...] = jnp.zeros_like(line)
    acc[...] = jnp.zeros_like(acc)
    acc_rows[...] = jnp.zeros_like(acc_rows)
    for ref in (d_pre_f, d_pre_r):
        for edge in (0, 1, GROUP + 2, GROUP + 3):
            ref[edge] = jnp.zeros((CH, LANES), f32)

    def body(k, _):
        b_rows = pk[k, 2 * CH : 2 * CH + LANES, :]
        c_rows = pk[k, 2 * CH + LANES : 2 * CH + 2 * LANES, :]
        step = [rows[k, rows_at(R_STEP_F + i), :] for i in range(2)]
        cum = [rows[k, rows_at(R_CUM_F + i), :] for i in range(2)]
        growth = [jnp.exp(c) for c in cum]
        total = [rows[k, rows_at(R_TOT_F + i), :] for i in range(2)]
        tail = [jnp.exp(total[i] - cum[i]) for i in range(2)]
        factor = [jnp.exp(total[i]) for i in range(2)]
        columns = jnp.concatenate(
            [cum[0], cum[1], jnp.zeros((LANES - 16, LANES), f32)], axis=0
        ).T
        into = (
            (states, state_bits, 0, u_f, R_PRE_F, 0),
            (states, state_bits, 1, u_r, R_POST_R, 2),
            (d_states, d_state_bits, 0, v_f, R_POST_F, 3),
            (d_states, d_state_bits, 1, v_r, R_PRE_R, 1),
        )
        for full, bits, index, local, decay_row, slot in into:
            decay = rows[k, rows_at(decay_row), :]
            for head in range(HEADS):
                at, to = heads_at(head), heads_at(head, index * CH)
                value = local[k, at, :] + decay[head : head + 1] * entry[slot, at, :]
                full[to, :] = value
                hi, lo = split2(value)
                bits[to, :LANES] = hi
                bits[to, LANES:] = lo
        reach[...] = dot(state_bits[...], jnp.concatenate([c_rows, c_rows], axis=1), NT)
        pulled[...] = dot(d_state_bits[...], jnp.concatenate([b_rows, b_rows], axis=1), NT)
        scores = dot(c_rows, b_rows, NT)
        d_g[...] = jnp.zeros_like(d_g)
        for head in range(HEADS):
            at = heads_at(head)
            one = slice(head, head + 1)
            gap_f = columns[:, head : head + 1] - cum[0][one]
            gap_r = columns[:, 8 + head : 9 + head] - cum[1][one]
            spread = jnp.exp(jnp.where(is_low, gap_f, gap_r))
            hi, lo = split2(scores * spread)
            a_hi[:, :LANES] = hi * low_one
            a_hi[:, LANES:] = hi * up_one
            a_lo[:, :LANES] = lo * low_one
            a_lo[:, LANES:] = lo * up_one
            grad_bits = pk[k, CH + head * WIDTH : CH + (head + 1) * WIDTH, :]
            grads = grad_bits.astype(f32)
            xs, bits = [], []
            for index, x_ref in enumerate((x_f, x_r)):
                scaled = x_ref[k, at, :] * step[index][one]
                xs.append(scaled)
                bits.append(split2(scaled))
            d_a = dot(
                jnp.concatenate([grad_bits, grad_bits], axis=0),
                jnp.concatenate(
                    [
                        jnp.concatenate([bits[0][0], bits[1][0]], axis=1),
                        jnp.concatenate([bits[0][1], bits[1][1]], axis=1),
                    ],
                    axis=0,
                ),
                TN,
            )
            d_g[...] += spread * (
                jnp.where(is_low, d_a[:, :LANES], 0.0) + jnp.where(is_up, d_a[:, LANES:], 0.0)
            )
            d_xs = dot(grad_bits, a_hi[...], NN) + dot(grad_bits, a_lo[...], NN)
            out = jnp.zeros((WIDTH, LANES), f32)
            d_skip_line = jnp.zeros((WIDTH, LANES), f32)
            for index, (x_ref, slope_ref, d_pre) in enumerate(
                ((x_f, slope_f, d_pre_f), (x_r, slope_r, d_pre_r))
            ):
                to = heads_at(head, index * CH)
                half = slice(index * LANES, (index + 1) * LANES)
                hi, lo = bits[index]
                y = (
                    dot(hi, a_hi[:, half], NT)
                    + dot(lo, a_hi[:, half], NT)
                    + dot(hi, a_lo[:, half], NT)
                    + growth[index][one] * reach[to, :]
                )
                x = x_ref[k, at, :]
                out += y + skip[one, :] * x
                d_skip_line += grads * x
                from_state = tail[index][one] * pulled[to, :]
                d_x = d_xs[:, half] + from_state
                d_pre[k + 2, at, :] = (step[index][one] * d_x + skip[one, :] * grads) * slope_ref[
                    k, at, :
                ]
                own = jnp.sum(x * d_x, axis=0, keepdims=True)
                line[index, one, :] = (
                    jnp.sum(grads * y, axis=0, keepdims=True) - step[index][one] * own
                )
                line[2 + index, one, :] = jnp.sum(
                    xs[index] * from_state
                    + factor[index][one] * (d_states[to, :] * states[to, :]),
                    axis=0,
                    keepdims=True,
                )
                line[4 + index, one, :] = own
                hi, lo = split2(grads * growth[index][one])
                gd[to, :LANES] = hi
                gd[to, LANES:] = lo
                hi, lo = split2(xs[index] * tail[index][one])
                xt[to, :LANES] = hi
                xt[to, LANES:] = lo
            layer[k, at, :] = out.astype(bf16)
            line[6, one, :] = jnp.sum(d_skip_line, axis=0, keepdims=True)
        g_hi, g_lo = split2(d_g[...])
        wide_c = dot(gd[:, :LANES], state_bits[...], TN)
        wide[k, LANES : 2 * LANES, :] = (
            dot(g_hi, b_rows, NN)
            + dot(g_lo, b_rows, NN)
            + wide_c[:, :LANES]
            + wide_c[:, LANES:]
            + dot(gd[:, LANES:], state_bits[:, :LANES], TN)
        )
        wide_b = dot(xt[:, :LANES], d_state_bits[...], TN)
        wide[k, :LANES, :] = (
            dot(g_hi, c_rows, TN)
            + dot(g_lo, c_rows, TN)
            + wide_b[:, :LANES]
            + wide_b[:, LANES:]
            + dot(xt[:, LANES:], d_state_bits[:, :LANES], TN)
        )
        d_args = jnp.zeros((8, LANES), f32)
        tables = code_tables(pk[k, 2 * CH + 2 * LANES : PACK, :].astype(f32))
        for index in range(2):
            d_log = exact_dot(line[index], (low_one, up_one)[index], NN) + exact_dot(
                line[2 + index], ones, NN
            )
            d_step = line[4 + index] + rate[...] * d_log
            d_arg = d_step * rows[k, rows_at(R_SIG_F + index), :]
            d_args += d_arg
            acc_rows[0] += d_log * rate[...] * step[index]
            acc_rows[2] += exact_dot(d_arg, tables[index], NT)
        acc_rows[1] += line[6]
        wide[k, 2 * LANES : 2 * LANES + 8, :] = d_args
        return 0

    lax.fori_loop(0, GROUP, body, 0)

    def spread_taps(tile, hid_of, store):
        for head in range(HEADS):
            at = heads_at(head)
            hid = hid_of(at).astype(f32)
            own_f, own_r = d_pre_f[tile + 1, at, :], d_pre_r[tile + 1, at, :]
            later_f, earlier_r = d_pre_f[tile + 2, at, :], d_pre_r[tile, at, :]
            both = own_f + own_r
            acc[4, at, :] += both
            acc[0, at, :] += hid * both
            total = cw[0, at, :] * both
            for tap in range(1, 4):
                shifted = pltpu.roll(
                    jnp.where(lane >= tap, own_f, later_f), LANES - tap, 1
                ) + pltpu.roll(jnp.where(lane < LANES - tap, own_r, earlier_r), tap, 1)
                acc[tap, at, :] += hid * shifted
                total += cw[tap, at, :] * shifted
            store(at, total)

    def store_spill(slot):
        def put(at, total):
            spill[slot, at, :] = total
        return put

    spread_taps(0, lambda at: before[at, :], store_spill(0))
    spread_taps(GROUP + 1, lambda at: after[at, :], store_spill(1))

    def inner(k, _):
        def put(at, total):
            d_hid[k, at, :] = total
        spread_taps(k + 1, lambda at: pk[k, at, :], put)
        return 0

    lax.fori_loop(0, GROUP, inner, 0)
    line_of = iota((8, LANES), 0)
    sums = jnp.zeros((8, CH), f32)
    for tap in range(5):
        hi, mid, lo = split3(acc[tap])
        marker = zero_one(line_of == tap)
        sums += dot(marker, hi, NT) + dot(marker, mid, NT) + dot(marker, lo, NT)
    conv_out[...] = sums
    lane_col = col
    head_out[...] = (
        exact_dot(acc_rows[0], zero_one(lane_col == 0), NN)
        + exact_dot(acc_rows[1], zero_one(lane_col == 1), NN)
        + acc_rows[2]
    )


def phase_two(pk, before, after, cw, rate, skip, saved, ups, downs):
    whole = pl.BlockSpec(memory_space=pltpu.VMEM)
    wide = jax.ShapeDtypeStruct((GROUP, 2 * LANES + 8, LANES), f32)
    return pl.pallas_call(
        phase_two_kernel,
        name="phase_two",
        out_shape=[
            jax.ShapeDtypeStruct((GROUP, CH, LANES), bf16),
            jax.ShapeDtypeStruct((GROUP, CH, LANES), f32),
            jax.ShapeDtypeStruct((2, CH, LANES), f32),
            wide,
            jax.ShapeDtypeStruct((8, CH), f32),
            jax.ShapeDtypeStruct((8, LANES), f32),
        ],
        in_specs=[whole] * 21,
        out_specs=[whole] * 6,
        scratch_shapes=[
            pltpu.VMEM((4, CH, LANES), f32),
            pltpu.VMEM((2 * CH, LANES), f32),
            pltpu.VMEM((2 * CH, LANES), f32),
            pltpu.VMEM((2 * CH, 2 * LANES), bf16),
            pltpu.VMEM((2 * CH, 2 * LANES), bf16),
            pltpu.VMEM((2 * CH, LANES), f32),
            pltpu.VMEM((2 * CH, LANES), f32),
            pltpu.VMEM((2 * CH, 2 * LANES), bf16),
            pltpu.VMEM((2 * CH, 2 * LANES), bf16),
            pltpu.VMEM((GROUP + 4, CH, LANES), f32),
            pltpu.VMEM((GROUP + 4, CH, LANES), f32),
            pltpu.VMEM((5, CH, LANES), f32),
            pltpu.VMEM((7, 8, LANES), f32),
            pltpu.VMEM((3, 8, LANES), f32),
            pltpu.VMEM((LANES, LANES), f32),
            pltpu.VMEM((LANES, 2 * LANES), bf16),
            pltpu.VMEM((LANES, 2 * LANES), bf16),
        ],
        compiler_params=pltpu.CompilerParams(vmem_limit_bytes=VMEM),
    )(pk, before, after, cw, rate, skip, *saved, *ups, *downs)


def unpack_kernel(layer, d_hid, wide, layer_out, hid_out, b_out, c_out, dt_out):
    row, col = square_masks()
    eye = zero_one(row == col)
    for source, target in ((layer, layer_out), (d_hid, hid_out)):
        for block in range(GROUP * CH // LANES):
            pieces = []
            for half in range(2):
                channel = block * LANES + half * WIDTH
                group, at = channel // CH, channel % CH
                pieces.append(source[group, at : at + WIDTH, :])
            both = jnp.concatenate(pieces, axis=0)
            target[:, block * LANES : (block + 1) * LANES] = dot(eye, both, NT).astype(bf16)
    for base, target in ((0, b_out), (LANES, c_out)):
        total = wide[0, base : base + LANES, :]
        for group in range(1, GROUP):
            total += wide[group, base : base + LANES, :]
        target[...] = total
    lines = jnp.concatenate(
        [wide[group, 2 * LANES : 2 * LANES + 8, :] for group in range(GROUP)]
        + [jnp.zeros((LANES - 8 * GROUP, LANES), f32)],
        axis=0,
    ).T
    pick_row, pick_col = iota((LANES, 40), 0), iota((LANES, 40), 1)
    pick = zero_one(
        ((pick_row % 8) < HEADS) & ((pick_row // 8) * HEADS + (pick_row % 8) == pick_col)
    )
    dt_out[...] = exact_dot(lines, pick, NN)


def unpack(layer, d_hid, wide):
    whole = pl.BlockSpec(memory_space=pltpu.VMEM)
    rows = jax.ShapeDtypeStruct((LANES, GROUP * CH), bf16)
    square = jax.ShapeDtypeStruct((LANES, LANES), f32)
    return pl.pallas_call(
        unpack_kernel,
        name="unpack",
        out_shape=[rows, rows, square, square, jax.ShapeDtypeStruct((LANES, 40), f32)],
        in_specs=[whole] * 3,
        out_specs=[whole] * 5,
        compiler_params=pltpu.CompilerParams(vmem_limit_bytes=VMEM),
    )(layer, d_hid, wide)


def exchange(array):
    return lax.all_to_all(array, "seq", 0, 0, axis_index_groups=Z_GROUPS)


def along_y(array, by):
    pairs = [
        (y * GROUP + z, (y + by) * GROUP + z)
        for y in range(ROWS)
        for z in range(GROUP)
        if 0 <= y + by < ROWS
    ]
    return lax.ppermute(array, "seq", pairs)


def flip_bit(array, axis, bit):
    count = lax.axis_size(axis)
    return lax.ppermute(array, axis, [(i, i ^ bit) for i in range(count)])


def total_over_all(array):
    for axis, bit in (("dp", 1), ("dp", 2), ("dp", 4), ("seq", 8), ("seq", 16)):
        array = array + flip_bit(array, axis, bit)
    array = array[None]
    place = lax.axis_index("seq")
    for bit in (1, 2, 4):
        other = flip_bit(array, "seq", bit)
        is_high = (place & bit) != 0
        array = jnp.concatenate(
            [jnp.where(is_high, other, array), jnp.where(is_high, array, other)], axis=0
        )
    return array


def per_device(
    hidden, b_proj, c_proj, dt_raw, base_ids, complement,
    a_log, d_skip, dt_bias, base_shift, conv_w, conv_b, grad_out,
):
    group = lax.axis_index("seq") % GROUP
    taps = jnp.concatenate([conv_w, conv_b[None]], axis=0).reshape(5, GROUP, CH)
    taps = lax.dynamic_index_in_dim(taps, group, 1, keepdims=False)
    cw = jnp.broadcast_to(taps[:, :, None], (5, CH, LANES))
    per_head = jnp.stack([-jnp.exp(a_log), d_skip], axis=0)
    tables = jnp.concatenate([dt_bias[None], base_shift], axis=0)
    tables = jnp.concatenate([per_head, tables], axis=0).reshape(15, GROUP, HEADS)
    tables = lax.dynamic_index_in_dim(tables, group, 1, keepdims=False)
    tables = jnp.pad(tables, ((0, 0), (0, 8 - HEADS)))
    rate = jnp.broadcast_to(tables[0][:, None], (8, LANES))
    skip = jnp.broadcast_to(tables[1][:, None], (8, LANES))
    shift_table = jnp.pad(tables[2:].T, ((0, 0), (2, LANES - 15)))

    packed = pack(complement, hidden[0], grad_out[0], b_proj[0], c_proj[0], dt_raw[0], base_ids)
    pk = exchange(packed)
    before = along_y(pk[GROUP - 1, :CH], 1)
    after = along_y(pk[0, :CH], -1)
    *saved, ends_up, ends_down = phase_one(pk, before, after, cw, shift_table, rate)
    ups = [along_y(ends_up, by) for by in (1, 2, 3)]
    downs = [along_y(ends_down, -by) for by in (1, 2, 3)]
    layer, d_hid, spill, wide, conv_sum, head_sum = phase_two(
        pk, before, after, cw, rate, skip, saved, ups, downs
    )
    from_next = along_y(spill[0], -1)
    from_prev = along_y(spill[1], 1)
    sums = total_over_all(jnp.concatenate([conv_sum, head_sum], axis=1))
    layer = exchange(layer)
    wide = exchange(wide)
    d_hid = jnp.concatenate(
        [
            (d_hid[:1] + from_prev[None]),
            d_hid[1 : GROUP - 1],
            (d_hid[GROUP - 1 :] + from_next[None]),
        ],
        axis=0,
    ).astype(bf16)
    d_hid = exchange(d_hid)
    layer_out, d_hidden, d_b, d_c, d_dt = unpack(layer, d_hid, wide)

    conv_all = sums[:, :5, :CH].transpose(1, 0, 2).reshape(5, GROUP * CH)
    head_all = sums[:, :HEADS, CH : CH + 15].reshape(GROUP * HEADS, 15)
    return (
        layer_out[None], d_hidden[None], d_b[None], d_c[None], d_dt[None],
        head_all[:, 0], head_all[:, 1], head_all[:, 2], head_all[:, 3:].T,
        conv_all[:4], conv_all[4],
    )


def solution(mesh):
    rows = P("dp", "seq", None)
    placed = (rows, rows, rows, rows, P("dp", "seq"), P(), P(), P(), P(), P(), P(), P(), rows)
    return jax.shard_map(
        per_device,
        mesh=mesh,
        in_specs=placed,
        out_specs=(rows,) * 5 + (P(),) * 6,
        check_vma=False,
    )
```

time: 1520 us -> 245 us (0.16); the launches traced: 1500 us -> 244 us
  waiting for transfers between devices: 629 us -> 130 us
  other arithmetic: 302 us -> 1.35 us
  local copies, waits for them, and re-layouts: 302 us -> 12.1 us
  blocking collectives: 160 us -> 0 us
  matrix products: 72.2 us -> 0 us
  Pallas kernels: 0 us -> 50.7 us
  starting transfers between devices: 13.1 us -> 49.3 us
    all_gather x4 -> x0, waiting for transfers between devices: 629 us -> none  [prefix(): pieces = jax.tree.map(lambda part: lax.all_gather(part, axis), value)]
    select_n x124 -> x3, other arithmetic: 244 us -> 0.03 us  [total_over_all(): jnp.where(is_high, other, array)]
    mul x126 -> x0, local copies, waits for them, and re-layouts: 101 us -> none  [the longest x124 101 us: chain_link(): later[1][:, None, None] * earlier[0] + later[0]]
    all_gather x2 -> x0, blocking collectives: 85.2 us -> none  [prefix(): pieces = jax.tree.map(lambda part: lax.all_gather(part, axis), value)]
    psum x1 -> x0, blocking collectives: 75.1 us -> none  [per_device(): lax.psum((params_fwd[0] + params_rev[0], params_fwd[1] + params_rev[1], p...]
    rev x13 -> x0, local copies, waits for them, and re-layouts: 73.2 us -> none  [the longest x4 60.4 us: prefix(): pieces = jax.tree.map(lambda part: part[::-1], pieces)]
    dot_general x28 -> x0, matrix products: 72.2 us -> none  [the longest x6 29.3 us: section_one(): jnp.einsum('tsh,shp->thp', weights, values, precision=exact_prec)]
    ppermute x4 -> x18, waiting for transfers between devices: 0.01 us -> 67.5 us  [the longest x8 43.8 us: flip_bit(): return lax.ppermute(array, axis, [(i, i ^ bit) for i in range(count)])]
  transfers between devices with their start and end apart: 8 -> 22, of which waited for: 4 -> 18; matrix products, arithmetic and copies ran while one was open for 27% -> 3% of each run, Pallas kernels for 0% -> 0%
where the time goes in v1:
time: 245 us; the launch traced here: 244 us
  waiting for transfers between devices  130 us (53%)
  Pallas kernels  50.7 us (21%)
  starting transfers between devices  49.3 us (20%)
  local copies, waits for them, and re-layouts  12.1 us (5%)
    all_to_all x4, waiting for transfers between devices, exchange(): return lax.all_to_all(array, 'seq', 0, 0, axis_index_groups=Z_GROUPS)  62.2 us
    ppermute x8, waiting for transfers between devices, flip_bit(): return lax.ppermute(array, axis, [(i, i ^ bit) for i in range(count)])  43.8 us
    pallas_call x1, Pallas kernels, phase_two(): pl.pallas_call(phase_two_kernel, name='phase_two', out_shape=[jax.ShapeDt...  26.8 us
    ppermute x10, waiting for transfers between devices, along_y(): return lax.ppermute(array, 'seq', pairs)  23.7 us
    all_to_all x4, starting transfers between devices, exchange(): return lax.all_to_all(array, 'seq', 0, 0, axis_index_groups=Z_GROUPS)  20.5 us
    ppermute x10, starting transfers between devices, along_y(): return lax.ppermute(array, 'seq', pairs)  19.3 us
    pallas_call x1, Pallas kernels, phase_one(): pl.pallas_call(phase_one_kernel, name='phase_one', out_shape=[block] * 8...  16.7 us
    ppermute x8, starting transfers between devices, flip_bit(): return lax.ppermute(array, axis, [(i, i ^ bit) for i in range(count)])  9.58 us
  transfers between devices with their start and end apart: 22, of which 18 were waited for; matrix products, arithmetic and copies ran while one was open for 3% of the time, Pallas kernels for 0%

profile of v1, /device:TPU:6, one launch (start us, length us, event | category | flops | bytes accessed | tf_op | source)
XLA Modules:
  0.0 244.3 jit_solution(3062604732971346988)
XLA Ops:
  0.6 1.5 copy.42
  2.1 3.7 %pack.1 = bf16[8,928,128]{2,1,0:T(8,128)(2,1)} custom-call(s32[12]{0:T(128)} %comp_ref.1, bf16[128,2560]{1,0:T(8,128)(2,1)} %bitcast.41, bf16[128,2560]{1,0:T(8,128)(2,1)} %bitcast.42, bf16[128,128]{1,0:T(8,128)(2,1)} %bitcast.46, bf16[128,128]{1,0:T(8,128)(2,1)} %bitcast.47, f32[128,40]{1,0:T(8,128)} %bitcast.43, s32[1,128]{1,0:T(1,128)} %ids_ref.1), custom_call_target="tpu_custom_call" | custom-call | tf_op jit(solution)/shard_map/pack/pallas_call | solution.py:98
  5.9 8.6 %all-to-all-start = ((bf16[8,928,128]{2,1,0:T(8,128)(2,1)}), bf16[8,928,128]{2,1,0:T(8,128)(2,1)S(1)}, u32[]{:S(2)}, u32[]{:S(2)}) async-start(bf16[8,928,128]{2,1,0:T(8,128)(2,1)} %pack.1), calls=%async_computation | async-start | bytes 3801088 | tf_op jit(solution)/shard_map/all_to_all | solution.py:568
  14.5 0.1 concatenate.36
  14.7 0.1 copy.43
  14.8 0.1 concatenate.49
  14.9 0.1 concatenate.50
  15.0 0.1 concatenate.51
  15.1 0.1 fusion.7
  15.2 46.2 %all-to-all-done.pk = bf16[8,928,128]{2,1,0:T(8,128)(2,1)S(1)} async-done(((bf16[8,928,128]{2,1,0:T(8,128)(2,1)}), bf16[8,928,128]{2,1,0:T(8,128)(2,1)S(1)}, u32[]{:S(2)}, u32[]{:S(2)}) %all-to-all-start) | async-done | bytes 1900576 | tf_op jit(solution)/shard_map/all_to_all | solution.py:568
  61.5 3.5 %collective-permute-start = (bf16[320,128]{1,0:T(8,128)(2,1)S(1)}, bf16[320,128]{1,0:T(8,128)(2,1)S(1)}, u32[]{:S(2)}, u32[]{:S(2)}) collective-permute-start(bf16[320,128]{1,0:T(8,128)(2,1)S(1)} %get-tuple-element.94), channel_id=1, source_target_pairs={{0,8},{1,9},{2,10},{3,11},{4,12},{5,13},{6,14},{7,15},{8,16},{9,17... | collective-permute-start | bytes 245768 | tf_op jit(solution)/shard_map/ppermute | solution.py:578
  65.0 1.3 collective-permute-start.1
  66.3 0.7 pad.9.shift_table
  67.0 0.2 slice_reduce_fusion.4
  67.2 4.1 %collective-permute-done.1.after = bf16[320,128]{1,0:T(8,128)(2,1)S(1)} collective-permute-done((bf16[320,128]{1,0:T(8,128)(2,1)S(1)}, bf16[320,128]{1,0:T(8,128)(2,1)S(1)}, u32[]{:S(2)}, u32[]{:S(2)}) %collective-permute-start.1) | collective-permute-done | bytes 81952 | tf_op jit(solution)/shard_map/ppermute | solution.py:578
  71.3 1.2 broadcast_in_dim.49.cw
  72.5 0.7 broadcast_in_dim.51.rate
  73.2 16.7 %phase_one.1 = (f32[8,320,128]{2,1,0:T(8,128)}, f32[8,320,128]{2,1,0:T(8,128)}, f32[8,320,128]{2,1,0:T(8,128)}, f32[8,320,128]{2,1,0:T(8,128)}, f32[8,320,128]{2...) custom-call(bf16[8,928,128]{2,1,0:T(8,128)(2,1)} %copy-done, ...), custom_call_target="tpu_custom_call" | custom-call | tf_op jit(solution)/shard_map/phase_one/pallas_call | solution.py:244
  89.8 3.5 %collective-permute-start.2 = (f32[656,128]{1,0:T(8,128)}, f32[656,128]{1,0:T(8,128)S(1)}, u32[]{:S(2)}, u32[]{:S(2)}) collective-permute-start(f32[656,128]{1,0:T(8,128)} %get-tuple-element.42), channel_id=1, source_target_pairs={{0,8},{1,9},{2,10},{3,11},{4,12},{5,13},{6,14},{7,15},{8,16},{9,17... | collective-permute-start | bytes 1007624 | tf_op jit(solution)/shard_map/ppermute | solution.py:578
  93.3 3.2 %collective-permute-start.3 = (f32[656,128]{1,0:T(8,128)}, f32[656,128]{1,0:T(8,128)S(1)}, u32[]{:S(2)}, u32[]{:S(2)}) collective-permute-start(f32[656,128]{1,0:T(8,128)} %get-tuple-element.42), channel_id=1, source_target_pairs={{0,16},{1,17},{2,18},{3,19},{4,20},{5,21},{6,22},{7,23},{8,24},{9,... | collective-permute-start | bytes 1007624 | tf_op jit(solution)/shard_map/ppermute | solution.py:578
  96.6 1.3 collective-permute-start.4
  97.9 1.3 collective-permute-start.5
  99.2 1.3 collective-permute-start.6
  100.5 1.3 collective-permute-start.7
  101.8 2.2 collective-permute-done.3.up_2
  104.0 1.7 collective-permute-done.4.up_3
  105.7 2.7 %collective-permute-done.5.down_1 = f32[656,128]{1,0:T(8,128)S(1)} collective-permute-done((f32[656,128]{1,0:T(8,128)}, f32[656,128]{1,0:T(8,128)S(1)}, u32[]{:S(2)}, u32[]{:S(2)}) %collective-permute-start.5) | collective-permute-done | bytes 335904 | tf_op jit(solution)/shard_map/ppermute | solution.py:578
  108.4 1.7 collective-permute-done.6.down_2
  110.1 5.0 %collective-permute-done.7.down_3 = f32[656,128]{1,0:T(8,128)S(1)} collective-permute-done((f32[656,128]{1,0:T(8,128)}, f32[656,128]{1,0:T(8,128)S(1)}, u32[]{:S(2)}, u32[]{:S(2)}) %collective-permute-start.7) | collective-permute-done | bytes 335904 | tf_op jit(solution)/shard_map/ppermute | solution.py:578
  115.1 0.7 broadcast_in_dim.53.skip
  115.8 26.8 %phase_two.1 = (bf16[8,320,128]{2,1,0:T(8,128)(2,1)}, f32[8,320,128]{2,1,0:T(8,128)}, f32[2,320,128]{2,1,0:T(8,128)}, f32[8,264,128]{2,1,0:T(8,128)}, f32[8,320]{1,0:T(8,128)}, /*index=5*/f32[8,128]{1,0:T(8,128)}) custom-call(bf16[8,928,128]{2,1,0:T(8,128)(2,1)} %copy-done, bf16[320,128]{1,0:T(8,128)(2,1)} %copy-done.11, bf16[320,128]{1,0:T(8,128)(2,1)} %copy-done.12, ...), custom_call_target="tpu_custom_call" | custom-call | tf_op jit(solution)/shard_map/phase_two/pallas_call | solution.py:488
  142.6 4.8 %all-to-all-start.1 = ((bf16[8,320,128]{2,1,0:T(8,128)(2,1)}), bf16[8,320,128]{2,1,0:T(8,128)(2,1)S(1)}, u32[]{:S(2)}, u32[]{:S(2)}) async-start(bf16[8,320,128]{2,1,0:T(8,128)(2,1)} %get-tuple-element.44), calls=%async_computation.1 | async-start | bytes 1310720 | tf_op jit(solution)/shard_map/all_to_all | solution.py:568
  147.4 1.0 slice_bitcast_fusion.1
  148.4 1.3 collective-permute-start.8
  149.7 1.3 collective-permute-start.9
  151.1 2.2 collective-permute-done.8
  153.4 4.1 %collective-permute-done.9 = f32[320,128]{1,0:T(8,128)S(1)} collective-permute-done((f32[320,128]{1,0:T(8,128)S(1)}, f32[320,128]{1,0:T(8,128)S(1)}, u32[]{:S(2)}, u32[]{:S(2)}) %collective-permute-start.9) | collective-permute-done | bytes 163872 | tf_op jit(solution)/shard_map/ppermute | solution.py:578
  157.5 0.9 pad_maximum_fusion
  158.5 9.4 %all-to-all-done.1.layer = bf16[8,320,128]{2,1,0:T(8,128)(2,1)S(1)} async-done(((bf16[8,320,128]{2,1,0:T(8,128)(2,1)}), bf16[8,320,128]{2,1,0:T(8,128)(2,1)S(1)}, u32[]{:S(2)}, u32[]{:S(2)}) %all-to-all-start.1) | async-done | bytes 655392 | tf_op jit(solution)/shard_map/all_to_all | solution.py:568
  167.9 3.5 %all-to-all-start.2 = ((bf16[8,320,128]{2,1,0:T(8,128)(2,1)}), bf16[8,320,128]{2,1,0:T(8,128)(2,1)S(1)}, u32[]{:S(2)}, u32[]{:S(2)}) async-start(bf16[8,320,128]{2,1,0:T(8,128)(2,1)} %pad_maximum_fusion), calls=%async_computation.2 | async-start | bytes 1310720 | tf_op jit(solution)/shard_map/all_to_all | solution.py:568
  171.5 0.1 pad_maximum_fusion.5
  171.6 1.2 collective-permute-done.10
  172.8 0.8 collective-permute-start.11
  173.7 2.9 %collective-permute-done.11 = f32[8,448]{1,0:T(8,128)S(1)} collective-permute-done((f32[8,448]{1,0:T(8,128)S(1)}, f32[8,448]{1,0:T(8,128)S(1)}, u32[]{:S(2)}, u32[]{:S(2)}) %collective-permute-start.11) | collective-permute-done | bytes 14368 | tf_op jit(solution)/shard_map/ppermute | solution.py:583
  176.6 1.4 collective-permute-start.12
  178.0 3.8 %collective-permute-done.12 = f32[8,448]{1,0:T(8,128)S(1)} collective-permute-done((f32[8,448]{1,0:T(8,128)S(1)}, f32[8,448]{1,0:T(8,128)S(1)}, u32[]{:S(2)}, u32[]{:S(2)}) %collective-permute-start.12) | collective-permute-done | bytes 14368 | tf_op jit(solution)/shard_map/ppermute | solution.py:583
  181.9 3.7 %collective-permute-done.13 = f32[8,448]{1,0:T(8,128)S(1)} collective-permute-done((f32[8,448]{1,0:T(8,128)S(1)}, f32[8,448]{1,0:T(8,128)S(1)}, u32[]{:S(2)}, u32[]{:S(2)}) %collective-permute-start.13) | collective-permute-done | bytes 14368 | tf_op jit(solution)/shard_map/ppermute | solution.py:583
  185.6 6.5 %all-to-all-done.2.d_hid = bf16[8,320,128]{2,1,0:T(8,128)(2,1)S(1)} async-done(((bf16[8,320,128]{2,1,0:T(8,128)(2,1)}), bf16[8,320,128]{2,1,0:T(8,128)(2,1)S(1)}, u32[]{:S(2)}, u32[]{:S(2)}) %all-to-all-start.2) | async-done | bytes 655392 | tf_op jit(solution)/shard_map/all_to_all | solution.py:568
  192.1 3.6 %all-to-all-start.3 = ((f32[8,264,128]{2,1,0:T(8,128)}), f32[8,264,128]{2,1,0:T(8,128)S(1)}, u32[]{:S(2)}, u32[]{:S(2)}) async-start(f32[8,264,128]{2,1,0:T(8,128)} %get-tuple-element.47), calls=%async_computation.3 | async-start | bytes 2162688 | tf_op jit(solution)/shard_map/all_to_all | solution.py:568
  195.7 2.0 collective-permute-start.15
  197.7 24.2 %collective-permute-done.15 = f32[1,8,448]{2,1,0:T(8,128)S(1)} collective-permute-done((f32[1,8,448]{2,1,0:T(8,128)S(1)}, f32[1,8,448]{2,1,0:T(8,128)S(1)}, u32[]{:S(2)}, u32[]{:S(2)}) %collective-permute-start.15) | collective-permute-done | bytes 14368 | tf_op jit(solution)/shard_map/ppermute | solution.py:583
  222.0 0.4 collective-permute-start.16
  222.3 4.5 %collective-permute-done.16 = f32[2,8,448]{2,1,0:T(8,128)S(1)} collective-permute-done((f32[2,8,448]{2,1,0:T(8,128)S(1)}, f32[2,8,448]{2,1,0:T(8,128)S(1)}, u32[]{:S(2)}, u32[]{:S(2)}) %collective-permute-start.16) | collective-permute-done | bytes 28704 | tf_op jit(solution)/shard_map/ppermute | solution.py:583
  226.9 4.9 %collective-permute-start.17 = (f32[4,8,448]{2,1,0:T(8,128)S(1)}, f32[4,8,448]{2,1,0:T(8,128)S(1)}, u32[]{:S(2)}, u32[]{:S(2)}) collective-permute-start(f32[4,8,448]{2,1,0:T(8,128)S(1)} %pad_maximum_fusion.2), channel_id=1, source_target_pairs={{0,4},{1,5},{2,6},{3,7},{4,0},{5,1},{6,2},{7,3},{8,12},{9,13},{10,... | collective-permute-start | bytes 172040 | tf_op jit(solution)/shard_map/ppermute | solution.py:583
  231.8 3.3 %collective-permute-done.17 = f32[4,8,448]{2,1,0:T(8,128)S(1)} collective-permute-done((f32[4,8,448]{2,1,0:T(8,128)S(1)}, f32[4,8,448]{2,1,0:T(8,128)S(1)}, u32[]{:S(2)}, u32[]{:S(2)}) %collective-permute-start.17) | collective-permute-done | bytes 57376 | tf_op jit(solution)/shard_map/ppermute | solution.py:583
  235.2 0.7 slice.76
  236.0 0.7 squeeze.58
  236.6 0.1 pad_maximum_fusion.3
  236.7 0.1 slice_bitcast_fusion.4
  236.8 0.7 copy.49
  237.5 0.7 slice_reduce_fusion
  238.2 1.0 copy-done.1
  239.2 3.5 %unpack.1 = (bf16[128,2560]{1,0:T(8,128)(2,1)}, bf16[128,2560]{1,0:T(8,128)(2,1)}, f32[128,128]{1,0:T(8,128)}, f32[128,128]{1,0:T(8,128)}, f32[128,40]{1,0:T(8,128)}) custom-call(bf16[8,320,128]{2,1,0:T(8,128)(2,1)} %copy-done.2, bf16[8,320,128]{2,1,0:T(8,128)(2,1)} %copy-done.3, f32[8,264,128]{2,1,0:T(8,128)} %copy-done.1), custom_call_target="tpu_custom_call" | custom-call | tf_op jit(solution)/shard_map/unpack/pallas_call | solution.py:557
  242.8 1.5 copy.48
  (72 shorter events, 0.7 us)
Async XLA Ops:
  5.8 8.6 %copy-start.14 = (f32[4,2560]{1,0:T(4,128)S(1)}, f32[4,2560]{1,0:T(4,128)}, u32[]{:S(2)}) copy-start(f32[4,2560]{1,0:T(4,128)} %param.23) | copy-start | bytes 122884
  5.8 8.7 %copy-start.16 = (f32[2560]{0:T(1024)S(1)}, f32[2560]{0:T(1024)}, u32[]{:S(2)}) copy-start(f32[2560]{0:T(1024)} %param.24) | copy-start | bytes 30724
  5.8 8.8 %copy-start.17 = (f32[12,40]{1,0:T(8,128)S(1)}, f32[12,40]{1,0:T(8,128)}, u32[]{:S(2)}) copy-start(f32[12,40]{1,0:T(8,128)} %param.22) | copy-start | bytes 5764
  5.8 8.9 %copy-start.20 = (f32[40]{0:T(128)S(1)}, f32[40]{0:T(128)}, u32[]{:S(2)}) copy-start(f32[40]{0:T(128)} %param.19) | copy-start | bytes 484
  5.8 9.1 %copy-start.18 = (f32[40]{0:T(128)S(1)}, f32[40]{0:T(128)}, u32[]{:S(2)}) copy-start(f32[40]{0:T(128)} %param.20) | copy-start | bytes 484
  5.8 9.2 %copy-start.19 = (f32[40]{0:T(128)S(1)}, f32[40]{0:T(128)}, u32[]{:S(2)}) copy-start(f32[40]{0:T(128)} %param.21) | copy-start | bytes 484
  5.9 55.6 %all-to-all-start = ((bf16[8,928,128]{2,1,0:T(8,128)(2,1)}), bf16[8,928,128]{2,1,0:T(8,128)(2,1)S(1)}, u32[]{:S(2)}, u32[]{:S(2)}) async-start(bf16[8,928,128]{2,1,0:T(8,128)(2,1)} %pack.1), calls=%async_computation | async-start | bytes 3801088 | tf_op jit(solution)/shard_map/all_to_all | solution.py:568
  61.4 11.7 %copy-start = (bf16[8,928,128]{2,1,0:T(8,128)(2,1)}, bf16[8,928,128]{2,1,0:T(8,128)(2,1)S(1)}, u32[]{:S(2)}) copy-start(bf16[8,928,128]{2,1,0:T(8,128)(2,1)S(1)} %all-to-all-done.pk) | copy-start | bytes 5701636
  61.5 5.7 %collective-permute-start = (bf16[320,128]{1,0:T(8,128)(2,1)S(1)}, bf16[320,128]{1,0:T(8,128)(2,1)S(1)}, u32[]{:S(2)}, u32[]{:S(2)}) collective-permute-start(bf16[320,128]{1,0:T(8,128)(2,1)S(1)} %get-tuple-element.94), channel_id=1, source_target_pairs={{0,8},{1,9},{2,10},{3,11},{4,12},{5,13},{6,14},{7,15},{8,16},{9,17... | collective-permute-start | bytes 245768 | tf_op jit(solution)/shard_map/ppermute | solution.py:578
  65.0 6.3 %collective-permute-start.1 = (bf16[320,128]{1,0:T(8,128)(2,1)S(1)}, bf16[320,128]{1,0:T(8,128)(2,1)S(1)}, u32[]{:S(2)}, u32[]{:S(2)}) collective-permute-start(bf16[320,128]{1,0:T(8,128)(2,1)S(1)} %get-tuple-element.93), channel_id=1, source_target_pairs={{8,0},{9,1},{10,2},{11,3},{12,4},{13,5},{14,6},{15,7},{16,8},{17,9... | collective-permute-start | bytes 245768 | tf_op jit(solution)/shard_map/ppermute | solution.py:578
  67.2 6.0 %copy-start.11 = (bf16[320,128]{1,0:T(8,128)(2,1)}, bf16[320,128]{1,0:T(8,128)(2,1)S(1)}, u32[]{:S(2)}) copy-start(bf16[320,128]{1,0:T(8,128)(2,1)S(1)} %collective-permute-done.before) | copy-start | bytes 245764
  71.3 1.9 copy-start.12
  89.8 10.7 %collective-permute-start.2 = (f32[656,128]{1,0:T(8,128)}, f32[656,128]{1,0:T(8,128)S(1)}, u32[]{:S(2)}, u32[]{:S(2)}) collective-permute-start(f32[656,128]{1,0:T(8,128)} %get-tuple-element.42), channel_id=1, source_target_pairs={{0,8},{1,9},{2,10},{3,11},{4,12},{5,13},{6,14},{7,15},{8,16},{9,17... | collective-permute-start | bytes 1007624 | tf_op jit(solution)/shard_map/ppermute | solution.py:578
  93.3 10.6 %collective-permute-start.3 = (f32[656,128]{1,0:T(8,128)}, f32[656,128]{1,0:T(8,128)S(1)}, u32[]{:S(2)}, u32[]{:S(2)}) collective-permute-start(f32[656,128]{1,0:T(8,128)} %get-tuple-element.42), channel_id=1, source_target_pairs={{0,16},{1,17},{2,18},{3,19},{4,20},{5,21},{6,22},{7,23},{8,24},{9,... | collective-permute-start | bytes 1007624 | tf_op jit(solution)/shard_map/ppermute | solution.py:578
  96.6 9.1 %collective-permute-start.4 = (f32[656,128]{1,0:T(8,128)}, f32[656,128]{1,0:T(8,128)S(1)}, u32[]{:S(2)}, u32[]{:S(2)}) collective-permute-start(f32[656,128]{1,0:T(8,128)} %get-tuple-element.42), channel_id=1, source_target_pairs={{0,24},{1,25},{2,26},{3,27},{4,28},{5,29},{6,30},{7,31},{32,56},{3... | collective-permute-start | bytes 1007624 | tf_op jit(solution)/shard_map/ppermute | solution.py:578
  97.9 10.5 %collective-permute-start.5 = (f32[656,128]{1,0:T(8,128)}, f32[656,128]{1,0:T(8,128)S(1)}, u32[]{:S(2)}, u32[]{:S(2)}) collective-permute-start(f32[656,128]{1,0:T(8,128)} %get-tuple-element.43), channel_id=1, source_target_pairs={{8,0},{9,1},{10,2},{11,3},{12,4},{13,5},{14,6},{15,7},{16,8},{17,9... | collective-permute-start | bytes 1007624 | tf_op jit(solution)/shard_map/ppermute | solution.py:578
  99.2 10.9 %collective-permute-start.6 = (f32[656,128]{1,0:T(8,128)}, f32[656,128]{1,0:T(8,128)S(1)}, u32[]{:S(2)}, u32[]{:S(2)}) collective-permute-start(f32[656,128]{1,0:T(8,128)} %get-tuple-element.43), channel_id=1, source_target_pairs={{16,0},{17,1},{18,2},{19,3},{20,4},{21,5},{22,6},{23,7},{24,8},{25... | collective-permute-start | bytes 1007624 | tf_op jit(solution)/shard_map/ppermute | solution.py:578
  100.5 15.3 %copy-start.5 = (f32[656,128]{1,0:T(8,128)}, f32[656,128]{1,0:T(8,128)S(1)}, u32[]{:S(2)}) copy-start(f32[656,128]{1,0:T(8,128)S(1)} %collective-permute-done.2.up_1) | copy-start | bytes 1007620
  100.5 14.6 %collective-permute-start.7 = (f32[656,128]{1,0:T(8,128)}, f32[656,128]{1,0:T(8,128)S(1)}, u32[]{:S(2)}, u32[]{:S(2)}) collective-permute-start(f32[656,128]{1,0:T(8,128)} %get-tuple-element.43), channel_id=1, source_target_pairs={{24,0},{25,1},{26,2},{27,3},{28,4},{29,5},{30,6},{31,7},{56,32},{5... | collective-permute-start | bytes 1007624 | tf_op jit(solution)/shard_map/ppermute | solution.py:578
  104.0 11.8 %copy-start.6 = (f32[656,128]{1,0:T(8,128)}, f32[656,128]{1,0:T(8,128)S(1)}, u32[]{:S(2)}) copy-start(f32[656,128]{1,0:T(8,128)S(1)} %collective-permute-done.3.up_2) | copy-start | bytes 1007620
  105.7 10.1 %copy-start.7 = (f32[656,128]{1,0:T(8,128)}, f32[656,128]{1,0:T(8,128)S(1)}, u32[]{:S(2)}) copy-start(f32[656,128]{1,0:T(8,128)S(1)} %collective-permute-done.4.up_3) | copy-start | bytes 1007620
  108.4 7.4 %copy-start.8 = (f32[656,128]{1,0:T(8,128)}, f32[656,128]{1,0:T(8,128)S(1)}, u32[]{:S(2)}) copy-start(f32[656,128]{1,0:T(8,128)S(1)} %collective-permute-done.5.down_1) | copy-start | bytes 1007620
  110.1 5.7 %copy-start.9 = (f32[656,128]{1,0:T(8,128)}, f32[656,128]{1,0:T(8,128)S(1)}, u32[]{:S(2)}) copy-start(f32[656,128]{1,0:T(8,128)S(1)} %collective-permute-done.6.down_2) | copy-start | bytes 1007620
  115.1 0.7 copy-start.10
  142.6 8.4 %copy-start.4 = (f32[8,320,128]{2,1,0:T(8,128)S(1)}, f32[8,320,128]{2,1,0:T(8,128)}, u32[]{:S(2)}) copy-start(f32[8,320,128]{2,1,0:T(8,128)} %get-tuple-element.45) | copy-start | bytes 3932164
  142.6 25.3 %all-to-all-start.1 = ((bf16[8,320,128]{2,1,0:T(8,128)(2,1)}), bf16[8,320,128]{2,1,0:T(8,128)(2,1)S(1)}, u32[]{:S(2)}, u32[]{:S(2)}) async-start(bf16[8,320,128]{2,1,0:T(8,128)(2,1)} %get-tuple-element.44), calls=%async_computation.1 | async-start | bytes 1310720 | tf_op jit(solution)/shard_map/all_to_all | solution.py:568
  148.4 4.9 %collective-permute-start.8 = (f32[320,128]{1,0:T(8,128)S(1)}, f32[320,128]{1,0:T(8,128)S(1)}, u32[]{:S(2)}, u32[]{:S(2)}) collective-permute-start(f32[320,128]{1,0:T(8,128)S(1)} %get-tuple-element.97), channel_id=1, source_target_pairs={{0,8},{1,9},{2,10},{3,11},{4,12},{5,13},{6,14},{7,15},{8,16},{9,17... | collective-permute-start | bytes 491528 | tf_op jit(solution)/shard_map/ppermute | solution.py:578
  149.7 7.7 %collective-permute-start.9 = (f32[320,128]{1,0:T(8,128)S(1)}, f32[320,128]{1,0:T(8,128)S(1)}, u32[]{:S(2)}, u32[]{:S(2)}) collective-permute-start(f32[320,128]{1,0:T(8,128)S(1)} %get-tuple-element.98), channel_id=1, source_target_pairs={{8,0},{9,1},{10,2},{11,3},{12,4},{13,5},{14,6},{15,7},{16,8},{17,9... | collective-permute-start | bytes 491528 | tf_op jit(solution)/shard_map/ppermute | solution.py:578
  157.5 13.9 %copy-start.13 = (f32[8,320]{1,0:T(8,128)S(1)}, f32[8,320]{1,0:T(8,128)}, u32[]{:S(2)}) copy-start(f32[8,320]{1,0:T(8,128)} %get-tuple-element.53) | copy-start | bytes 30724
  157.5 13.9 %copy-start.15 = (f32[8,128]{1,0:T(8,128)S(1)}, f32[8,128]{1,0:T(8,128)}, u32[]{:S(2)}) copy-start(f32[8,128]{1,0:T(8,128)} %get-tuple-element.54) | copy-start | bytes 12292
  167.9 24.2 %copy-start.2 = (bf16[8,320,128]{2,1,0:T(8,128)(2,1)}, bf16[8,320,128]{2,1,0:T(8,128)(2,1)S(1)}, u32[]{:S(2)}) copy-start(bf16[8,320,128]{2,1,0:T(8,128)(2,1)S(1)} %all-to-all-done.1.layer) | copy-start | bytes 1966084
  167.9 24.2 %all-to-all-start.2 = ((bf16[8,320,128]{2,1,0:T(8,128)(2,1)}), bf16[8,320,128]{2,1,0:T(8,128)(2,1)S(1)}, u32[]{:S(2)}, u32[]{:S(2)}) async-start(bf16[8,320,128]{2,1,0:T(8,128)(2,1)} %pad_maximum_fusion), calls=%async_computation.2 | async-start | bytes 1310720 | tf_op jit(solution)/shard_map/all_to_all | solution.py:568
  171.5 1.2 collective-permute-start.10
  172.8 3.8 %collective-permute-start.11 = (f32[8,448]{1,0:T(8,128)S(1)}, f32[8,448]{1,0:T(8,128)S(1)}, u32[]{:S(2)}, u32[]{:S(2)}) collective-permute-start(f32[8,448]{1,0:T(8,128)S(1)} %fusion.8), channel_id=1, source_target_pairs={{0,64},{32,96},{64,0},{96,32},{128,192},{160,224},{192,128},{224,1... | collective-permute-start | bytes 43016 | tf_op jit(solution)/shard_map/ppermute | solution.py:583
  176.6 5.2 %collective-permute-start.12 = (f32[8,448]{1,0:T(8,128)S(1)}, f32[8,448]{1,0:T(8,128)S(1)}, u32[]{:S(2)}, u32[]{:S(2)}) collective-permute-start(f32[8,448]{1,0:T(8,128)S(1)} %add.40), channel_id=1, source_target_pairs={{0,128},{32,160},{64,192},{96,224},{128,0},{160,32},{192,64},{224,... | collective-permute-start | bytes 43016 | tf_op jit(solution)/shard_map/ppermute | solution.py:583
  181.9 3.7 %collective-permute-start.13 = (f32[8,448]{1,0:T(8,128)S(1)}, f32[8,448]{1,0:T(8,128)S(1)}, u32[]{:S(2)}, u32[]{:S(2)}) collective-permute-start(f32[8,448]{1,0:T(8,128)S(1)} %add.41), channel_id=1, source_target_pairs={{0,8},{1,9},{2,10},{3,11},{4,12},{5,13},{6,14},{7,15},{8,0},{9,1},... | collective-permute-start | bytes 43016 | tf_op jit(solution)/shard_map/ppermute | solution.py:583
  185.6 10.1 %collective-permute-start.14 = (f32[8,448]{1,0:T(8,128)S(1)}, f32[8,448]{1,0:T(8,128)S(1)}, u32[]{:S(2)}, u32[]{:S(2)}) collective-permute-start(f32[8,448]{1,0:T(8,128)S(1)} %add.42), channel_id=1, source_target_pairs={{0,16},{1,17},{2,18},{3,19},{4,20},{5,21},{6,22},{7,23},{8,24},{9,... | collective-permute-start | bytes 43016 | tf_op jit(solution)/shard_map/ppermute | solution.py:583
  192.1 34.8 %copy-start.3 = (bf16[8,320,128]{2,1,0:T(8,128)(2,1)}, bf16[8,320,128]{2,1,0:T(8,128)(2,1)S(1)}, u32[]{:S(2)}) copy-start(bf16[8,320,128]{2,1,0:T(8,128)(2,1)S(1)} %all-to-all-done.2.d_hid) | copy-start | bytes 1966084
  192.1 46.1 %all-to-all-start.3 = ((f32[8,264,128]{2,1,0:T(8,128)}), f32[8,264,128]{2,1,0:T(8,128)S(1)}, u32[]{:S(2)}, u32[]{:S(2)}) async-start(f32[8,264,128]{2,1,0:T(8,128)} %get-tuple-element.47), calls=%async_computation.3 | async-start | bytes 2162688 | tf_op jit(solution)/shard_map/all_to_all | solution.py:568
  195.7 26.2 %collective-permute-start.15 = (f32[1,8,448]{2,1,0:T(8,128)S(1)}, f32[1,8,448]{2,1,0:T(8,128)S(1)}, u32[]{:S(2)}, u32[]{:S(2)}) collective-permute-start(f32[1,8,448]{2,1,0:T(8,128)S(1)} %add_bitcast_fusion), channel_id=1, source_target_pairs={{0,1},{1,0},{2,3},{3,2},{4,5},{5,4},{6,7},{7,6},{8,9},{9,8},{10,11... | collective-permute-start | bytes 43016 | tf_op jit(solution)/shard_map/ppermute | solution.py:583
  222.0 4.9 %collective-permute-start.16 = (f32[2,8,448]{2,1,0:T(8,128)S(1)}, f32[2,8,448]{2,1,0:T(8,128)S(1)}, u32[]{:S(2)}, u32[]{:S(2)}) collective-permute-start(f32[2,8,448]{2,1,0:T(8,128)S(1)} %pad_maximum_fusion.4), channel_id=1, source_target_pairs={{0,2},{1,3},{2,0},{3,1},{4,6},{5,7},{6,4},{7,5},{8,10},{9,11},{10,... | collective-permute-start | bytes 86024 | tf_op jit(solution)/shard_map/ppermute | solution.py:583
  226.9 8.3 %collective-permute-start.17 = (f32[4,8,448]{2,1,0:T(8,128)S(1)}, f32[4,8,448]{2,1,0:T(8,128)S(1)}, u32[]{:S(2)}, u32[]{:S(2)}) collective-permute-start(f32[4,8,448]{2,1,0:T(8,128)S(1)} %pad_maximum_fusion.2), channel_id=1, source_target_pairs={{0,4},{1,5},{2,6},{3,7},{4,0},{5,1},{6,2},{7,3},{8,12},{9,13},{10,... | collective-permute-start | bytes 172040 | tf_op jit(solution)/shard_map/ppermute | solution.py:583
  238.2 1.0 copy-start.1

commit v2 on v0

v2 whole, which is shorter than its diff:
```python
import functools

import jax
import jax.numpy as jnp
from jax import lax
from jax.experimental import pallas as pl
from jax.experimental.pallas import tpu as pltpu
from jax.sharding import PartitionSpec as P

bf16 = jnp.bfloat16
f32 = jnp.float32

GROUP = 8
ROWS = 4
LANES = 128
HEADS = 5
WIDTH = 64
CH = HEADS * WIDTH
SETS = ((0, 2), (2, 5))
SHARED = 2 * SETS[0][1] * WIDTH
TAIL = SHARED + 2 * LANES
PACK = TAIL + 64
PACK_2 = 2 * (SETS[1][1] - SETS[1][0]) * WIDTH
EDGE = 2 * LANES + 8
WIDE = EDGE + 24
VMEM = 58 * 1024 * 1024

Y_GROUPS = [[y * GROUP + z for y in range(ROWS)] for z in range(GROUP)]
Z_GROUPS = [[y * GROUP + z for z in range(GROUP)] for y in range(ROWS)]

NN = (((1,), (0,)), ((), ()))
NT = (((1,), (1,)), ((), ()))
TN = (((0,), (0,)), ((), ()))


def dot(a, b, dims):
    return lax.dot_general(a, b, dims, preferred_element_type=f32)


def split2(a):
    hi = a.astype(bf16)
    return hi, (a - hi.astype(f32)).astype(bf16)


def split3(a):
    hi = a.astype(bf16)
    rest = a - hi.astype(f32)
    mid = rest.astype(bf16)
    return hi, mid, (rest - mid.astype(f32)).astype(bf16)


def exact_dot(a, table, dims):
    hi, mid, lo = split3(a)
    return dot(hi, table, dims) + dot(mid, table, dims) + dot(lo, table, dims)


def iota(shape, axis):
    return lax.broadcasted_iota(jnp.int32, shape, axis)


def zero_one(condition):
    return jnp.where(condition, 1.0, 0.0).astype(bf16)


def square_masks():
    row, col = iota((LANES, LANES), 0), iota((LANES, LANES), 1)
    return row, col


def pack_kernel(
    comp_ref, hid_ref, grad_ref, b_ref, c_ref, dt_ref, ids_ref, before_ref, after_ref, out_1, out_2
):
    row, col = square_masks()
    eye = zero_one(row == col)
    cut = SETS[0][1] * WIDTH
    for source, order in ((hid_ref, 0), (grad_ref, 1)):
        for block in range(GROUP * CH // LANES):
            piece = source[:, block * LANES : (block + 1) * LANES]
            flipped = dot(eye, piece, NT).astype(bf16)
            for half in range(2):
                channel = block * LANES + half * WIDTH
                target, at = channel // CH, channel % CH
                out, at = (out_1, at + order * cut) if at < cut else (
                    out_2, at - cut + order * (CH - cut)
                )
                out[target, at : at + WIDTH, :] = flipped[half * WIDTH : (half + 1) * WIDTH]
    pick_row, pick_col = iota((GROUP * 8, 40), 0), iota((GROUP * 8, 40), 1)
    pick = zero_one(
        ((pick_row % 8) < HEADS) & ((pick_row // 8) * HEADS + (pick_row % 8) == pick_col)
    )
    parts = [dot(pick, part, NT) for part in split3(dt_ref[...])]
    ids = ids_ref[...]
    partner = jnp.zeros_like(ids)
    for code in range(12):
        partner = jnp.where(ids == code, comp_ref[code], partner)
    both = jnp.concatenate([ids, partner, jnp.zeros((6, LANES), jnp.int32)], axis=0).astype(f32)
    beside = jnp.where(
        iota((8, GROUP * CH), 0) >= 5, before_ref[...].astype(f32), after_ref[...].astype(f32)
    )
    b_rows, c_rows = b_ref[...], c_ref[...]
    for target in range(GROUP):
        out_1[target, SHARED : SHARED + LANES, :] = b_rows
        out_1[target, SHARED + LANES : SHARED + 2 * LANES, :] = c_rows
        mine = beside[:, target * CH : (target + 1) * CH]
        mine = jnp.concatenate([mine, jnp.zeros((8, 3 * LANES - CH), f32)], axis=1)
        tail = jnp.concatenate(
            [part[target * 8 : target * 8 + 8] for part in parts]
            + [both]
            + [mine[:, j * LANES : (j + 1) * LANES] for j in range(3)]
            + [jnp.zeros((8, LANES), f32)],
            axis=0,
        )
        out_1[target, TAIL:PACK, :] = tail.astype(bf16)


WHOLE = pl.BlockSpec(memory_space=pltpu.VMEM)


def pack(complement, hidden, grad, b_rows, c_rows, dt_rows, ids, before, after):
    return pl.pallas_call(
        pack_kernel,
        name="pack",
        out_shape=[
            jax.ShapeDtypeStruct((GROUP, PACK, LANES), bf16),
            jax.ShapeDtypeStruct((GROUP, PACK_2, LANES), bf16),
        ],
        in_specs=[pl.BlockSpec(memory_space=pltpu.SMEM)] + [WHOLE] * 8,
        out_specs=[WHOLE] * 2,
        compiler_params=pltpu.CompilerParams(vmem_limit_bytes=VMEM),
    )(complement, hidden, grad, b_rows, c_rows, dt_rows, ids, before, after)


def cost(heads):
    return pl.CostEstimate(flops=heads * 4_000_000_000, bytes_accessed=8_000_000, transcendentals=0)


def kept(shape):
    return pl.BlockSpec(shape, lambda k: (0,) * len(shape))


def chunked(shape):
    return pl.BlockSpec((1,) + shape, lambda k: (k, 0, 0))


(R_STEP_F, R_STEP_R, R_CUM_F, R_CUM_R, R_SIG_F, R_SIG_R, R_TOT_F, R_TOT_R,
 R_PRE_F, R_POST_F, R_PRE_R, R_POST_R) = range(12)


def code_tables(tail):
    code = iota((LANES, LANES), 0)
    tables = []
    for line in (24, 25):
        ids = (tail[line : line + 1] + 3.0).astype(jnp.int32)
        tables.append(zero_one((code == ids) | (code == 2)))
    return tables


def rows_at(slot):
    return slice(slot * 8, slot * 8 + 8)


def heads_at(head, offset=0):
    return slice(offset + head * WIDTH, offset + (head + 1) * WIDTH)


def beside_chunk(pk1, which, place, block):
    tail = pk1[which, TAIL:PACK, :].astype(f32)
    lines = tail[32 + 8 * block : 40 + 8 * block]
    lines = jnp.concatenate([lines, jnp.zeros((8, LANES), f32)], axis=0).astype(bf16)
    return dot(lines, place, TN).astype(bf16)


def fill_edges(ext, pk1, first):
    token, place = iota((16, LANES), 0), iota((16, LANES), 1)
    before = zero_one((token >= 5) & (token < 8) & (place == token + LANES - 8))
    after = zero_one((token < 3) & (place == token))
    count = ext.shape[1]
    for start in range(0, count, LANES):
        size = min(LANES, count - start)
        block = (first * WIDTH + start) // LANES
        ext[0, start : start + size, :] = beside_chunk(pk1, 0, before, block)[:size]
        ext[GROUP + 1, start : start + size, :] = beside_chunk(pk1, GROUP - 1, after, block)[:size]


def phase_one_kernel(first, heads, *refs):
    if first == 0:
        pk1, cw, shift_table, rate = refs[:4]
        pk, refs = pk1, refs[4:]
        rows = refs[8]
        x_f, x_r, slope_f, slope_r, u_f, u_r, v_f, v_r = refs[:8]
        refs = refs[9:]
    else:
        pk1, pk, cw, rows = refs[:4]
        x_f, x_r, slope_f, slope_r, u_f, u_r, v_f, v_r = refs[4:12]
        refs = refs[12:]
    ends_up, ends_down, ext, left_x, left_g, run = refs
    width = heads * WIDTH
    k = pl.program_id(0)
    lane = iota((WIDTH, LANES), 1)

    @pl.when(k == 0)
    def _():
        fill_edges(ext, pk1, first)
        for chunk in range(GROUP):
            ext[chunk + 1] = pk[chunk, :width, :]
        if first == 0:
            row, col = square_masks()
            upper = zero_one(row <= col)
            lower = zero_one(row >= col)
            ones = jnp.ones((LANES, LANES), bf16)
            pre = [jnp.zeros((8, LANES), f32)] * 2
            for chunk in range(GROUP):
                tail = pk1[chunk, TAIL:PACK, :].astype(f32)
                dt = tail[0:8] + tail[8:16] + tail[16:24]
                for index, table in enumerate(code_tables(tail)):
                    arg = dt + exact_dot(shift_table[...], table, NN)
                    decay = jnp.exp(-jnp.abs(arg))
                    step = jnp.maximum(arg, 0.0) + jnp.log1p(decay)
                    log_decay = rate[...] * step
                    total = exact_dot(log_decay, ones, NN)
                    rows[chunk, rows_at(R_STEP_F + index), :] = step
                    rows[chunk, rows_at(R_SIG_F + index), :] = (
                        jnp.where(arg >= 0, 1.0, decay) / (1.0 + decay)
                    )
                    rows[chunk, rows_at(R_CUM_F + index), :] = exact_dot(
                        log_decay, (upper, lower)[index], NN
                    )
                    rows[chunk, rows_at(R_TOT_F + index), :] = total
                    rows[chunk, rows_at((R_PRE_F, R_PRE_R)[index]), :] = jnp.exp(pre[index])
                    pre[index] = pre[index] + total
            post = [jnp.zeros((8, LANES), f32)] * 2
            for chunk in reversed(range(GROUP)):
                for index in range(2):
                    rows[chunk, rows_at((R_POST_F, R_POST_R)[index]), :] = jnp.exp(post[index])
                    post[index] = post[index] + rows[chunk, rows_at(R_TOT_F + index), :]

    cums = (rows[k, rows_at(R_CUM_F), :], rows[k, rows_at(R_CUM_R), :])
    growth = [jnp.exp(c) for c in cums]
    tails = [
        jnp.exp(rows[k, rows_at(R_TOT_F + i), :] - cums[i]) * rows[k, rows_at(R_STEP_F + i), :]
        for i in range(2)
    ]
    for head in range(heads):
        at = heads_at(head)
        one = slice(first + head, first + head + 1)
        cur = ext[k + 1, at, :].astype(f32)
        prv = ext[k, at, :].astype(f32)
        nxt = ext[k + 2, at, :].astype(f32)
        base = cw[4, at, :] + cw[0, at, :] * cur
        pre_f, pre_r = base, base
        for tap in range(1, 4):
            weight = cw[tap, at, :]
            pre_f += weight * pltpu.roll(jnp.where(lane < LANES - tap, cur, prv), tap, 1)
            pre_r += weight * pltpu.roll(jnp.where(lane >= tap, cur, nxt), LANES - tap, 1)
        grads = pk[k, width + head * WIDTH : width + (head + 1) * WIDTH, :].astype(f32)
        for index, (pre_act, x_ref, slope_ref) in enumerate(
            ((pre_f, x_f, slope_f), (pre_r, x_r, slope_r))
        ):
            gate = 1.0 / (1.0 + jnp.exp(-pre_act))
            x = pre_act * gate
            x_ref[0, at, :] = x
            slope_ref[0, at, :] = gate + x * (1.0 - gate)
            hi, lo = split2(x * tails[index][one])
            out_at = heads_at(head, index * width)
            left_x[out_at, :LANES] = hi
            left_x[out_at, LANES:] = lo
            hi, lo = split2(grads * growth[index][one])
            left_g[out_at, :LANES] = hi
            left_g[out_at, LANES:] = lo
    b_rows = pk1[k, SHARED : SHARED + LANES, :]
    c_rows = pk1[k, SHARED + LANES : SHARED + 2 * LANES, :]
    states = dot(left_x[...], jnp.concatenate([b_rows, b_rows], axis=0), NN)
    u_f[k] = states[:width]
    u_r[k] = states[width:]
    pulls = dot(left_g[...], jnp.concatenate([c_rows, c_rows], axis=0), NN)
    v_f[k] = pulls[:width]
    v_r[k] = pulls[width:]

    @pl.when(k == GROUP - 1)
    def _():
        run[...] = jnp.zeros_like(run)

        def scan(step, _):
            up, down = step, GROUP - 1 - step
            moves = (
                (u_f, up, R_TOT_F), (v_r, up, R_TOT_R), (u_r, down, R_TOT_R), (v_f, down, R_TOT_F)
            )
            for slot, (ref, at_chunk, total) in enumerate(moves):
                factor = jnp.exp(rows[at_chunk, rows_at(total), :])
                for head in range(heads):
                    at = heads_at(head)
                    held = run[slot, at, :]
                    own = ref[at_chunk, at, :]
                    ref[at_chunk, at, :] = held
                    run[slot, at, :] = factor[first + head : first + head + 1] * held + own
            return 0

        lax.fori_loop(0, GROUP, scan, 0)
        whole = [
            rows[GROUP - 1, rows_at(pre), :] * jnp.exp(rows[GROUP - 1, rows_at(total), :])
            for pre, total in ((R_PRE_F, R_TOT_F), (R_PRE_R, R_TOT_R))
        ]
        for ends, pair in ((ends_up, (0, 1)), (ends_down, (2, 3))):
            ends[0:width, :] = run[pair[0]]
            ends[width : 2 * width, :] = run[pair[1]]
            ends[2 * width : 2 * width + 8, :] = whole[0]
            ends[2 * width + 8 : 2 * width + 16, :] = whole[1]


def phase_one(which, pk1, pk, cw, extra):
    first, last = SETS[which]
    heads = last - first
    width = heads * WIDTH
    block = jax.ShapeDtypeStruct((GROUP, width, LANES), f32)
    rows = jax.ShapeDtypeStruct((GROUP, 96, LANES), f32)
    ends = jax.ShapeDtypeStruct((2 * width + 16, LANES), f32)
    outs = [block] * 8 + ([rows] if which == 0 else []) + [ends, ends]
    specs = [chunked((width, LANES))] * 4 + [kept(out.shape) for out in outs[4:]]
    operands = [pk1, cw, *extra] if which == 0 else [pk1, pk, cw, *extra]
    return pl.pallas_call(
        functools.partial(phase_one_kernel, first, heads),
        name=f"phase_one_{which}",
        grid=(GROUP,),
        out_shape=outs,
        in_specs=[kept(operand.shape) for operand in operands],
        out_specs=specs,
        scratch_shapes=[
            pltpu.VMEM((GROUP + 2, width, LANES), bf16),
            pltpu.VMEM((2 * width, 2 * LANES), bf16),
            pltpu.VMEM((2 * width, 2 * LANES), bf16),
            pltpu.VMEM((4, width, LANES), f32),
        ],
        cost_estimate=cost(heads),
        compiler_params=pltpu.CompilerParams(vmem_limit_bytes=VMEM),
    )(*operands)


def phase_two_kernel(first, heads, *refs):
    (
        place_y, pk1, pk, cw, rate, skip,
        x_f, x_r, slope_f, slope_r, u_f, u_r, v_f, v_r, rows, ends,
    ) = refs[:16]
    refs = refs[16:]
    if first:
        wide_in, edges_in = refs[:2]
        refs = refs[2:]
    (
        rows_out, wide, edges, conv_out, head_out,
        ext, entry, states, d_states, state_bits, d_state_bits, reach, pulled, gd, xt,
        d_pre_f, d_pre_r, acc, line, acc_rows, d_g, a_hi, a_lo,
    ) = refs
    width = heads * WIDTH
    k = pl.program_id(0)
    row, col = square_masks()
    is_low = row >= col
    is_up = row <= col
    low_one, up_one = zero_one(is_low), zero_one(is_up)
    ones = jnp.ones((LANES, LANES), bf16)
    lane = iota((WIDTH, LANES), 1)

    def held(start, stop):
        return wide_in[0, start:stop, :] if first else 0.0

    @pl.when(k == 0)
    def _():
        fill_edges(ext, pk1, first)
        entry[...] = jnp.zeros_like(entry)
        here = place_y[0]
        for order in range(ROWS - 1):
            for other, slots, reached in (
                (order, ((0, 0, 0), (1, 1, 1)), order < here),
                (ROWS - 1 - order, ((2, 0, 1), (3, 1, 0)), ROWS - 1 - order > here),
            ):

                @pl.when(reached)
                def _(other=other, slots=slots):
                    for slot, part, total in slots:
                        start = 2 * width + total * 8
                        factor = ends[other, start : start + 8, :]
                        for head in range(heads):
                            at = heads_at(head)
                            entry[slot, at, :] = (
                                factor[first + head : first + head + 1] * entry[slot, at, :]
                                + ends[other, heads_at(head, part * width), :]
                            )

        line[...] = jnp.zeros_like(line)
        acc[...] = jnp.zeros_like(acc)
        acc_rows[...] = jnp.zeros_like(acc_rows)
        for ref in (d_pre_f, d_pre_r):
            for edge in (0, 1, GROUP + 2, GROUP + 3):
                ref[edge] = jnp.zeros((width, LANES), f32)

    b_rows = pk1[k, SHARED : SHARED + LANES, :]
    c_rows = pk1[k, SHARED + LANES : SHARED + 2 * LANES, :]
    step = [rows[0, rows_at(R_STEP_F + i), :] for i in range(2)]
    cum = [rows[0, rows_at(R_CUM_F + i), :] for i in range(2)]
    growth = [jnp.exp(c) for c in cum]
    total = [rows[0, rows_at(R_TOT_F + i), :] for i in range(2)]
    tail = [jnp.exp(total[i] - cum[i]) for i in range(2)]
    factor = [jnp.exp(total[i]) for i in range(2)]
    columns = jnp.concatenate(
        [cum[0], cum[1], jnp.zeros((LANES - 16, LANES), f32)], axis=0
    ).T
    into = (
        (states, state_bits, 0, u_f, R_PRE_F, 0),
        (states, state_bits, 1, u_r, R_POST_R, 2),
        (d_states, d_state_bits, 0, v_f, R_POST_F, 3),
        (d_states, d_state_bits, 1, v_r, R_PRE_R, 1),
    )
    for full, bits, index, local, decay_row, slot in into:
        decay = rows[0, rows_at(decay_row), :]
        for head in range(heads):
            at, to = heads_at(head), heads_at(head, index * width)
            value = local[0, at, :] + decay[first + head : first + head + 1] * entry[slot, at, :]
            full[to, :] = value
            hi, lo = split2(value)
            bits[to, :LANES] = hi
            bits[to, LANES:] = lo
    reach[...] = dot(state_bits[...], jnp.concatenate([c_rows, c_rows], axis=1), NT)
    pulled[...] = dot(d_state_bits[...], jnp.concatenate([b_rows, b_rows], axis=1), NT)
    scores = dot(c_rows, b_rows, NT)
    d_g[...] = jnp.zeros_like(d_g)
    for head in range(heads):
        at = heads_at(head)
        one = slice(first + head, first + head + 1)
        gap_f = columns[:, first + head : first + head + 1] - cum[0][one]
        gap_r = columns[:, 8 + first + head : 9 + first + head] - cum[1][one]
        spread = jnp.exp(jnp.where(is_low, gap_f, gap_r))
        hi, lo = split2(scores * spread)
        a_hi[:, :LANES] = hi * low_one
        a_hi[:, LANES:] = hi * up_one
        a_lo[:, :LANES] = lo * low_one
        a_lo[:, LANES:] = lo * up_one
        grad_bits = pk[k, width + head * WIDTH : width + (head + 1) * WIDTH, :]
        grads = grad_bits.astype(f32)
        xs, bits = [], []
        for index, x_ref in enumerate((x_f, x_r)):
            scaled = x_ref[0, at, :] * step[index][one]
            xs.append(scaled)
            bits.append(split2(scaled))
        d_a = dot(
            jnp.concatenate([grad_bits, grad_bits], axis=0),
            jnp.concatenate(
                [
                    jnp.concatenate([bits[0][0], bits[1][0]], axis=1),
                    jnp.concatenate([bits[0][1], bits[1][1]], axis=1),
                ],
                axis=0,
            ),
            TN,
        )
        d_g[...] += spread * (
            jnp.where(is_low, d_a[:, :LANES], 0.0) + jnp.where(is_up, d_a[:, LANES:], 0.0)
        )
        d_xs = dot(grad_bits, a_hi[...], NN) + dot(grad_bits, a_lo[...], NN)
        out = jnp.zeros((WIDTH, LANES), f32)
        d_skip_line = jnp.zeros((WIDTH, LANES), f32)
        for index, (x_ref, slope_ref, d_pre) in enumerate(
            ((x_f, slope_f, d_pre_f), (x_r, slope_r, d_pre_r))
        ):
            to = heads_at(head, index * width)
            half = slice(index * LANES, (index + 1) * LANES)
            hi, lo = bits[index]
            y = (
                dot(hi, a_hi[:, half], NT)
                + dot(lo, a_hi[:, half], NT)
                + dot(hi, a_lo[:, half], NT)
                + growth[index][one] * reach[to, :]
            )
            x = x_ref[0, at, :]
            out += y + skip[one, :] * x
            d_skip_line += grads * x
            from_state = tail[index][one] * pulled[to, :]
            d_x = d_xs[:, half] + from_state
            d_pre[k + 2, at, :] = (step[index][one] * d_x + skip[one, :] * grads) * slope_ref[
                0, at, :
            ]
            own = jnp.sum(x * d_x, axis=0, keepdims=True)
            line[index, one, :] = (
                jnp.sum(grads * y, axis=0, keepdims=True) - step[index][one] * own
            )
            line[2 + index, one, :] = jnp.sum(
                xs[index] * from_state
                + factor[index][one] * (d_states[to, :] * states[to, :]),
                axis=0,
                keepdims=True,
            )
            line[4 + index, one, :] = own
            hi, lo = split2(grads * growth[index][one])
            gd[to, :LANES] = hi
            gd[to, LANES:] = lo
            hi, lo = split2(xs[index] * tail[index][one])
            xt[to, :LANES] = hi
            xt[to, LANES:] = lo
        rows_out[k, at, :] = out.astype(bf16)
        line[6, one, :] = jnp.sum(d_skip_line, axis=0, keepdims=True)
    g_hi, g_lo = split2(d_g[...])
    wide_c = dot(gd[:, :LANES], state_bits[...], TN)
    wide[0, LANES : 2 * LANES, :] = held(LANES, 2 * LANES) + (
        dot(g_hi, b_rows, NN)
        + dot(g_lo, b_rows, NN)
        + wide_c[:, :LANES]
        + wide_c[:, LANES:]
        + dot(gd[:, LANES:], state_bits[:, :LANES], TN)
    )
    wide_b = dot(xt[:, :LANES], d_state_bits[...], TN)
    wide[0, :LANES, :] = held(0, LANES) + (
        dot(g_hi, c_rows, TN)
        + dot(g_lo, c_rows, TN)
        + wide_b[:, :LANES]
        + wide_b[:, LANES:]
        + dot(xt[:, LANES:], d_state_bits[:, :LANES], TN)
    )
    d_args = jnp.zeros((8, LANES), f32)
    tables = code_tables(pk1[k, TAIL:PACK, :].astype(f32))
    for index in range(2):
        d_log = exact_dot(line[index], (low_one, up_one)[index], NN) + exact_dot(
            line[2 + index], ones, NN
        )
        d_step = line[4 + index] + rate[...] * d_log
        d_arg = d_step * rows[0, rows_at(R_SIG_F + index), :]
        d_args += d_arg
        acc_rows[0] += d_log * rate[...] * step[index]
        acc_rows[2] += exact_dot(d_arg, tables[index], NT)
    acc_rows[1] += line[6]
    wide[0, 2 * LANES : EDGE, :] = held(2 * LANES, EDGE) + d_args
    wide[0, EDGE:, :] = jnp.zeros((WIDE - EDGE, LANES), f32)

    @pl.when(k == GROUP - 1)
    def _():
        edges[...] = edges_in[...] if first else jnp.zeros_like(edges)
        token, place = iota((8, LANES), 0), iota((8, LANES), 1)
        first_rows = zero_one((token < 3) & (place == token))
        last_rows = zero_one((token >= 5) & (place == token + LANES - 8))

        def lines_of(marker, tile):
            hi, mid, lo = split3(tile)
            return dot(marker, hi, NT) + dot(marker, mid, NT) + dot(marker, lo, NT)

        def put_edge(slot, marker):
            def put(head, total):
                channel = (first + head) * WIDTH
                block, offset = channel // LANES, channel % LANES
                edges[slot, block * 8 : block * 8 + 8, offset : offset + WIDTH] = lines_of(
                    marker, total
                )
            return put

        def taps_of(tile, hid, puts):
            for head in range(heads):
                at = heads_at(head)
                hid_here = hid[at, :].astype(f32)
                own_f, own_r = d_pre_f[tile + 1, at, :], d_pre_r[tile + 1, at, :]
                later_f, earlier_r = d_pre_f[tile + 2, at, :], d_pre_r[tile, at, :]
                both = own_f + own_r
                acc[4, at, :] += both
                acc[0, at, :] += hid_here * both
                total = cw[0, at, :] * both
                for tap in range(1, 4):
                    shifted = pltpu.roll(
                        jnp.where(lane >= tap, own_f, later_f), LANES - tap, 1
                    ) + pltpu.roll(jnp.where(lane < LANES - tap, own_r, earlier_r), tap, 1)
                    acc[tap, at, :] += hid_here * shifted
                    total += cw[tap, at, :] * shifted
                for put in puts:
                    put(head, total)

        def keep_chunk(chunk):
            def put(head, total):
                rows_out[chunk, heads_at(head, width), :] = total.astype(bf16)
            return put

        taps_of(0, ext[0], [put_edge(2, last_rows)])
        taps_of(GROUP + 1, ext[GROUP + 1], [put_edge(3, first_rows)])
        taps_of(1, pk[0], [keep_chunk(0), put_edge(0, first_rows)])
        taps_of(GROUP, pk[GROUP - 1], [keep_chunk(GROUP - 1), put_edge(1, last_rows)])

        def inner(chunk, _):
            taps_of(chunk + 1, pk.at[chunk], [keep_chunk(chunk)])
            return 0

        lax.fori_loop(1, GROUP - 1, inner, 0)
        sums = jnp.zeros((8, width), f32)
        for tap in range(5):
            sums += lines_of(zero_one(token == tap), acc[tap])
        conv_out[...] = sums
        head_out[...] = (
            exact_dot(acc_rows[0], zero_one(col == 0), NN)
            + exact_dot(acc_rows[1], zero_one(col == 1), NN)
            + acc_rows[2]
        )


def phase_two(which, place_y, pk1, pk, cw, rate, skip, saved, rows, ends, carried):
    first, last = SETS[which]
    heads = last - first
    width = heads * WIDTH
    outs = [
        jax.ShapeDtypeStruct((GROUP, 2 * width, LANES), bf16),
        jax.ShapeDtypeStruct((GROUP, WIDE, LANES), f32),
        jax.ShapeDtypeStruct((4, 24, LANES), f32),
        jax.ShapeDtypeStruct((8, width), f32),
        jax.ShapeDtypeStruct((8, LANES), f32),
    ]
    whole = [pk1, pk, cw, rate, skip]
    in_specs = (
        [pl.BlockSpec(memory_space=pltpu.SMEM)]
        + [kept(operand.shape) for operand in whole]
        + [chunked((width, LANES))] * 8
        + [chunked((96, LANES)), kept(ends.shape)]
    )
    if which:
        in_specs += [chunked((WIDE, LANES)), kept((4, 24, LANES))]
    return pl.pallas_call(
        functools.partial(phase_two_kernel, first, heads),
        name=f"phase_two_{which}",
        grid=(GROUP,),
        out_shape=outs,
        in_specs=in_specs,
        out_specs=[kept(outs[0].shape), chunked((WIDE, LANES))] + [kept(o.shape) for o in outs[2:]],
        scratch_shapes=[
            pltpu.VMEM((GROUP + 2, width, LANES), bf16),
            pltpu.VMEM((4, width, LANES), f32),
            pltpu.VMEM((2 * width, LANES), f32),
            pltpu.VMEM((2 * width, LANES), f32),
            pltpu.VMEM((2 * width, 2 * LANES), bf16),
            pltpu.VMEM((2 * width, 2 * LANES), bf16),
            pltpu.VMEM((2 * width, LANES), f32),
            pltpu.VMEM((2 * width, LANES), f32),
            pltpu.VMEM((2 * width, 2 * LANES), bf16),
            pltpu.VMEM((2 * width, 2 * LANES), bf16),
            pltpu.VMEM((GROUP + 4, width, LANES), f32),
            pltpu.VMEM((GROUP + 4, width, LANES), f32),
            pltpu.VMEM((5, width, LANES), f32),
            pltpu.VMEM((7, 8, LANES), f32),
            pltpu.VMEM((3, 8, LANES), f32),
            pltpu.VMEM((LANES, LANES), f32),
            pltpu.VMEM((LANES, 2 * LANES), bf16),
            pltpu.VMEM((LANES, 2 * LANES), bf16),
        ],
        cost_estimate=cost(2 * heads),
        compiler_params=pltpu.CompilerParams(vmem_limit_bytes=VMEM),
    )(place_y, *whole, *saved, rows, ends, *carried)


def unpack_kernel(place_z, rows_1, rows_2, wide, layer_out, hid_out, b_out, c_out, dt_out):
    row, col = square_masks()
    eye = zero_one(row == col)
    cut = SETS[0][1] * WIDTH
    line = iota((16, LANES), 0)
    at_start = (line < 3) & (place_z[0] == 0)
    at_end = (line >= 13) & (place_z[0] == GROUP - 1)
    blank = jnp.zeros((8, LANES), f32)
    for order, target in enumerate((layer_out, hid_out)):
        for block in range(GROUP * CH // LANES):
            pieces, edge = [], []
            for half in range(2):
                channel = block * LANES + half * WIDTH
                group, at = channel // CH, channel % CH
                offset = at % LANES
                start = EDGE + at // LANES * 8
                edge.append(wide[group, start : start + 8, offset : offset + WIDTH])
                ref, at = (rows_1, at + order * cut) if at < cut else (
                    rows_2, at - cut + order * (CH - cut)
                )
                pieces.append(ref[group, at : at + WIDTH, :])
            lanes = slice(block * LANES, (block + 1) * LANES)
            flipped = dot(eye, jnp.concatenate(pieces, axis=0), NT)
            if order:
                edge = jnp.concatenate(edge, axis=1)
                head = jnp.where(at_start, jnp.concatenate([edge, blank], axis=0), flipped[:16])
                tail = jnp.where(
                    at_end, jnp.concatenate([blank, edge], axis=0), flipped[LANES - 16 :]
                )
                flipped = jnp.concatenate([head, flipped[16 : LANES - 16], tail], axis=0)
            target[:, lanes] = flipped.astype(bf16)
    for base, target in ((0, b_out), (LANES, c_out)):
        total = wide[0, base : base + LANES, :]
        for group in range(1, GROUP):
            total += wide[group, base : base + LANES, :]
        target[...] = total
    lines = jnp.concatenate(
        [wide[group, 2 * LANES : 2 * LANES + 8, :] for group in range(GROUP)]
        + [jnp.zeros((LANES - 8 * GROUP, LANES), f32)],
        axis=0,
    ).T
    pick_row, pick_col = iota((LANES, 40), 0), iota((LANES, 40), 1)
    pick = zero_one(
        ((pick_row % 8) < HEADS) & ((pick_row // 8) * HEADS + (pick_row % 8) == pick_col)
    )
    dt_out[...] = exact_dot(lines, pick, NN)


def unpack(place_z, rows_1, rows_2, wide):
    rows = jax.ShapeDtypeStruct((LANES, GROUP * CH), bf16)
    square = jax.ShapeDtypeStruct((LANES, LANES), f32)
    return pl.pallas_call(
        unpack_kernel,
        name="unpack",
        out_shape=[rows, rows, square, square, jax.ShapeDtypeStruct((LANES, 40), f32)],
        in_specs=[pl.BlockSpec(memory_space=pltpu.SMEM)] + [WHOLE] * 3,
        out_specs=[WHOLE] * 5,
        compiler_params=pltpu.CompilerParams(vmem_limit_bytes=VMEM),
    )(place_z, rows_1, rows_2, wide)


def exchange(array):
    return lax.all_to_all(array, "seq", 0, 0, axis_index_groups=Z_GROUPS)


def along_y(array, by):
    pairs = [
        (y * GROUP + z, (y + by) * GROUP + z)
        for y in range(ROWS)
        for z in range(GROUP)
        if 0 <= y + by < ROWS
    ]
    return lax.ppermute(array, "seq", pairs)


def beside(array, by):
    count = lax.axis_size("seq")
    return lax.ppermute(array, "seq", [(i, i + by) for i in range(count) if 0 <= i + by < count])


def cross_y(up, down, run):
    later = (jnp.arange(ROWS) > run)[:, None, None]
    return lax.all_to_all(
        jnp.where(later, up[None], down[None]), "seq", 0, 0, axis_index_groups=Y_GROUPS
    )


def flip_bit(array, axis, bit):
    count = lax.axis_size(axis)
    return lax.ppermute(array, axis, [(i, i ^ bit) for i in range(count)])


def total_over_all(array):
    for axis, bit in (("dp", 1), ("dp", 2), ("dp", 4), ("seq", 8), ("seq", 16)):
        array = array + flip_bit(array, axis, bit)
    array = array[None]
    place = lax.axis_index("seq")
    for bit in (1, 2, 4):
        other = flip_bit(array, "seq", bit)
        is_high = (place & bit) != 0
        array = jnp.concatenate(
            [jnp.where(is_high, other, array), jnp.where(is_high, array, other)], axis=0
        )
    return array


def per_device(
    hidden, b_proj, c_proj, dt_raw, base_ids, complement,
    a_log, d_skip, dt_bias, base_shift, conv_w, conv_b, grad_out,
):
    place = lax.axis_index("seq")
    group, run = place % GROUP, place // GROUP
    here_z, here_y = group[None].astype(jnp.int32), run[None].astype(jnp.int32)
    before = beside(hidden[0, -8:], 1)
    after = beside(hidden[0, :8], -1)
    taps = jnp.concatenate([conv_w, conv_b[None]], axis=0).reshape(5, GROUP, CH)
    taps = lax.dynamic_index_in_dim(taps, group, 1, keepdims=False)
    cw = jnp.broadcast_to(taps[:, :, None], (5, CH, LANES))
    per_head = jnp.stack([-jnp.exp(a_log), d_skip], axis=0)
    tables = jnp.concatenate([dt_bias[None], base_shift], axis=0)
    tables = jnp.concatenate([per_head, tables], axis=0).reshape(15, GROUP, HEADS)
    tables = lax.dynamic_index_in_dim(tables, group, 1, keepdims=False)
    tables = jnp.pad(tables, ((0, 0), (0, 8 - HEADS)))
    rate = jnp.broadcast_to(tables[0][:, None], (8, LANES))
    skip = jnp.broadcast_to(tables[1][:, None], (8, LANES))
    shift_table = jnp.pad(tables[2:].T, ((0, 0), (2, LANES - 15)))

    cut = SETS[0][1] * WIDTH
    taps = (cw[:, :cut], cw[:, cut:])

    packed = pack(
        complement, hidden[0], grad_out[0], b_proj[0], c_proj[0], dt_raw[0], base_ids, before, after
    )
    pk = [exchange(part) for part in packed]
    *saved_0, rows, up_0, down_0 = phase_one(0, pk[0], pk[0], taps[0], (shift_table, rate))
    ends_0 = cross_y(up_0, down_0, run)
    *saved_1, up_1, down_1 = phase_one(1, pk[0], pk[1], taps[1], (rows,))
    ends_1 = cross_y(up_1, down_1, run)
    rows_0, wide, edges, conv_0, head_0 = phase_two(
        0, here_y, pk[0], pk[0], taps[0], rate, skip, saved_0, rows, ends_0, ()
    )
    rows_0 = exchange(rows_0)
    rows_1, wide, edges, conv_1, head_1 = phase_two(
        1, here_y, pk[0], pk[1], taps[1], rate, skip, saved_1, rows, ends_1, (wide, edges)
    )
    rows_1 = exchange(rows_1)
    from_next = along_y(edges[2], -1)
    from_prev = along_y(edges[3], 1)
    wide = wide.at[0, EDGE:].set(edges[0] + from_prev)
    wide = wide.at[GROUP - 1, EDGE:].set(edges[1] + from_next)
    wide = exchange(wide)
    sums = total_over_all(jnp.concatenate([conv_0, conv_1, head_0 + head_1], axis=1))
    layer_out, d_hidden, d_b, d_c, d_dt = unpack(here_z, rows_0, rows_1, wide)

    conv_all = sums[:, :5, :CH].transpose(1, 0, 2).reshape(5, GROUP * CH)
    head_all = sums[:, :HEADS, CH : CH + 15].reshape(GROUP * HEADS, 15)
    return (
        layer_out[None], d_hidden[None], d_b[None], d_c[None], d_dt[None],
        head_all[:, 0], head_all[:, 1], head_all[:, 2], head_all[:, 3:].T,
        conv_all[:4], conv_all[4],
    )


def solution(mesh):
    rows = P("dp", "seq", None)
    placed = (rows, rows, rows, rows, P("dp", "seq"), P(), P(), P(), P(), P(), P(), P(), rows)
    return jax.shard_map(
        per_device,
        mesh=mesh,
        in_specs=placed,
        out_specs=(rows,) * 5 + (P(),) * 6,
        check_vma=False,
    )
```

time: 1520 us -> 226 us (0.15); the launches traced: 1500 us -> 224 us
  waiting for transfers between devices: 629 us -> 75.6 us
  other arithmetic: 302 us -> 8.32 us
  local copies, waits for them, and re-layouts: 302 us -> 16.3 us
  blocking collectives: 160 us -> 0 us
  matrix products: 72.2 us -> 0 us
  Pallas kernels: 0 us -> 62.5 us
  starting transfers between devices: 13.1 us -> 60.6 us
    all_gather x4 -> x0, waiting for transfers between devices: 629 us -> none  [prefix(): pieces = jax.tree.map(lambda part: lax.all_gather(part, axis), value)]
    select_n x124 -> x5, other arithmetic: 244 us -> 3.96 us  [the longest x2 3.94 us: cross_y(): jnp.where(later, up[None], down[None])]
    mul x126 -> x0, local copies, waits for them, and re-layouts: 101 us -> none  [the longest x124 101 us: chain_link(): later[1][:, None, None] * earlier[0] + later[0]]
    all_gather x2 -> x0, blocking collectives: 85.2 us -> none  [prefix(): pieces = jax.tree.map(lambda part: lax.all_gather(part, axis), value)]
    psum x1 -> x0, blocking collectives: 75.1 us -> none  [per_device(): lax.psum((params_fwd[0] + params_rev[0], params_fwd[1] + params_rev[1], p...]
    rev x13 -> x0, local copies, waits for them, and re-layouts: 73.2 us -> none  [the longest x4 60.4 us: prefix(): pieces = jax.tree.map(lambda part: part[::-1], pieces)]
    dot_general x28 -> x0, matrix products: 72.2 us -> none  [the longest x6 29.3 us: section_one(): jnp.einsum('tsh,shp->thp', weights, values, precision=exact_prec)]
    pallas_call x0 -> x6, Pallas kernels: none -> 62.5 us  [the longest x2 35 us: phase_two(): pl.pallas_call(functools.partial(phase_two_kernel, first, heads), name=f'...]
  transfers between devices with their start and end apart: 8 -> 19, of which waited for: 4 -> 11; matrix products, arithmetic and copies ran while one was open for 27% -> 9% of each run, Pallas kernels for 0% -> 25%
where the time goes in v2:
time: 226 us; the launch traced here: 224 us
  waiting for transfers between devices  75.6 us (33%)
  Pallas kernels  62.5 us (28%)
  starting transfers between devices  60.6 us (27%)
  local copies, waits for them, and re-layouts  16.3 us (7%)
  other arithmetic  8.32 us (4%)
    all_to_all x5, waiting for transfers between devices, exchange(): return lax.all_to_all(array, 'seq', 0, 0, axis_index_groups=Z_GROUPS)  47.1 us
    pallas_call x2, Pallas kernels, phase_two(): pl.pallas_call(functools.partial(phase_two_kernel, first, heads), name=f'...  35 us
    all_to_all x5, starting transfers between devices, exchange(): return lax.all_to_all(array, 'seq', 0, 0, axis_index_groups=Z_GROUPS)  26.2 us
    ppermute x8, waiting for transfers between devices, flip_bit(): return lax.ppermute(array, axis, [(i, i ^ bit) for i in range(count)])  25.3 us
    pallas_call x2, Pallas kernels, phase_one(): pl.pallas_call(functools.partial(phase_one_kernel, first, heads), name=f'...  20.2 us
    ppermute x8, starting transfers between devices, flip_bit(): return lax.ppermute(array, axis, [(i, i ^ bit) for i in range(count)])  14.8 us
    all_to_all x2, starting transfers between devices, cross_y(): lax.all_to_all(jnp.where(later, up[None], down[None]), 'seq', 0, 0, axis_...  9.26 us
    unnamed x47, local copies, waits for them, and re-layouts  5.5 us
  transfers between devices with their start and end apart: 19, of which 11 were waited for; matrix products, arithmetic and copies ran while one was open for 9% of the time, Pallas kernels for 25%

profile of v2, /device:TPU:6, one launch (start us, length us, event | category | flops | bytes accessed | tf_op | source)
XLA Modules:
  0.0 224.4 jit_solution(18243371307013884632)
XLA Ops:
  0.6 0.8 slice_bitcast_fusion
  1.5 3.8 %collective-permute-start = (bf16[8,2560]{1,0:T(8,128)(2,1)S(1)}, bf16[8,2560]{1,0:T(8,128)(2,1)S(1)}, u32[]{:S(2)}, u32[]{:S(2)}) collective-permute-start(bf16[8,2560]{1,0:T(8,128)(2,1)S(1)} %get-tuple-element.150), channel_id=1, source_target_pairs={{0,1},{1,2},{2,3},{3,4},{4,5},{5,6},{6,7},{7,8},{8,9},{9,10},{10,1... | collective-permute-start | bytes 122888 | tf_op jit(solution)/shard_map/ppermute | solution.py:724
  5.3 1.3 collective-permute-start.1
  6.6 1.5 copy.42
  8.0 3.1 %collective-permute-done.1.after_ref = bf16[8,2560]{1,0:T(8,128)(2,1)S(1)} collective-permute-done((bf16[8,2560]{1,0:T(8,128)(2,1)S(1)}, bf16[8,2560]{1,0:T(8,128)(2,1)S(1)}, u32[]{:S(2)}, u32[]{:S(2)}) %collective-permute-start.1) | collective-permute-done | bytes 40992 | tf_op jit(solution)/shard_map/ppermute | solution.py:724
  11.2 0.6 copy-done.10
  11.8 3.7 %pack.1 = (bf16[8,576,128]{2,1,0:T(8,128)(2,1)}, bf16[8,384,128]{2,1,0:T(8,128)(2,1)}) custom-call(s32[12]{0:T(128)} %comp_ref.1, bf16[128,2560]{1,0:T(8,128)(2,1)} %bitcast.49, bf16[128,2560]{1,0:T(8,128)(2,1)} %bitcast.50, bf16[128,128]{1,0:T(8,128)(2,1)} %bitcast.55, bf16[128,128]{1,0:T(8,128)(2,1)} %bitcast.56, f32[128,40]{1,0:T(8,128)} %bitcast.51, ...), custom_call_target="tpu_custom_call" | custom-call | tf_op jit(solution)/shard_map/pack/pallas_call | solution.py:120
  15.5 8.5 %all-to-all-start = ((bf16[8,576,128]{2,1,0:T(8,128)(2,1)}), bf16[8,576,128]{2,1,0:T(8,128)(2,1)S(1)}, u32[]{:S(2)}, u32[]{:S(2)}) async-start(bf16[8,576,128]{2,1,0:T(8,128)(2,1)} %get-tuple-element.73), calls=%async_computation | async-start | bytes 2359296 | tf_op jit(solution)/shard_map/all_to_all | solution.py:709
  24.0 0.1 concatenate.40
  24.2 29.9 %all-to-all-done.refs_0_.refs_1_.refs_2_ = bf16[8,576,128]{2,1,0:T(8,128)(2,1)S(1)} async-done(((bf16[8,576,128]{2,1,0:T(8,128)(2,1)}), bf16[8,576,128]{2,1,0:T(8,128)(2,1)S(1)}, u32[]{:S(2)}, u32[]{:S(2)}) %all-to-all-start) | async-done | bytes 1179680 | tf_op jit(solution)/shard_map/all_to_all | solution.py:709
  54.1 3.5 %all-to-all-start.3 = ((bf16[8,384,128]{2,1,0:T(8,128)(2,1)}), bf16[8,384,128]{2,1,0:T(8,128)(2,1)S(1)}, u32[]{:S(2)}, u32[]{:S(2)}) async-start(bf16[8,384,128]{2,1,0:T(8,128)(2,1)} %get-tuple-element.86), calls=%async_computation.3 | async-start | bytes 1572864 | tf_op jit(solution)/shard_map/all_to_all | solution.py:709
  57.7 0.1 concatenate.53
  57.8 0.1 concatenate.54
  58.0 0.1 concatenate.55
  58.1 0.1 copy.43
  58.2 0.1 fusion.5
  58.3 0.7 pad.17.refs_2_
  59.0 0.2 slice_reduce_fusion.4
  59.2 0.9 broadcast_in_dim.107.refs_1_.refs_3_
  60.1 0.7 broadcast_in_dim.109.refs_3_.refs_4_
  60.8 10.9 %phase_one_0.1 = (f32[8,128,128]{2,1,0:T(8,128)}, f32[8,128,128]{2,1,0:T(8,128)}, f32[8,128,128]{2,1,0:T(8,128)}, f32[8,128,128]{2,1,0:T(8,128)}, f32[8,128,128]...) custom-call(bf16[8,576,128]{2,1,0:T(8,128)(2,1)} %copy-done.3, ...), custom_call_target="tpu_custom_call" | custom-call | flops 8000000000 | bytes 8000000 | tf_op jit(solution)/shard_map/phase_one_0/pallas_call | solution.py:320
  71.7 1.9 broadcast_select_fusion.1
  73.5 7.6 %all-to-all-done.3.refs_1_.refs_2_ = bf16[8,384,128]{2,1,0:T(8,128)(2,1)S(1)} async-done(((bf16[8,384,128]{2,1,0:T(8,128)(2,1)}), bf16[8,384,128]{2,1,0:T(8,128)(2,1)S(1)}, u32[]{:S(2)}, u32[]{:S(2)}) %all-to-all-start.3) | async-done | bytes 786464 | tf_op jit(solution)/shard_map/all_to_all | solution.py:709
  81.2 4.5 %all-to-all-start.1 = ((f32[4,272,128]{2,1,0:T(8,128)}), f32[4,272,128]{2,1,0:T(8,128)S(1)}, u32[]{:S(2)}, u32[]{:S(2)}) async-start(f32[4,272,128]{2,1,0:T(8,128)} %broadcast_select_fusion.1), calls=%async_computation.1 | async-start | bytes 1114112 | tf_op jit(solution)/shard_map/all_to_all | solution.py:729
  85.6 1.0 broadcast_in_dim.115.refs_2_.refs_3_
  86.6 9.3 %phase_one_1.1 = (f32[8,192,128]{2,1,0:T(8,128)}, f32[8,192,128]{2,1,0:T(8,128)}, f32[8,192,128]{2,1,0:T(8,128)}, f32[8,192,128]{2,1,0:T(8,128)}, f32[8,192,128]...) custom-call(bf16[8,576,128]{2,1,0:T(8,128)(2,1)} %copy-done.3, ...), custom_call_target="tpu_custom_call" | custom-call | flops 12000000000 | bytes 8000000 | tf_op jit(solution)/shard_map/phase_one_1/pallas_call | solution.py:320
  95.9 2.1 broadcast_select_fusion
  98.0 4.8 %all-to-all-start.4 = ((f32[4,400,128]{2,1,0:T(8,128)}), f32[4,400,128]{2,1,0:T(8,128)S(1)}, u32[]{:S(2)}, u32[]{:S(2)}) async-start(f32[4,400,128]{2,1,0:T(8,128)} %broadcast_select_fusion), calls=%async_computation.4 | async-start | bytes 1638400 | tf_op jit(solution)/shard_map/all_to_all | solution.py:729
  102.8 0.7 broadcast_in_dim.111.refs_5_
  103.4 15.6 %phase_two_0.1 = (bf16[8,256,128]{2,1,0:T(8,128)(2,1)}, f32[8,288,128]{2,1,0:T(8,128)}, f32[4,24,128]{2,1,0:T(8,128)}, f32[8,128]{1,0:T(8,128)}, f32[8,128]{1,0:T(8,128)}) custom-call(s32[1]{0:T(128)} %bitcast.1.refs_0_, bf16[8,576,128]{2,1,0:T(8,128)(2,1)} %copy-done.3, bf16[8,576,128]{2,1,0:T(8,128)(2,1)} %copy-done.3, ...), custom_call_target="tpu_custom_call" | custom-call | flops 16000000000 | bytes 8000000 | tf_op jit(solution)/shard_map/phase_two_0/pallas_call | solution.py:615
  119.1 3.5 %all-to-all-start.2 = ((bf16[8,256,128]{2,1,0:T(8,128)(2,1)}), bf16[8,256,128]{2,1,0:T(8,128)(2,1)S(1)}, u32[]{:S(2)}, u32[]{:S(2)}) async-start(bf16[8,256,128]{2,1,0:T(8,128)(2,1)} %get-tuple-element.85), calls=%async_computation.2 | async-start | bytes 1048576 | tf_op jit(solution)/shard_map/all_to_all | solution.py:709
  122.6 19.4 %phase_two_1.1 = (bf16[8,384,128]{2,1,0:T(8,128)(2,1)}, f32[8,288,128]{2,1,0:T(8,128)}, f32[4,24,128]{2,1,0:T(8,128)}, f32[8,192]{1,0:T(8,128)}, f32[8,128]{1,0:T(8,128)}) custom-call(s32[1]{0:T(128)} %bitcast.1.refs_0_, bf16[8,576,128]{2,1,0:T(8,128)(2,1)} %copy-done.3, bf16[8,384,128]{2,1,0:T(8,128)(2,1)} %copy-done.5, ...), custom_call_target="tpu_custom_call" | custom-call | flops 24000000000 | bytes 8000000 | tf_op jit(solution)/shard_map/phase_two_1/pallas_call | solution.py:615
  142.1 7.1 %all-to-all-start.5 = ((bf16[8,384,128]{2,1,0:T(8,128)(2,1)}), bf16[8,384,128]{2,1,0:T(8,128)(2,1)S(1)}, u32[]{:S(2)}, u32[]{:S(2)}) async-start(bf16[8,384,128]{2,1,0:T(8,128)(2,1)} %get-tuple-element.99), calls=%async_computation.5 | async-start | bytes 1572864 | tf_op jit(solution)/shard_map/all_to_all | solution.py:709
  149.2 0.6 fusion.7
  149.8 0.7 and_reduce_fusion
  150.5 3.9 %collective-permute-start.2 = (f32[24,128]{1,0:T(8,128)S(1)}, f32[24,128]{1,0:T(8,128)S(1)}, u32[]{:S(2)}, u32[]{:S(2)}) collective-permute-start(f32[24,128]{1,0:T(8,128)S(1)} %get-tuple-element.156), channel_id=1, source_target_pairs={{0,8},{1,9},{2,10},{3,11},{4,12},{5,13},{6,14},{7,15},{8,16},{9,17... | collective-permute-start | bytes 36872 | tf_op jit(solution)/shard_map/ppermute | solution.py:719
  154.4 1.3 collective-permute-start.3
  155.9 2.7 %bitcast_select_fusion = f32[1,24,128]{2,1,0:T(8,128)S(1)} fusion(f32[24,128]{1,0:T(8,128)S(1)} %collective-permute-done.2, f32[8,288,128]{2,1,0:T(8,128)} %get-tuple-element.100, s32[]{:T(128)} %bitcast.14, s32[]{:T(128)} %bitcast.15, f32[4,24,128]{2,1,0:T(8,128)S(1)} %copy-done.7, pred[]{:T(512)} %and_reduce_fusion), kind=kLoop, calls=%fused_computation.29 | loop fusion | flops 6144 | bytes 49161 | tf_op jit(solution)/shard_map/select.2
  158.6 2.6 %scatter.6 = f32[8,288,128]{2,1,0:T(8,128)} dynamic-update-slice(f32[8,288,128]{2,1,0:T(8,128)} %get-tuple-element.100, f32[1,24,128]{2,1,0:T(8,128)S(1)} %bitcast_select_fusion, s32[]{:T(128)} %bitcast.14, s32[]{:T(128)} %bitcast.15, s32[]{:T(128)} %constant.91.clone.1) | dynamic-update-slice | bytes 24580 | tf_op jit(solution)/shard_map/scatter | solution.py:795
  161.2 0.6 bitcast_dynamic-update-slice_fusion
  161.8 9.6 %all-to-all-done.5.rows_2 = bf16[8,384,128]{2,1,0:T(8,128)(2,1)S(1)} async-done(((bf16[8,384,128]{2,1,0:T(8,128)(2,1)}), bf16[8,384,128]{2,1,0:T(8,128)(2,1)S(1)}, u32[]{:S(2)}, u32[]{:S(2)}) %all-to-all-start.5) | async-done | bytes 786464 | tf_op jit(solution)/shard_map/all_to_all | solution.py:709
  171.4 3.6 %all-to-all-start.6 = ((f32[8,288,128]{2,1,0:T(8,128)}), f32[8,288,128]{2,1,0:T(8,128)S(1)}, u32[]{:S(2)}, u32[]{:S(2)}) async-start(f32[8,288,128]{2,1,0:T(8,128)} %bitcast_dynamic-update-slice_fusion), calls=%async_computation.6 | async-start | bytes 2359296 | tf_op jit(solution)/shard_map/all_to_all | solution.py:709
  175.1 0.9 collective-permute-start.5
  175.9 2.9 %collective-permute-done.5 = f32[8,448]{1,0:T(8,128)S(1)} collective-permute-done((f32[8,448]{1,0:T(8,128)S(1)}, f32[8,448]{1,0:T(8,128)S(1)}, u32[]{:S(2)}, u32[]{:S(2)}) %collective-permute-start.5) | collective-permute-done | bytes 14368 | tf_op jit(solution)/shard_map/ppermute | solution.py:736
  178.8 1.4 collective-permute-start.6
  180.3 3.8 %collective-permute-done.6 = f32[8,448]{1,0:T(8,128)S(1)} collective-permute-done((f32[8,448]{1,0:T(8,128)S(1)}, f32[8,448]{1,0:T(8,128)S(1)}, u32[]{:S(2)}, u32[]{:S(2)}) %collective-permute-start.6) | collective-permute-done | bytes 14368 | tf_op jit(solution)/shard_map/ppermute | solution.py:736
  184.1 1.7 collective-permute-start.7
  185.8 2.0 collective-permute-done.7
  187.8 3.2 %collective-permute-start.8 = (f32[8,448]{1,0:T(8,128)S(1)}, f32[8,448]{1,0:T(8,128)S(1)}, u32[]{:S(2)}, u32[]{:S(2)}) collective-permute-start(f32[8,448]{1,0:T(8,128)S(1)} %add.51), channel_id=1, source_target_pairs={{0,16},{1,17},{2,18},{3,19},{4,20},{5,21},{6,22},{7,23},{8,24},{9,... | collective-permute-start | bytes 43016 | tf_op jit(solution)/shard_map/ppermute | solution.py:736
  191.1 2.0 collective-permute-done.8
  193.1 1.9 collective-permute-start.9
  195.0 7.0 %collective-permute-done.9 = f32[1,8,448]{2,1,0:T(8,128)S(1)} collective-permute-done((f32[1,8,448]{2,1,0:T(8,128)S(1)}, f32[1,8,448]{2,1,0:T(8,128)S(1)}, u32[]{:S(2)}, u32[]{:S(2)}) %collective-permute-start.9) | collective-permute-done | bytes 14368 | tf_op jit(solution)/shard_map/ppermute | solution.py:736
  202.1 0.8 collective-permute-start.10
  202.9 4.1 %collective-permute-done.10 = f32[2,8,448]{2,1,0:T(8,128)S(1)} collective-permute-done((f32[2,8,448]{2,1,0:T(8,128)S(1)}, f32[2,8,448]{2,1,0:T(8,128)S(1)}, u32[]{:S(2)}, u32[]{:S(2)}) %collective-permute-start.10) | collective-permute-done | bytes 28704 | tf_op jit(solution)/shard_map/ppermute | solution.py:736
  207.0 4.9 %collective-permute-start.11 = (f32[4,8,448]{2,1,0:T(8,128)S(1)}, f32[4,8,448]{2,1,0:T(8,128)S(1)}, u32[]{:S(2)}, u32[]{:S(2)}) collective-permute-start(f32[4,8,448]{2,1,0:T(8,128)S(1)} %pad_maximum_fusion.1), channel_id=1, source_target_pairs={{0,4},{1,5},{2,6},{3,7},{4,0},{5,1},{6,2},{7,3},{8,12},{9,13},{10,... | collective-permute-start | bytes 172040 | tf_op jit(solution)/shard_map/ppermute | solution.py:736
  211.9 3.4 %collective-permute-done.11 = f32[4,8,448]{2,1,0:T(8,128)S(1)} collective-permute-done((f32[4,8,448]{2,1,0:T(8,128)S(1)}, f32[4,8,448]{2,1,0:T(8,128)S(1)}, u32[]{:S(2)}, u32[]{:S(2)}) %collective-permute-start.11) | collective-permute-done | bytes 57376 | tf_op jit(solution)/shard_map/ppermute | solution.py:736
  215.3 0.1 pad_maximum_fusion.2
  215.4 0.7 copy.49
  216.1 0.7 slice.138
  216.9 0.7 squeeze.66
  217.6 0.7 slice_reduce_fusion
  218.3 1.0 copy-done
  219.3 3.6 %unpack.1 = (bf16[128,2560]{1,0:T(8,128)(2,1)}, bf16[128,2560]{1,0:T(8,128)(2,1)}, f32[128,128]{1,0:T(8,128)}, f32[128,128]{1,0:T(8,128)}, f32[128,40]{1,0:T(8,128)}) custom-call(s32[1]{0:T(128)} %bitcast.place_z, bf16[8,256,128]{2,1,0:T(8,128)(2,1)} %copy-done.2, bf16[8,384,128]{2,1,0:T(8,128)(2,1)} %copy-done.1, f32[8,288,128]{2,1,0:T(8,128)} %copy-done), custom_call_target="tpu_custom_call" | custom-call | tf_op jit(solution)/shard_map/unpack/pallas_call | solution.py:698
  222.9 1.5 copy.48
  (78 shorter events, 0.7 us)
Async XLA Ops:
  1.5 6.6 %collective-permute-start = (bf16[8,2560]{1,0:T(8,128)(2,1)S(1)}, bf16[8,2560]{1,0:T(8,128)(2,1)S(1)}, u32[]{:S(2)}, u32[]{:S(2)}) collective-permute-start(bf16[8,2560]{1,0:T(8,128)(2,1)S(1)} %get-tuple-element.150), channel_id=1, source_target_pairs={{0,1},{1,2},{2,3},{3,4},{4,5},{5,6},{6,7},{7,8},{8,9},{9,10},{10,1... | collective-permute-start | bytes 122888 | tf_op jit(solution)/shard_map/ppermute | solution.py:724
  5.3 5.9 %collective-permute-start.1 = (bf16[8,2560]{1,0:T(8,128)(2,1)S(1)}, bf16[8,2560]{1,0:T(8,128)(2,1)S(1)}, u32[]{:S(2)}, u32[]{:S(2)}) collective-permute-start(bf16[8,2560]{1,0:T(8,128)(2,1)S(1)} %get-tuple-element.149), channel_id=1, source_target_pairs={{1,0},{2,1},{3,2},{4,3},{5,4},{6,5},{7,6},{8,7},{9,8},{10,9},{11,1... | collective-permute-start | bytes 122888 | tf_op jit(solution)/shard_map/ppermute | solution.py:724
  8.0 3.1 %copy-start.9 = (bf16[8,2560]{1,0:T(8,128)(2,1)}, bf16[8,2560]{1,0:T(8,128)(2,1)S(1)}, u32[]{:S(2)}) copy-start(bf16[8,2560]{1,0:T(8,128)(2,1)S(1)} %collective-permute-done.before_ref) | copy-start | bytes 122884
  11.2 0.6 copy-start.10
  15.5 8.5 %copy-start.8 = (f32[4,2560]{1,0:T(4,128)S(1)}, f32[4,2560]{1,0:T(4,128)}, u32[]{:S(2)}) copy-start(f32[4,2560]{1,0:T(4,128)} %param.27) | copy-start | bytes 122884
  15.5 8.6 %copy-start.13 = (f32[2560]{0:T(1024)S(1)}, f32[2560]{0:T(1024)}, u32[]{:S(2)}) copy-start(f32[2560]{0:T(1024)} %param.28) | copy-start | bytes 30724
  15.5 8.7 %copy-start.20 = (f32[40]{0:T(128)S(1)}, f32[40]{0:T(128)}, u32[]{:S(2)}) copy-start(f32[40]{0:T(128)} %param.23) | copy-start | bytes 484
  15.5 38.6 %all-to-all-start = ((bf16[8,576,128]{2,1,0:T(8,128)(2,1)}), bf16[8,576,128]{2,1,0:T(8,128)(2,1)S(1)}, u32[]{:S(2)}, u32[]{:S(2)}) async-start(bf16[8,576,128]{2,1,0:T(8,128)(2,1)} %get-tuple-element.73), calls=%async_computation | async-start | bytes 2359296 | tf_op jit(solution)/shard_map/all_to_all | solution.py:709
  24.0 33.8 %copy-start.17 = (f32[40]{0:T(128)S(1)}, f32[40]{0:T(128)}, u32[]{:S(2)}) copy-start(f32[40]{0:T(128)} %param.24) | copy-start | bytes 484
  24.0 34.0 %copy-start.18 = (f32[40]{0:T(128)S(1)}, f32[40]{0:T(128)}, u32[]{:S(2)}) copy-start(f32[40]{0:T(128)} %param.25) | copy-start | bytes 484
  24.0 34.1 %copy-start.14 = (f32[12,40]{1,0:T(8,128)S(1)}, f32[12,40]{1,0:T(8,128)}, u32[]{:S(2)}) copy-start(f32[12,40]{1,0:T(8,128)} %param.26) | copy-start | bytes 5764
  54.1 6.0 %copy-start.3 = (bf16[8,576,128]{2,1,0:T(8,128)(2,1)}, bf16[8,576,128]{2,1,0:T(8,128)(2,1)S(1)}, u32[]{:S(2)}) copy-start(bf16[8,576,128]{2,1,0:T(8,128)(2,1)S(1)} %all-to-all-done.refs_0_.refs_1_.refs_2_) | copy-start | bytes 3538948
  54.1 27.1 %all-to-all-start.3 = ((bf16[8,384,128]{2,1,0:T(8,128)(2,1)}), bf16[8,384,128]{2,1,0:T(8,128)(2,1)S(1)}, u32[]{:S(2)}, u32[]{:S(2)}) async-start(bf16[8,384,128]{2,1,0:T(8,128)(2,1)} %get-tuple-element.86), calls=%async_computation.3 | async-start | bytes 1572864 | tf_op jit(solution)/shard_map/all_to_all | solution.py:709
  81.2 5.4 %copy-start.5 = (bf16[8,384,128]{2,1,0:T(8,128)(2,1)}, bf16[8,384,128]{2,1,0:T(8,128)(2,1)S(1)}, u32[]{:S(2)}) copy-start(bf16[8,384,128]{2,1,0:T(8,128)(2,1)S(1)} %all-to-all-done.3.refs_1_.refs_2_) | copy-start | bytes 2359300
  81.2 16.8 %all-to-all-start.1 = ((f32[4,272,128]{2,1,0:T(8,128)}), f32[4,272,128]{2,1,0:T(8,128)S(1)}, u32[]{:S(2)}, u32[]{:S(2)}) async-start(f32[4,272,128]{2,1,0:T(8,128)} %broadcast_select_fusion.1), calls=%async_computation.1 | async-start | bytes 1114112 | tf_op jit(solution)/shard_map/all_to_all | solution.py:729
  98.0 5.5 %copy-start.6 = (f32[4,272,128]{2,1,0:T(8,128)}, f32[4,272,128]{2,1,0:T(8,128)S(1)}, u32[]{:S(2)}) copy-start(f32[4,272,128]{2,1,0:T(8,128)S(1)} %all-to-all-done.1.refs_15_) | copy-start | bytes 1671172
  98.0 21.1 %all-to-all-start.4 = ((f32[4,400,128]{2,1,0:T(8,128)}), f32[4,400,128]{2,1,0:T(8,128)S(1)}, u32[]{:S(2)}, u32[]{:S(2)}) async-start(f32[4,400,128]{2,1,0:T(8,128)} %broadcast_select_fusion), calls=%async_computation.4 | async-start | bytes 1638400 | tf_op jit(solution)/shard_map/all_to_all | solution.py:729
  119.0 3.5 %copy-start.4 = (f32[4,400,128]{2,1,0:T(8,128)}, f32[4,400,128]{2,1,0:T(8,128)S(1)}, u32[]{:S(2)}) copy-start(f32[4,400,128]{2,1,0:T(8,128)S(1)} %all-to-all-done.4.refs_15_) | copy-start | bytes 2457604
  119.1 23.0 %all-to-all-start.2 = ((bf16[8,256,128]{2,1,0:T(8,128)(2,1)}), bf16[8,256,128]{2,1,0:T(8,128)(2,1)S(1)}, u32[]{:S(2)}, u32[]{:S(2)}) async-start(bf16[8,256,128]{2,1,0:T(8,128)(2,1)} %get-tuple-element.85), calls=%async_computation.2 | async-start | bytes 1048576 | tf_op jit(solution)/shard_map/all_to_all | solution.py:709
  142.0 7.8 %copy-start.19 = (s32[3]{0:T(128)S(1)}, s32[3]{0:T(128)}, u32[]{:S(2)}) copy-start(s32[3]{0:T(128)} %constant.100.clone.1) | copy-start | bytes 40
  142.0 8.5 %copy-start.7 = (f32[4,24,128]{2,1,0:T(8,128)S(1)}, f32[4,24,128]{2,1,0:T(8,128)}, u32[]{:S(2)}) copy-start(f32[4,24,128]{2,1,0:T(8,128)} %get-tuple-element.101) | copy-start | bytes 147460
  142.0 13.7 %copy-start.15 = (f32[8,128]{1,0:T(8,128)S(1)}, f32[8,128]{1,0:T(8,128)}, u32[]{:S(2)}) copy-start(f32[8,128]{1,0:T(8,128)} %get-tuple-element.109) | copy-start | bytes 12292
  142.0 13.7 %copy-start.16 = (f32[8,128]{1,0:T(8,128)S(1)}, f32[8,128]{1,0:T(8,128)}, u32[]{:S(2)}) copy-start(f32[8,128]{1,0:T(8,128)} %get-tuple-element.110) | copy-start | bytes 12292
  142.1 13.7 %copy-start.11 = (f32[8,192]{1,0:T(8,128)S(1)}, f32[8,192]{1,0:T(8,128)}, u32[]{:S(2)}) copy-start(f32[8,192]{1,0:T(8,128)} %get-tuple-element.108) | copy-start | bytes 18436
  142.1 13.7 %copy-start.12 = (f32[8,128]{1,0:T(8,128)S(1)}, f32[8,128]{1,0:T(8,128)}, u32[]{:S(2)}) copy-start(f32[8,128]{1,0:T(8,128)} %get-tuple-element.107) | copy-start | bytes 12292
  142.1 29.3 %copy-start.2 = (bf16[8,256,128]{2,1,0:T(8,128)(2,1)}, bf16[8,256,128]{2,1,0:T(8,128)(2,1)S(1)}, u32[]{:S(2)}) copy-start(bf16[8,256,128]{2,1,0:T(8,128)(2,1)S(1)} %all-to-all-done.2.rows_1) | copy-start | bytes 1572868
  142.1 29.3 %all-to-all-start.5 = ((bf16[8,384,128]{2,1,0:T(8,128)(2,1)}), bf16[8,384,128]{2,1,0:T(8,128)(2,1)S(1)}, u32[]{:S(2)}, u32[]{:S(2)}) async-start(bf16[8,384,128]{2,1,0:T(8,128)(2,1)} %get-tuple-element.99), calls=%async_computation.5 | async-start | bytes 1572864 | tf_op jit(solution)/shard_map/all_to_all | solution.py:709
  150.5 5.4 %collective-permute-start.2 = (f32[24,128]{1,0:T(8,128)S(1)}, f32[24,128]{1,0:T(8,128)S(1)}, u32[]{:S(2)}, u32[]{:S(2)}) collective-permute-start(f32[24,128]{1,0:T(8,128)S(1)} %get-tuple-element.156), channel_id=1, source_target_pairs={{0,8},{1,9},{2,10},{3,11},{4,12},{5,13},{6,14},{7,15},{8,16},{9,17... | collective-permute-start | bytes 36872 | tf_op jit(solution)/shard_map/ppermute | solution.py:719
  154.4 6.8 %collective-permute-start.3 = (f32[24,128]{1,0:T(8,128)S(1)}, f32[24,128]{1,0:T(8,128)S(1)}, u32[]{:S(2)}, u32[]{:S(2)}) collective-permute-start(f32[24,128]{1,0:T(8,128)S(1)} %get-tuple-element.155), channel_id=1, source_target_pairs={{8,0},{9,1},{10,2},{11,3},{12,4},{13,5},{14,6},{15,7},{16,8},{17,9... | collective-permute-start | bytes 36872 | tf_op jit(solution)/shard_map/ppermute | solution.py:719
  155.9 19.1 %collective-permute-start.4 = (f32[8,448]{1,0:T(8,128)S(1)}, f32[8,448]{1,0:T(8,128)S(1)}, u32[]{:S(2)}, u32[]{:S(2)}) collective-permute-start(f32[8,448]{1,0:T(8,128)S(1)} %pad_maximum_fusion.4), channel_id=1, source_target_pairs={{0,32},{32,0},{64,96},{96,64},{128,160},{160,128},{192,224},{224,1... | collective-permute-start | bytes 43016 | tf_op jit(solution)/shard_map/ppermute | solution.py:736
  171.4 3.7 %copy-start.1 = (bf16[8,384,128]{2,1,0:T(8,128)(2,1)}, bf16[8,384,128]{2,1,0:T(8,128)(2,1)S(1)}, u32[]{:S(2)}) copy-start(bf16[8,384,128]{2,1,0:T(8,128)(2,1)S(1)} %all-to-all-done.5.rows_2) | copy-start | bytes 2359300
  171.4 46.9 %all-to-all-start.6 = ((f32[8,288,128]{2,1,0:T(8,128)}), f32[8,288,128]{2,1,0:T(8,128)S(1)}, u32[]{:S(2)}, u32[]{:S(2)}) async-start(f32[8,288,128]{2,1,0:T(8,128)} %bitcast_dynamic-update-slice_fusion), calls=%async_computation.6 | async-start | bytes 2359296 | tf_op jit(solution)/shard_map/all_to_all | solution.py:709
  175.1 3.8 %collective-permute-start.5 = (f32[8,448]{1,0:T(8,128)S(1)}, f32[8,448]{1,0:T(8,128)S(1)}, u32[]{:S(2)}, u32[]{:S(2)}) collective-permute-start(f32[8,448]{1,0:T(8,128)S(1)} %fusion.6), channel_id=1, source_target_pairs={{0,64},{32,96},{64,0},{96,32},{128,192},{160,224},{192,128},{224,1... | collective-permute-start | bytes 43016 | tf_op jit(solution)/shard_map/ppermute | solution.py:736
  178.8 5.2 %collective-permute-start.6 = (f32[8,448]{1,0:T(8,128)S(1)}, f32[8,448]{1,0:T(8,128)S(1)}, u32[]{:S(2)}, u32[]{:S(2)}) collective-permute-start(f32[8,448]{1,0:T(8,128)S(1)} %add.49), channel_id=1, source_target_pairs={{0,128},{32,160},{64,192},{96,224},{128,0},{160,32},{192,64},{224,... | collective-permute-start | bytes 43016 | tf_op jit(solution)/shard_map/ppermute | solution.py:736
  184.1 3.7 %collective-permute-start.7 = (f32[8,448]{1,0:T(8,128)S(1)}, f32[8,448]{1,0:T(8,128)S(1)}, u32[]{:S(2)}, u32[]{:S(2)}) collective-permute-start(f32[8,448]{1,0:T(8,128)S(1)} %add.50), channel_id=1, source_target_pairs={{0,8},{1,9},{2,10},{3,11},{4,12},{5,13},{6,14},{7,15},{8,0},{9,1},... | collective-permute-start | bytes 43016 | tf_op jit(solution)/shard_map/ppermute | solution.py:736
  187.8 5.2 %collective-permute-start.8 = (f32[8,448]{1,0:T(8,128)S(1)}, f32[8,448]{1,0:T(8,128)S(1)}, u32[]{:S(2)}, u32[]{:S(2)}) collective-permute-start(f32[8,448]{1,0:T(8,128)S(1)} %add.51), channel_id=1, source_target_pairs={{0,16},{1,17},{2,18},{3,19},{4,20},{5,21},{6,22},{7,23},{8,24},{9,... | collective-permute-start | bytes 43016 | tf_op jit(solution)/shard_map/ppermute | solution.py:736
  193.1 9.0 %collective-permute-start.9 = (f32[1,8,448]{2,1,0:T(8,128)S(1)}, f32[1,8,448]{2,1,0:T(8,128)S(1)}, u32[]{:S(2)}, u32[]{:S(2)}) collective-permute-start(f32[1,8,448]{2,1,0:T(8,128)S(1)} %add_bitcast_fusion), channel_id=1, source_target_pairs={{0,1},{1,0},{2,3},{3,2},{4,5},{5,4},{6,7},{7,6},{8,9},{9,8},{10,11... | collective-permute-start | bytes 43016 | tf_op jit(solution)/shard_map/ppermute | solution.py:736
  202.1 4.9 %collective-permute-start.10 = (f32[2,8,448]{2,1,0:T(8,128)S(1)}, f32[2,8,448]{2,1,0:T(8,128)S(1)}, u32[]{:S(2)}, u32[]{:S(2)}) collective-permute-start(f32[2,8,448]{2,1,0:T(8,128)S(1)} %pad_maximum_fusion.3), channel_id=1, source_target_pairs={{0,2},{1,3},{2,0},{3,1},{4,6},{5,7},{6,4},{7,5},{8,10},{9,11},{10,... | collective-permute-start | bytes 86024 | tf_op jit(solution)/shard_map/ppermute | solution.py:736
  207.0 8.3 %collective-permute-start.11 = (f32[4,8,448]{2,1,0:T(8,128)S(1)}, f32[4,8,448]{2,1,0:T(8,128)S(1)}, u32[]{:S(2)}, u32[]{:S(2)}) collective-permute-start(f32[4,8,448]{2,1,0:T(8,128)S(1)} %pad_maximum_fusion.1), channel_id=1, source_target_pairs={{0,4},{1,5},{2,6},{3,7},{4,0},{5,1},{6,2},{7,3},{8,12},{9,13},{10,... | collective-permute-start | bytes 172040 | tf_op jit(solution)/shard_map/ppermute | solution.py:736
  218.3 1.0 copy-start

commit v3 on v2

v3 whole, which is shorter than its diff:
```python
import functools

import jax
import jax.numpy as jnp
from jax import lax
from jax.experimental import pallas as pl
from jax.experimental.pallas import tpu as pltpu
from jax.sharding import PartitionSpec as P

bf16 = jnp.bfloat16
f32 = jnp.float32

GROUP = 8
ROWS = 4
LANES = 128
HEADS = 5
WIDTH = 64
CH = HEADS * WIDTH
SETS = ((0, 2), (2, 5))
SHARED = 2 * SETS[0][1] * WIDTH
TAIL = SHARED + 2 * LANES
PACK = TAIL + 64
EDGE = 2 * LANES + 8
PARAMS = EDGE + 24
WIDE = PARAMS + 32
UNROLL = 2
VMEM = 58 * 1024 * 1024

Z_GROUPS = [[y * GROUP + z for z in range(GROUP)] for y in range(ROWS)]

NN = (((1,), (0,)), ((), ()))
NT = (((1,), (1,)), ((), ()))
TN = (((0,), (0,)), ((), ()))


def dot(a, b, dims):
    return lax.dot_general(a, b, dims, preferred_element_type=f32)


def split2(a):
    hi = a.astype(bf16)
    return hi, (a - hi.astype(f32)).astype(bf16)


def split3(a):
    hi = a.astype(bf16)
    rest = a - hi.astype(f32)
    mid = rest.astype(bf16)
    return hi, mid, (rest - mid.astype(f32)).astype(bf16)


def exact_dot(a, table, dims):
    count = a.shape[0]
    hi = a.astype(bf16).astype(f32)
    rest = a - hi
    mid = rest.astype(bf16).astype(f32)
    out = dot(jnp.concatenate([hi, mid, rest - mid], axis=0).astype(bf16), table, dims)
    return out[:count] + out[count : 2 * count] + out[2 * count :]


def iota(shape, axis):
    return lax.broadcasted_iota(jnp.int32, shape, axis)


def zero_one(condition):
    return jnp.where(condition, 1.0, 0.0).astype(bf16)


def square_masks():
    row, col = iota((LANES, LANES), 0), iota((LANES, LANES), 1)
    return row, col


def set_row(channel, order):
    for which, (first, last) in enumerate(SETS):
        if channel < last * WIDTH:
            return which, channel - first * WIDTH + order * (last - first) * WIDTH


def pack_kernel(comp_ref, hid_ref, grad_ref, b_ref, c_ref, dt_ref, ids_ref, *outs):
    out_1 = outs[0]
    row, col = square_masks()
    eye = zero_one(row == col)
    for source, order in ((hid_ref, 0), (grad_ref, 1)):
        for block in range(GROUP * CH // LANES):
            piece = source[:, block * LANES : (block + 1) * LANES]
            flipped = dot(eye, piece, NT).astype(bf16)
            for half in range(2):
                channel = block * LANES + half * WIDTH
                target, at = channel // CH, channel % CH
                which, at = set_row(at, order)
                outs[which][target, at : at + WIDTH, :] = flipped[half * WIDTH : (half + 1) * WIDTH]
    pick_row, pick_col = iota((GROUP * 8, 40), 0), iota((GROUP * 8, 40), 1)
    pick = zero_one(
        ((pick_row % 8) < HEADS) & ((pick_row // 8) * HEADS + (pick_row % 8) == pick_col)
    )
    parts = [dot(pick, part, NN) for part in split3(dt_ref[...])]
    ids = ids_ref[...]
    partner = jnp.zeros_like(ids)
    for code in range(12):
        partner = jnp.where(ids == code, comp_ref[code], partner)
    both = jnp.concatenate([ids, partner, jnp.zeros((6, LANES), jnp.int32)], axis=0).astype(f32)
    b_rows, c_rows = b_ref[...], c_ref[...]
    for target in range(GROUP):
        out_1[target, SHARED : SHARED + LANES, :] = b_rows
        out_1[target, SHARED + LANES : SHARED + 2 * LANES, :] = c_rows
        tail = jnp.concatenate(
            [part[target * 8 : target * 8 + 8] for part in parts] + [both], axis=0
        )
        out_1[target, TAIL : TAIL + 32, :] = tail.astype(bf16)


def rows_beside_kernel(before_ref, after_ref, _, out, lines, sem):
    beside = jnp.where(
        iota((8, GROUP * CH), 0) >= 5, before_ref[...].astype(f32), after_ref[...].astype(f32)
    )
    for target in range(GROUP):
        mine = beside[:, target * CH : (target + 1) * CH]
        mine = jnp.concatenate([mine, jnp.zeros((8, 4 * LANES - CH), f32)], axis=1)
        lines[target] = jnp.concatenate(
            [mine[:, j * LANES : (j + 1) * LANES] for j in range(4)], axis=0
        ).astype(bf16)
    copy = pltpu.make_async_copy(lines, out.at[:, TAIL + 32 : PACK, :], sem)
    copy.start()
    copy.wait()


WHOLE = pl.BlockSpec(memory_space=pltpu.VMEM)


def pack(complement, hidden, grad, b_rows, c_rows, dt_rows, ids):
    rows = [PACK] + [2 * (last - first) * WIDTH for first, last in SETS[1:]]
    return pl.pallas_call(
        pack_kernel,
        name="pack",
        out_shape=[jax.ShapeDtypeStruct((GROUP, count, LANES), bf16) for count in rows],
        in_specs=[pl.BlockSpec(memory_space=pltpu.SMEM)] + [WHOLE] * 6,
        out_specs=[WHOLE] * len(SETS),
        compiler_params=pltpu.CompilerParams(vmem_limit_bytes=VMEM),
    )(complement, hidden, grad, b_rows, c_rows, dt_rows, ids)


def add_rows_beside(before, after, packed):
    anywhere = pl.BlockSpec(memory_space=pl.ANY)
    return pl.pallas_call(
        rows_beside_kernel,
        name="rows_beside",
        out_shape=jax.ShapeDtypeStruct(packed.shape, bf16),
        in_specs=[WHOLE, WHOLE, anywhere],
        out_specs=anywhere,
        scratch_shapes=[
            pltpu.VMEM((GROUP, PACK - TAIL - 32, LANES), bf16),
            pltpu.SemaphoreType.DMA,
        ],
        input_output_aliases={2: 0},
        compiler_params=pltpu.CompilerParams(vmem_limit_bytes=VMEM),
    )(before, after, packed)


def cost(heads):
    return pl.CostEstimate(flops=heads * 4_000_000_000, bytes_accessed=8_000_000, transcendentals=0)


def kept(shape):
    return pl.BlockSpec(shape, lambda k: (0,) * len(shape))


def chunked(shape):
    return pl.BlockSpec((UNROLL,) + shape, lambda k: (k, 0, 0))


(R_STEP_F, R_STEP_R, R_CUM_F, R_CUM_R, R_SIG_F, R_SIG_R, R_TOT_F, R_TOT_R,
 R_PRE_F, R_POST_F, R_PRE_R, R_POST_R) = range(12)


def code_tables(tail):
    code = iota((LANES, LANES), 0)
    tables = []
    for line in (24, 25):
        ids = (tail[line : line + 1] + 3.0).astype(jnp.int32)
        tables.append(zero_one((code == ids) | (code == 2)))
    return tables


def rows_at(slot):
    return slice(slot * 8, slot * 8 + 8)


def heads_at(head, offset=0):
    return slice(offset + head * WIDTH, offset + (head + 1) * WIDTH)


def beside_chunk(pk1, which, place, block):
    tail = pk1[which, TAIL:PACK, :].astype(f32)
    lines = tail[32 + 8 * block : 40 + 8 * block]
    lines = jnp.concatenate([lines, jnp.zeros((8, LANES), f32)], axis=0).astype(bf16)
    return dot(lines, place, TN).astype(bf16)


def fill_edges(ext, pk1, first):
    token, place = iota((16, LANES), 0), iota((16, LANES), 1)
    before = zero_one((token >= 5) & (token < 8) & (place == token + LANES - 8))
    after = zero_one((token < 3) & (place == token))
    count = ext.shape[1]
    for start in range(0, count, LANES):
        size = min(LANES, count - start)
        block = (first * WIDTH + start) // LANES
        ext[0, start : start + size, :] = beside_chunk(pk1, 0, before, block)[:size]
        ext[GROUP + 1, start : start + size, :] = beside_chunk(pk1, GROUP - 1, after, block)[:size]


def phase_one_kernel(first, heads, *refs):
    if first == 0:
        pk1, cw, shift_table, rate = refs[:4]
        pk, refs = pk1, refs[4:]
        rows = refs[8]
        x_f, x_r, slope_f, slope_r, u_f, u_r, v_f, v_r = refs[:8]
        refs = refs[9:]
    else:
        pk1, pk, cw, rows = refs[:4]
        x_f, x_r, slope_f, slope_r, u_f, u_r, v_f, v_r = refs[4:12]
        refs = refs[12:]
    ends_up, ends_down, ext, left_x, left_g, run = refs
    width = heads * WIDTH
    pair = pl.program_id(0)
    lane = iota((WIDTH, LANES), 1)

    @pl.when(pair == 0)
    def _():
        fill_edges(ext, pk1, first)
        for chunk in range(GROUP):
            ext[chunk + 1] = pk[chunk, :width, :]
        if first == 0:
            row, col = square_masks()
            upper = zero_one(row <= col)
            lower = zero_one(row >= col)
            ones = jnp.ones((LANES, LANES), bf16)
            logs = [[], []]
            for chunk in range(GROUP):
                tail = pk1[chunk, TAIL:PACK, :].astype(f32)
                dt = tail[0:8] + tail[8:16] + tail[16:24]
                for index, table in enumerate(code_tables(tail)):
                    arg = dt + exact_dot(shift_table[...], table, NN)
                    decay = jnp.exp(-jnp.abs(arg))
                    step = jnp.maximum(arg, 0.0) + jnp.log1p(decay)
                    logs[index].append(rate[...] * step)
                    rows[chunk, rows_at(R_STEP_F + index), :] = step
                    rows[chunk, rows_at(R_SIG_F + index), :] = (
                        jnp.where(arg >= 0, 1.0, decay) / (1.0 + decay)
                    )
            totals = exact_dot(jnp.concatenate(logs[0] + logs[1], axis=0), ones, NN)
            for index in range(2):
                sums = exact_dot(jnp.concatenate(logs[index], axis=0), (upper, lower)[index], NN)
                pre = jnp.zeros((8, LANES), f32)
                post = jnp.zeros((8, LANES), f32)
                offset = index * GROUP * 8
                for chunk in range(GROUP):
                    rows[chunk, rows_at(R_CUM_F + index), :] = sums[chunk * 8 : chunk * 8 + 8]
                    total = totals[offset + chunk * 8 : offset + chunk * 8 + 8]
                    rows[chunk, rows_at(R_TOT_F + index), :] = total
                    rows[chunk, rows_at((R_PRE_F, R_PRE_R)[index]), :] = jnp.exp(pre)
                    pre = pre + total
                for chunk in reversed(range(GROUP)):
                    rows[chunk, rows_at((R_POST_F, R_POST_R)[index]), :] = jnp.exp(post)
                    post = post + totals[offset + chunk * 8 : offset + chunk * 8 + 8]

    for sub in range(UNROLL):
        k = pair * UNROLL + sub
        cums = (rows[k, rows_at(R_CUM_F), :], rows[k, rows_at(R_CUM_R), :])
        growth = [jnp.exp(c) for c in cums]
        tails = [
            jnp.exp(rows[k, rows_at(R_TOT_F + i), :] - cums[i]) * rows[k, rows_at(R_STEP_F + i), :]
            for i in range(2)
        ]
        for head in range(heads):
            at = heads_at(head)
            one = slice(first + head, first + head + 1)
            cur = ext[k + 1, at, :].astype(f32)
            prv = ext[k, at, :].astype(f32)
            nxt = ext[k + 2, at, :].astype(f32)
            base = cw[4, at, :] + cw[0, at, :] * cur
            pre_f, pre_r = base, base
            for tap in range(1, 4):
                weight = cw[tap, at, :]
                pre_f += weight * pltpu.roll(jnp.where(lane < LANES - tap, cur, prv), tap, 1)
                pre_r += weight * pltpu.roll(jnp.where(lane >= tap, cur, nxt), LANES - tap, 1)
            grads = pk[k, width + head * WIDTH : width + (head + 1) * WIDTH, :].astype(f32)
            for index, (pre_act, x_ref, slope_ref) in enumerate(
                ((pre_f, x_f, slope_f), (pre_r, x_r, slope_r))
            ):
                gate = 1.0 / (1.0 + jnp.exp(-pre_act))
                x = pre_act * gate
                x_ref[sub, at, :] = x
                slope_ref[sub, at, :] = gate + x * (1.0 - gate)
                hi, lo = split2(x * tails[index][one])
                out_at = heads_at(head, index * width)
                left_x[sub, out_at, :LANES] = hi
                left_x[sub, out_at, LANES:] = lo
                hi, lo = split2(grads * growth[index][one])
                left_g[sub, out_at, :LANES] = hi
                left_g[sub, out_at, LANES:] = lo
        b_rows = pk1[k, SHARED : SHARED + LANES, :]
        c_rows = pk1[k, SHARED + LANES : SHARED + 2 * LANES, :]
        states = dot(left_x[sub], jnp.concatenate([b_rows, b_rows], axis=0), NN)
        u_f[k] = states[:width]
        u_r[k] = states[width:]
        pulls = dot(left_g[sub], jnp.concatenate([c_rows, c_rows], axis=0), NN)
        v_f[k] = pulls[:width]
        v_r[k] = pulls[width:]

    @pl.when(pair == GROUP // UNROLL - 1)
    def _():
        run[...] = jnp.zeros_like(run)

        def scan(step, _):
            up, down = step, GROUP - 1 - step
            moves = (
                (u_f, up, R_TOT_F), (v_r, up, R_TOT_R), (u_r, down, R_TOT_R), (v_f, down, R_TOT_F)
            )
            for slot, (ref, at_chunk, total) in enumerate(moves):
                factor = jnp.exp(rows[at_chunk, rows_at(total), :])
                for head in range(heads):
                    at = heads_at(head)
                    held = run[slot, at, :]
                    own = ref[at_chunk, at, :]
                    ref[at_chunk, at, :] = held
                    run[slot, at, :] = factor[first + head : first + head + 1] * held + own
            return 0

        lax.fori_loop(0, GROUP, scan, 0)
        whole = [
            rows[GROUP - 1, rows_at(pre), :] * jnp.exp(rows[GROUP - 1, rows_at(total), :])
            for pre, total in ((R_PRE_F, R_TOT_F), (R_PRE_R, R_TOT_R))
        ]
        for ends, pair in ((ends_up, (0, 1)), (ends_down, (2, 3))):
            ends[0:width, :] = run[pair[0]]
            ends[width : 2 * width, :] = run[pair[1]]
            ends[2 * width : 2 * width + 8, :] = whole[0]
            ends[2 * width + 8 : 2 * width + 16, :] = whole[1]


def phase_one(which, pk1, pk, cw, extra):
    first, last = SETS[which]
    heads = last - first
    width = heads * WIDTH
    block = jax.ShapeDtypeStruct((GROUP, width, LANES), f32)
    rows = jax.ShapeDtypeStruct((GROUP, 96, LANES), f32)
    ends = jax.ShapeDtypeStruct((2 * width + 16, LANES), f32)
    outs = [block] * 8 + ([rows] if which == 0 else []) + [ends, ends]
    specs = [chunked((width, LANES))] * 4 + [kept(out.shape) for out in outs[4:]]
    operands = [pk1, cw, *extra] if which == 0 else [pk1, pk, cw, *extra]
    return pl.pallas_call(
        functools.partial(phase_one_kernel, first, heads),
        name=f"phase_one_{which}",
        grid=(GROUP // UNROLL,),
        out_shape=outs,
        in_specs=[kept(operand.shape) for operand in operands],
        out_specs=specs,
        scratch_shapes=[
            pltpu.VMEM((GROUP + 2, width, LANES), bf16),
            pltpu.VMEM((UNROLL, 2 * width, 2 * LANES), bf16),
            pltpu.VMEM((UNROLL, 2 * width, 2 * LANES), bf16),
            pltpu.VMEM((4, width, LANES), f32),
        ],
        cost_estimate=cost(heads),
        compiler_params=pltpu.CompilerParams(vmem_limit_bytes=VMEM),
    )(*operands)


def phase_two_kernel(first, heads, *refs):
    (
        place_y, pk1, pk, cw, rate, skip,
        x_f, x_r, slope_f, slope_r, u_f, u_r, v_f, v_r, rows, *ends,
    ) = refs[:18]
    refs = refs[18:]
    if first:
        wide_in, edges_in, params_in = refs[:3]
        refs = refs[3:]
    (
        rows_out, wide, edges, params,
        ext, entry, d_pre_f, d_pre_r, acc, lines, *of_chunk,
    ) = refs
    width = heads * WIDTH
    pair = pl.program_id(0)
    row, col = square_masks()
    is_low = row >= col
    is_up = row <= col
    low_one, up_one = zero_one(is_low), zero_one(is_up)
    ones = jnp.ones((LANES, LANES), bf16)
    lane = iota((WIDTH, LANES), 1)

    def held(sub, start, stop):
        return wide_in[sub, start:stop, :] if first else 0.0

    @pl.when(pair == 0)
    def _():
        fill_edges(ext, pk1, first)
        entry[...] = jnp.zeros_like(entry)
        here = place_y[0]
        for away in (3, 2, 1):
            for shift, slots, reached in (
                (away, ((0, 0, 0), (1, 1, 1)), here >= away),
                (ROWS - away, ((2, 0, 1), (3, 1, 0)), here + away < ROWS),
            ):

                @pl.when(reached)
                def _(came=ends[shift - 1], slots=slots):
                    for slot, part, total in slots:
                        start = 2 * width + total * 8
                        factor = came[start : start + 8, :]
                        for head in range(heads):
                            at = heads_at(head)
                            entry[slot, at, :] = (
                                factor[first + head : first + head + 1] * entry[slot, at, :]
                                + came[heads_at(head, part * width), :]
                            )

        of_chunk[8][...] = jnp.zeros_like(of_chunk[8])
        acc[...] = jnp.zeros_like(acc)
        for ref in (d_pre_f, d_pre_r):
            for edge in (0, 1, GROUP + 2, GROUP + 3):
                ref[edge] = jnp.zeros((width, LANES), f32)

    for sub in range(UNROLL):
        k = pair * UNROLL + sub
        (
            states, d_states, state_bits, d_state_bits, reach, pulled, gd, xt, line, a_hi, a_lo,
        ) = [ref.at[sub] for ref in of_chunk]
        b_rows = pk1[k, SHARED : SHARED + LANES, :]
        c_rows = pk1[k, SHARED + LANES : SHARED + 2 * LANES, :]
        step = [rows[k, rows_at(R_STEP_F + i), :] for i in range(2)]
        cum = [rows[k, rows_at(R_CUM_F + i), :] for i in range(2)]
        growth = [jnp.exp(c) for c in cum]
        total = [rows[k, rows_at(R_TOT_F + i), :] for i in range(2)]
        tail = [jnp.exp(total[i] - cum[i]) for i in range(2)]
        factor = [jnp.exp(total[i]) for i in range(2)]
        columns = jnp.concatenate(
            [cum[0], cum[1], jnp.zeros((LANES - 16, LANES), f32)], axis=0
        ).T
        into = (
            (states, state_bits, 0, u_f, R_PRE_F, 0),
            (states, state_bits, 1, u_r, R_POST_R, 2),
            (d_states, d_state_bits, 0, v_f, R_POST_F, 3),
            (d_states, d_state_bits, 1, v_r, R_PRE_R, 1),
        )
        for full, bits, index, local, decay_row, slot in into:
            decay = rows[k, rows_at(decay_row), :]
            for head in range(heads):
                at, to = heads_at(head), heads_at(head, index * width)
                value = local[sub, at, :] + decay[first + head : first + head + 1] * entry[slot, at, :]
                full[to, :] = value
                hi, lo = split2(value)
                bits[to, :LANES] = hi
                bits[to, LANES:] = lo
        reach[...] = dot(state_bits[...], jnp.concatenate([c_rows, c_rows], axis=1), NT)
        pulled[...] = dot(d_state_bits[...], jnp.concatenate([b_rows, b_rows], axis=1), NT)
        scores = dot(c_rows, b_rows, NT)
        d_g = jnp.zeros((LANES, LANES), f32)
        for head in range(heads):
            at = heads_at(head)
            one = slice(first + head, first + head + 1)
            gap_f = columns[:, first + head : first + head + 1] - cum[0][one]
            gap_r = columns[:, 8 + first + head : 9 + first + head] - cum[1][one]
            spread = jnp.exp(jnp.where(is_low, gap_f, gap_r))
            hi, lo = split2(scores * spread)
            a_hi[head, :, :LANES] = hi * low_one
            a_hi[head, :, LANES:] = hi * up_one
            a_lo[head, :, :LANES] = lo * low_one
            a_lo[head, :, LANES:] = lo * up_one
            grad_bits = pk[k, width + head * WIDTH : width + (head + 1) * WIDTH, :]
            grads = grad_bits.astype(f32)
            xs, bits = [], []
            for index, x_ref in enumerate((x_f, x_r)):
                scaled = x_ref[sub, at, :] * step[index][one]
                xs.append(scaled)
                bits.append(split2(scaled))
            d_a = dot(
                jnp.concatenate([grad_bits, grad_bits], axis=0),
                jnp.concatenate(
                    [
                        jnp.concatenate([bits[0][0], bits[1][0]], axis=1),
                        jnp.concatenate([bits[0][1], bits[1][1]], axis=1),
                    ],
                    axis=0,
                ),
                TN,
            )
            d_g += spread * (
                jnp.where(is_low, d_a[:, :LANES], 0.0) + jnp.where(is_up, d_a[:, LANES:], 0.0)
            )
            d_xs = dot(grad_bits, a_hi[head], NN) + dot(grad_bits, a_lo[head], NN)
            out = jnp.zeros((WIDTH, LANES), f32)
            d_skip_line = jnp.zeros((WIDTH, LANES), f32)
            for index, (x_ref, slope_ref, d_pre) in enumerate(
                ((x_f, slope_f, d_pre_f), (x_r, slope_r, d_pre_r))
            ):
                to = heads_at(head, index * width)
                half = slice(index * LANES, (index + 1) * LANES)
                hi, lo = bits[index]
                y = (
                    dot(hi, a_hi[head, :, half], NT)
                    + dot(lo, a_hi[head, :, half], NT)
                    + dot(hi, a_lo[head, :, half], NT)
                    + growth[index][one] * reach[to, :]
                )
                x = x_ref[sub, at, :]
                out += y + skip[one, :] * x
                d_skip_line += grads * x
                from_state = tail[index][one] * pulled[to, :]
                d_x = d_xs[:, half] + from_state
                d_pre[k + 2, at, :] = (step[index][one] * d_x + skip[one, :] * grads) * slope_ref[
                    sub, at, :
                ]
                own = jnp.sum(x * d_x, axis=0, keepdims=True)
                line[index, one, :] = (
                    jnp.sum(grads * y, axis=0, keepdims=True) - step[index][one] * own
                )
                line[2 + index, one, :] = jnp.sum(
                    xs[index] * from_state
                    + factor[index][one] * (d_states[to, :] * states[to, :]),
                    axis=0,
                    keepdims=True,
                )
                line[4 + index, one, :] = own
                hi, lo = split2(grads * growth[index][one])
                gd[to, :LANES] = hi
                gd[to, LANES:] = lo
                hi, lo = split2(xs[index] * tail[index][one])
                xt[to, :LANES] = hi
                xt[to, LANES:] = lo
            rows_out[k, at, :] = out.astype(bf16)
            line[6, one, :] = jnp.sum(d_skip_line, axis=0, keepdims=True)
        g_hi, g_lo = split2(d_g)
        wide_c = dot(gd[:, :LANES], state_bits[...], TN)
        wide[k, LANES : 2 * LANES, :] = held(sub, LANES, 2 * LANES) + (
            dot(g_hi, b_rows, NN)
            + dot(g_lo, b_rows, NN)
            + wide_c[:, :LANES]
            + wide_c[:, LANES:]
            + dot(gd[:, LANES:], state_bits[:, :LANES], TN)
        )
        wide_b = dot(xt[:, :LANES], d_state_bits[...], TN)
        wide[k, :LANES, :] = held(sub, 0, LANES) + (
            dot(g_hi, c_rows, TN)
            + dot(g_lo, c_rows, TN)
            + wide_b[:, :LANES]
            + wide_b[:, LANES:]
            + dot(xt[:, LANES:], d_state_bits[:, :LANES], TN)
        )
        wide[k, 2 * LANES : EDGE, :] = jnp.zeros((8, LANES), f32) + held(sub, 2 * LANES, EDGE)
        lines[:, pl.ds(pl.multiple_of(k * 8, 8), 8), :] = line[...]

    @pl.when(pair == GROUP // UNROLL - 1)
    def _():
        edges[...] = edges_in[...] if first else jnp.zeros_like(edges)
        token, place = iota((8, LANES), 0), iota((8, LANES), 1)
        first_rows = zero_one((token < 3) & (place == token))
        last_rows = zero_one((token >= 5) & (place == token + LANES - 8))

        def lines_of(marker, tile):
            hi, mid, lo = split3(tile)
            return dot(marker, hi, NT) + dot(marker, mid, NT) + dot(marker, lo, NT)

        def put_edge(slot, marker):
            def put(head, total):
                channel = (first + head) * WIDTH
                block, offset = channel // LANES, channel % LANES
                edges[slot, block * 8 : block * 8 + 8, offset : offset + WIDTH] = lines_of(
                    marker, total
                )
            return put

        def taps_of(tile, hid, puts):
            for head in range(heads):
                at = heads_at(head)
                hid_here = hid[at, :].astype(f32)
                own_f, own_r = d_pre_f[tile + 1, at, :], d_pre_r[tile + 1, at, :]
                later_f, earlier_r = d_pre_f[tile + 2, at, :], d_pre_r[tile, at, :]
                both = own_f + own_r
                acc[4, at, :] += both
                acc[0, at, :] += hid_here * both
                total = cw[0, at, :] * both
                for tap in range(1, 4):
                    shifted = pltpu.roll(
                        jnp.where(lane >= tap, own_f, later_f), LANES - tap, 1
                    ) + pltpu.roll(jnp.where(lane < LANES - tap, own_r, earlier_r), tap, 1)
                    acc[tap, at, :] += hid_here * shifted
                    total += cw[tap, at, :] * shifted
                for put in puts:
                    put(head, total)

        def keep_chunk(chunk):
            def put(head, total):
                rows_out[chunk, heads_at(head, width), :] = total.astype(bf16)
            return put

        taps_of(0, ext[0], [put_edge(2, last_rows)])
        taps_of(GROUP + 1, ext[GROUP + 1], [put_edge(3, first_rows)])
        taps_of(1, pk[0], [keep_chunk(0), put_edge(0, first_rows)])
        taps_of(GROUP, pk[GROUP - 1], [keep_chunk(GROUP - 1), put_edge(1, last_rows)])

        def inner(chunk, _):
            taps_of(chunk + 1, pk.at[chunk], [keep_chunk(chunk)])
            return 0

        lax.fori_loop(1, GROUP - 1, inner, 0)
        sums = jnp.zeros((8, width), f32)
        for tap in range(5):
            sums += lines_of(zero_one(token == tap), acc[tap])
        params[...] = params_in[...] if first else jnp.zeros_like(params)
        for start in range(0, width, LANES):
            size = min(LANES, width - start)
            block = (first * WIDTH + start) // LANES
            params[block * 8 : block * 8 + 8, :size] = sums[:, start : start + size]
        def all_rows(slot):
            return jnp.concatenate([rows[c, rows_at(slot), :] for c in range(GROUP)], axis=0)

        def over_chunks(value):
            total = value[0:8]
            for c in range(1, GROUP):
                total = total + value[c * 8 : c * 8 + 8]
            return total

        rates = jnp.concatenate([rate[...]] * GROUP, axis=0)
        tails_here = exact_dot(jnp.concatenate([lines[2], lines[3]], axis=0), ones, NN)
        d_args, d_rate = [], jnp.zeros((GROUP * 8, LANES), f32)
        for index in range(2):
            offset = index * GROUP * 8
            d_log = exact_dot(lines[index], (low_one, up_one)[index], NN) + tails_here[
                offset : offset + GROUP * 8
            ]
            d_args.append((lines[4 + index] + rates * d_log) * all_rows(R_SIG_F + index))
            d_rate += d_log * rates * all_rows(R_STEP_F + index)
        by_code = jnp.zeros((8, LANES), f32)
        for c in range(GROUP):
            own = slice(c * 8, c * 8 + 8)
            wide[c, 2 * LANES : EDGE, :] += d_args[0][own] + d_args[1][own]
            for index, table in enumerate(code_tables(pk1[c, TAIL:PACK, :].astype(f32))):
                by_code += exact_dot(d_args[index][own], table, NT)
        params[24:32, :] += (
            exact_dot(over_chunks(d_rate), zero_one(col == 0), NN)
            + exact_dot(over_chunks(lines[6]), zero_one(col == 1), NN)
            + by_code
        )


def phase_two(which, place_y, pk1, pk, cw, rate, skip, saved, rows, ends, carried):
    first, last = SETS[which]
    heads = last - first
    width = heads * WIDTH
    outs = [
        jax.ShapeDtypeStruct((GROUP, 2 * width, LANES), bf16),
        jax.ShapeDtypeStruct((GROUP, WIDE, LANES), f32),
        jax.ShapeDtypeStruct((4, 24, LANES), f32),
        jax.ShapeDtypeStruct((32, LANES), f32),
    ]
    whole = [pk1, pk, cw, rate, skip]
    in_specs = (
        [pl.BlockSpec(memory_space=pltpu.SMEM)]
        + [kept(operand.shape) for operand in whole]
        + [chunked((width, LANES))] * 8
        + [kept(rows.shape)] + [kept(end.shape) for end in ends]
    )
    if which:
        in_specs += [chunked((WIDE, LANES)), kept((4, 24, LANES)), kept((32, LANES))]
    return pl.pallas_call(
        functools.partial(phase_two_kernel, first, heads),
        name=f"phase_two_{which}",
        grid=(GROUP // UNROLL,),
        out_shape=outs,
        in_specs=in_specs,
        out_specs=[kept(out.shape) for out in outs],
        scratch_shapes=[
            pltpu.VMEM((GROUP + 2, width, LANES), bf16),
            pltpu.VMEM((4, width, LANES), f32),
            pltpu.VMEM((GROUP + 4, width, LANES), f32),
            pltpu.VMEM((GROUP + 4, width, LANES), f32),
            pltpu.VMEM((5, width, LANES), f32),
            pltpu.VMEM((7, GROUP * 8, LANES), f32),
            pltpu.VMEM((UNROLL, 2 * width, LANES), f32),
            pltpu.VMEM((UNROLL, 2 * width, LANES), f32),
            pltpu.VMEM((UNROLL, 2 * width, 2 * LANES), bf16),
            pltpu.VMEM((UNROLL, 2 * width, 2 * LANES), bf16),
            pltpu.VMEM((UNROLL, 2 * width, LANES), f32),
            pltpu.VMEM((UNROLL, 2 * width, LANES), f32),
            pltpu.VMEM((UNROLL, 2 * width, 2 * LANES), bf16),
            pltpu.VMEM((UNROLL, 2 * width, 2 * LANES), bf16),
            pltpu.VMEM((UNROLL, 7, 8, LANES), f32),
            pltpu.VMEM((UNROLL, heads, LANES, 2 * LANES), bf16),
            pltpu.VMEM((UNROLL, heads, LANES, 2 * LANES), bf16),
        ],
        cost_estimate=cost(2 * heads),
        compiler_params=pltpu.CompilerParams(vmem_limit_bytes=VMEM),
    )(place_y, *whole, *saved, rows, *ends, *carried)


def finish_kernel(edges, from_prev, from_next, sums, _, out, lines, sem):
    for target in range(GROUP):
        lines[target, :24, :] = jnp.zeros((24, LANES), f32)
        lines[target, 24:, :] = sums[...]
    lines[0, :24, :] = edges[0] + from_prev[...]
    lines[GROUP - 1, :24, :] = edges[1] + from_next[...]
    copy = pltpu.make_async_copy(lines, out.at[:, EDGE:WIDE, :], sem)
    copy.start()
    copy.wait()


def finish(edges, from_prev, from_next, sums, wide):
    anywhere = pl.BlockSpec(memory_space=pl.ANY)
    return pl.pallas_call(
        finish_kernel,
        name="finish",
        out_shape=jax.ShapeDtypeStruct(wide.shape, f32),
        in_specs=[WHOLE] * 4 + [anywhere],
        out_specs=anywhere,
        scratch_shapes=[pltpu.VMEM((GROUP, WIDE - EDGE, LANES), f32), pltpu.SemaphoreType.DMA],
        input_output_aliases={4: 0},
        compiler_params=pltpu.CompilerParams(vmem_limit_bytes=VMEM),
    )(edges, from_prev, from_next, sums, wide)


def unpack_kernel(place_z, *refs):
    sets, wide = refs[: len(SETS)], refs[len(SETS)]
    (
        layer_out, hid_out, b_out, c_out, dt_out, taps_out, bias_out, rate_out, skip_out, shift_out, code_out,
    ) = refs[len(SETS) + 1 :]
    row, col = square_masks()
    eye = zero_one(row == col)
    line = iota((16, LANES), 0)
    at_start = (line < 3) & (place_z[0] == 0)
    at_end = (line >= 13) & (place_z[0] == GROUP - 1)
    blank = jnp.zeros((8, LANES), f32)
    for order, target in enumerate((layer_out, hid_out)):
        for block in range(GROUP * CH // LANES):
            pieces, edge, taps = [], [], []
            for half in range(2):
                channel = block * LANES + half * WIDTH
                group, at = channel // CH, channel % CH
                offset = at % LANES
                start = EDGE + at // LANES * 8
                taps.append(wide[group, start + 24 : start + 32, offset : offset + WIDTH])
                edge.append(wide[group, start : start + 8, offset : offset + WIDTH])
                which, at = set_row(at, order)
                pieces.append(sets[which][group, at : at + WIDTH, :])
            lanes = slice(block * LANES, (block + 1) * LANES)
            flipped = dot(eye, jnp.concatenate(pieces, axis=0), NT)
            if order:
                taps = jnp.concatenate(taps, axis=1)
                taps_out[:, lanes] = taps[:4]
                bias_out[:, lanes] = taps[4:5]
                edge = jnp.concatenate(edge, axis=1)
                head = jnp.where(at_start, jnp.concatenate([edge, blank], axis=0), flipped[:16])
                tail = jnp.where(
                    at_end, jnp.concatenate([blank, edge], axis=0), flipped[LANES - 16 :]
                )
                flipped = jnp.concatenate([head, flipped[16 : LANES - 16], tail], axis=0)
            target[:, lanes] = flipped.astype(bf16)
    for base, target in ((0, b_out), (LANES, c_out)):
        total = wide[0, base : base + LANES, :]
        for group in range(1, GROUP):
            total += wide[group, base : base + LANES, :]
        target[...] = total
    lines = jnp.concatenate(
        [wide[group, 2 * LANES : EDGE, :] for group in range(GROUP)], axis=0
    )
    pick_row, pick_col = iota((40, GROUP * 8), 0), iota((40, GROUP * 8), 1)
    pick = zero_one(
        ((pick_col % 8) < HEADS) & ((pick_col // 8) * HEADS + (pick_col % 8) == pick_row)
    )
    hi, mid, lo = split3(lines)
    dt_out[...] = dot(pick, hi, NN) + dot(pick, mid, NN) + dot(pick, lo, NN)
    heads = jnp.concatenate([wide[group, WIDE - 8 : WIDE, :] for group in range(GROUP)], axis=0)
    by_head = sum(
        lax.dot_general(part, pick, (((0,), (1,)), ((), ())), preferred_element_type=f32)
        for part in split3(heads)
    )
    rate_out[...] = by_head[0:1]
    skip_out[...] = by_head[1:2]
    shift_out[...] = by_head[2:3]
    code_out[...] = by_head[3:15]


def unpack(place_z, sets, wide):
    rows = jax.ShapeDtypeStruct((LANES, GROUP * CH), bf16)
    square = jax.ShapeDtypeStruct((LANES, LANES), f32)
    return pl.pallas_call(
        unpack_kernel,
        name="unpack",
        out_shape=[rows, rows, square, square, jax.ShapeDtypeStruct((40, LANES), f32)]
        + [
            jax.ShapeDtypeStruct(shape, f32)
            for shape in ((4, GROUP * CH), (1, GROUP * CH), (1, 40), (1, 40), (1, 40), (12, 40))
        ],
        in_specs=[pl.BlockSpec(memory_space=pltpu.SMEM)] + [WHOLE] * (len(SETS) + 1),
        out_specs=[WHOLE] * 11,
        compiler_params=pltpu.CompilerParams(vmem_limit_bytes=VMEM),
    )(place_z, *sets, wide)


def exchange(array):
    return lax.all_to_all(array, "seq", 0, 0, axis_index_groups=Z_GROUPS)


def along_y(array, by):
    pairs = [
        (y * GROUP + z, (y + by) * GROUP + z)
        for y in range(ROWS)
        for z in range(GROUP)
        if 0 <= y + by < ROWS
    ]
    return lax.ppermute(array, "seq", pairs)


def beside(array, by):
    count = lax.axis_size("seq")
    return lax.ppermute(array, "seq", [(i, i + by) for i in range(count) if 0 <= i + by < count])


def cross_y(up, down, run):
    came = []
    for shift in range(1, ROWS):
        pairs = [
            (y * GROUP + z, (y + shift) % ROWS * GROUP + z) for y in range(ROWS) for z in range(GROUP)
        ]
        came.append(lax.ppermute(jnp.where(run + shift < ROWS, up, down), "seq", pairs))
    return came


def flip_bit(array, axis, bit):
    count = lax.axis_size(axis)
    return lax.ppermute(array, axis, [(i, i ^ bit) for i in range(count)])


def total_over_runs(array):
    for axis, bit in (("dp", 1), ("dp", 2), ("dp", 4), ("seq", 8), ("seq", 16)):
        array = array + flip_bit(array, axis, bit)
    return array


def per_device(
    hidden, b_proj, c_proj, dt_raw, base_ids, complement,
    a_log, d_skip, dt_bias, base_shift, conv_w, conv_b, grad_out,
):
    place = lax.axis_index("seq")
    group, run = place % GROUP, place // GROUP
    here_z, here_y = group[None].astype(jnp.int32), run[None].astype(jnp.int32)
    before = beside(hidden[0, -8:], 1)
    after = beside(hidden[0, :8], -1)
    taps = jnp.concatenate([conv_w, conv_b[None]], axis=0).reshape(5, GROUP, CH)
    taps = lax.dynamic_index_in_dim(taps, group, 1, keepdims=False)
    cw = jnp.broadcast_to(taps[:, :, None], (5, CH, LANES))
    per_head = jnp.stack([-jnp.exp(a_log), d_skip], axis=0)
    tables = jnp.concatenate([dt_bias[None], base_shift], axis=0)
    tables = jnp.concatenate([per_head, tables], axis=0).reshape(15, GROUP, HEADS)
    tables = lax.dynamic_index_in_dim(tables, group, 1, keepdims=False)
    tables = jnp.pad(tables, ((0, 0), (0, 8 - HEADS)))
    rate = jnp.broadcast_to(tables[0][:, None], (8, LANES))
    skip = jnp.broadcast_to(tables[1][:, None], (8, LANES))
    shift_table = jnp.pad(tables[2:].T, ((0, 0), (2, LANES - 15)))

    taps = [cw[:, first * WIDTH : last * WIDTH] for first, last in SETS]

    packed = pack(
        complement, hidden[0], grad_out[0], b_proj[0], c_proj[0], dt_raw[0].T, base_ids
    )
    packed = [add_rows_beside(before, after, packed[0]), *packed[1:]]
    pk = [exchange(part) for part in packed]
    saved, ends, sets, carried = [], [], [], ()
    for which, tap in enumerate(taps):
        *blocks, up, down = phase_one(
            which, pk[0], pk[which], tap, (rows,) if which else (shift_table, rate)
        )
        if not which:
            rows = blocks.pop()
        saved.append(blocks)
        ends.append(cross_y(up, down, run))
    for which, tap in enumerate(taps):
        out, *carried = phase_two(
            which, here_y, pk[0], pk[which], tap, rate, skip, saved[which], rows, ends[which], carried
        )
        sets.append(exchange(out))
    wide, edges, sums = carried
    from_next = along_y(edges[2], -1)
    from_prev = along_y(edges[3], 1)
    wide = exchange(finish(edges, from_prev, from_next, total_over_runs(sums), wide))
    layer_out, d_hidden, d_b, d_c, d_dt, taps, bias, rates, skips, shifts, codes = unpack(
        here_z, sets, wide
    )
    return (
        layer_out[None], d_hidden[None], d_b[None], d_c[None], d_dt.T[None],
        rates[0], skips[0], shifts[0], codes, taps, bias[0],
    )


def solution(mesh):
    rows = P("dp", "seq", None)
    placed = (rows, rows, rows, rows, P("dp", "seq"), P(), P(), P(), P(), P(), P(), P(), rows)
    return jax.shard_map(
        per_device,
        mesh=mesh,
        in_specs=placed,
        out_specs=(rows,) * 5 + (P(),) * 6,
        check_vma=False,
    )
```

time: 226 us -> 207 us (0.916)
  blocking collectives: 0 us -> 37.9 us
  waiting for transfers between devices: 75.6 us -> 51 us
  starting transfers between devices: 60.6 us -> 48.9 us
  local copies, waits for them, and re-layouts: 16.3 us -> 7.67 us
  Pallas kernels: 62.5 us -> 55.2 us
  other arithmetic: 8.32 us -> 4.14 us
    all_to_all x0 -> x1, blocking collectives: none -> 37.9 us  [exchange(): return lax.all_to_all(array, 'seq', 0, 0, axis_index_groups=Z_GROUPS)]
    ppermute x8 -> x5, waiting for transfers between devices: 25.3 us -> 11.4 us  [flip_bit(): return lax.ppermute(array, axis, [(i, i ^ bit) for i in range(count)])]
    ppermute x8 -> x5, starting transfers between devices: 14.8 us -> 4.29 us  [flip_bit(): return lax.ppermute(array, axis, [(i, i ^ bit) for i in range(count)])]
    ppermute x0 -> x6, starting transfers between devices: none -> 9.36 us  [cross_y(): lax.ppermute(jnp.where(run + shift < ROWS, up, down), 'seq', pairs)]
    all_to_all x2 -> x0, starting transfers between devices: 9.26 us -> none  [cross_y(): lax.all_to_all(jnp.where(later, up[None], down[None]), 'seq', 0, 0, axis_...]
    all_to_all x5 -> x4, waiting for transfers between devices: 47.1 us -> 38.8 us  [exchange(): return lax.all_to_all(array, 'seq', 0, 0, axis_index_groups=Z_GROUPS)]
    pallas_call x2, Pallas kernels: 20.2 us -> 14.6 us  [phase_one(): pl.pallas_call(functools.partial(phase_one_kernel, first, heads), name=f'...]
    pallas_call x2, Pallas kernels: 35 us -> 30.2 us  [phase_two(): pl.pallas_call(functools.partial(phase_two_kernel, first, heads), name=f'...]
  transfers between devices with their start and end apart: 19 -> 19, of which waited for: 11 -> 7; matrix products, arithmetic and copies ran while one was open for 9% -> 4% of each run, Pallas kernels for 25% -> 24%
where the time goes in v3:
time: 207 us; the launch traced here: 206 us
  Pallas kernels  55.2 us (27%)
  waiting for transfers between devices  51 us (25%)
  starting transfers between devices  48.9 us (24%)
  blocking collectives  37.9 us (18%)
  local copies, waits for them, and re-layouts  7.67 us (4%)
  other arithmetic  4.14 us (2%)
    all_to_all x4, waiting for transfers between devices, exchange(): return lax.all_to_all(array, 'seq', 0, 0, axis_index_groups=Z_GROUPS)  38.8 us
    all_to_all x1, blocking collectives, exchange(): return lax.all_to_all(array, 'seq', 0, 0, axis_index_groups=Z_GROUPS)  37.9 us
    pallas_call x2, Pallas kernels, phase_two(): pl.pallas_call(functools.partial(phase_two_kernel, first, heads), name=f'...  30.2 us
    all_to_all x4, starting transfers between devices, exchange(): return lax.all_to_all(array, 'seq', 0, 0, axis_index_groups=Z_GROUPS)  23.6 us
    pallas_call x2, Pallas kernels, phase_one(): pl.pallas_call(functools.partial(phase_one_kernel, first, heads), name=f'...  14.6 us
    ppermute x5, waiting for transfers between devices, flip_bit(): return lax.ppermute(array, axis, [(i, i ^ bit) for i in range(count)])  11.4 us
    ppermute x6, starting transfers between devices, cross_y(): lax.ppermute(jnp.where(run + shift < ROWS, up, down), 'seq', pairs)  9.36 us
    ppermute x2, starting transfers between devices, beside(): lax.ppermute(array, 'seq', [(i, i + by) for i in range(count) if 0 <= i +...  5.83 us
  transfers between devices with their start and end apart: 19, of which 7 were waited for; matrix products, arithmetic and copies ran while one was open for 4% of the time, Pallas kernels for 24%

profile of v3, /device:TPU:6, one launch (start us, length us, event | category | flops | bytes accessed | tf_op | source)
XLA Modules:
  0.0 205.9 jit_solution(17533057167739460349)
XLA Ops:
  0.6 0.8 slice_bitcast_fusion
  1.5 1.3 collective-permute-start.1
  2.7 4.5 %collective-permute-start = (bf16[8,2560]{1,0:T(8,128)(2,1)S(1)}, bf16[8,2560]{1,0:T(8,128)(2,1)S(1)}, u32[]{:S(2)}, u32[]{:S(2)}) collective-permute-start(bf16[8,2560]{1,0:T(8,128)(2,1)S(1)} %get-tuple-element.98), channel_id=1, source_target_pairs={{0,1},{1,2},{2,3},{3,4},{4,5},{5,6},{6,7},{7,8},{8,9},{9,10},{10,1... | collective-permute-start | bytes 122888 | tf_op jit(solution)/shard_map/ppermute | solution.py:816
  7.3 3.6 %pack.1 = (bf16[8,576,128]{2,1,0:T(8,128)(2,1)}, bf16[8,384,128]{2,1,0:T(8,128)(2,1)}) custom-call(s32[12]{0:T(128)} %comp_ref.1, bf16[128,2560]{1,0:T(8,128)(2,1)} %bitcast.36, bf16[128,2560]{1,0:T(8,128)(2,1)} %bitcast.37, bf16[128,128]{1,0:T(8,128)(2,1)} %bitcast.40, bf16[128,128]{1,0:T(8,128)(2,1)} %bitcast.41, f32[40,128]{1,0:T(8,128)} %bitcast.42, ...), custom_call_target="tpu_custom_call" | custom-call | tf_op jit(solution)/shard_map/pack/pallas_call | solution.py:133
  11.0 0.6 copy-done.6
  11.5 0.0 copy-done.7
  11.6 1.5 rows_beside.1
  13.1 0.0 copy-start.12
  13.1 9.4 %all-to-all-start = ((bf16[8,576,128]{2,1,0:T(8,128)(2,1)}), bf16[8,576,128]{2,1,0:T(8,128)(2,1)S(1)}, u32[]{:S(2)}, u32[]{:S(2)}) async-start(bf16[8,576,128]{2,1,0:T(8,128)(2,1)} %rows_beside.1), calls=%async_computation | async-start | bytes 2359296 | tf_op jit(solution)/shard_map/all_to_all | solution.py:801
  22.5 0.0 copy-start.13
  22.5 0.0 copy-start.14
  22.6 0.1 concatenate.21
  22.7 0.1 concatenate.20
  22.8 0.1 copy.30
  22.9 30.6 %all-to-all-done.refs_0_.refs_1_.refs_2_ = bf16[8,576,128]{2,1,0:T(8,128)(2,1)S(1)} async-done(((bf16[8,576,128]{2,1,0:T(8,128)(2,1)}), bf16[8,576,128]{2,1,0:T(8,128)(2,1)S(1)}, u32[]{:S(2)}, u32[]{:S(2)}) %all-to-all-start) | async-done | bytes 1179680 | tf_op jit(solution)/shard_map/all_to_all | solution.py:801
  53.5 3.5 %all-to-all-start.2 = ((bf16[8,384,128]{2,1,0:T(8,128)(2,1)}), bf16[8,384,128]{2,1,0:T(8,128)(2,1)S(1)}, u32[]{:S(2)}, u32[]{:S(2)}) async-start(bf16[8,384,128]{2,1,0:T(8,128)(2,1)} %get-tuple-element.66), calls=%async_computation.2 | async-start | bytes 1572864 | tf_op jit(solution)/shard_map/all_to_all | solution.py:801
  57.1 0.1 concatenate.28
  57.2 0.1 concatenate.29
  57.3 0.1 concatenate.30
  57.4 0.1 fusion.4
  57.5 0.1 slice_bitcast_fusion.4
  57.6 0.7 pad.9.refs_2_
  58.3 0.2 slice_reduce_fusion
  58.5 0.7 broadcast_in_dim.52.refs_3_.refs_4_
  59.1 0.9 broadcast_in_dim.50.refs_1_.refs_3_
  60.0 6.7 %phase_one_0.1 = (f32[8,128,128]{2,1,0:T(8,128)}, f32[8,128,128]{2,1,0:T(8,128)}, f32[8,128,128]{2,1,0:T(8,128)}, f32[8,128,128]{2,1,0:T(8,128)}, f32[8,128,128]...) custom-call(bf16[8,576,128]{2,1,0:T(8,128)(2,1)} %copy-done.2, ...), custom_call_target="tpu_custom_call" | custom-call | flops 8000000000 | bytes 8000000 | tf_op jit(solution)/shard_map/phase_one_0/pallas_call | solution.py:352
  66.7 1.0 broadcast_select_fusion.3
  67.7 3.2 %collective-permute-start.4 = (f32[272,128]{1,0:T(8,128)S(1)}, f32[272,128]{1,0:T(8,128)S(1)}, u32[]{:S(2)}, u32[]{:S(2)}) collective-permute-start(f32[272,128]{1,0:T(8,128)S(1)} %get-tuple-element.102), channel_id=1, source_target_pairs={{0,24},{1,25},{2,26},{3,27},{4,28},{5,29},{6,30},{7,31},{8,0},{9,1... | collective-permute-start | bytes 417800 | tf_op jit(solution)/shard_map/ppermute | solution.py:825
  70.9 0.5 collective-permute-start.3
  71.4 1.0 collective-permute-start.2
  72.4 8.2 %all-to-all-done.2.refs_1_.refs_2_ = bf16[8,384,128]{2,1,0:T(8,128)(2,1)S(1)} async-done(((bf16[8,384,128]{2,1,0:T(8,128)(2,1)}), bf16[8,384,128]{2,1,0:T(8,128)(2,1)S(1)}, u32[]{:S(2)}, u32[]{:S(2)}) %all-to-all-start.2) | async-done | bytes 786464 | tf_op jit(solution)/shard_map/all_to_all | solution.py:801
  80.6 1.0 broadcast_in_dim.55.refs_2_.refs_3_
  81.7 7.9 %phase_one_1.1 = (f32[8,192,128]{2,1,0:T(8,128)}, f32[8,192,128]{2,1,0:T(8,128)}, f32[8,192,128]{2,1,0:T(8,128)}, f32[8,192,128]{2,1,0:T(8,128)}, f32[8,192,128]...) custom-call(bf16[8,576,128]{2,1,0:T(8,128)(2,1)} %copy-done.2, ...), custom_call_target="tpu_custom_call" | custom-call | flops 12000000000 | bytes 8000000 | tf_op jit(solution)/shard_map/phase_one_1/pallas_call | solution.py:352
  89.6 1.1 broadcast_select_fusion
  90.6 1.4 collective-permute-start.7
  92.1 2.3 %collective-permute-start.6 = (f32[400,128]{1,0:T(8,128)S(1)}, f32[400,128]{1,0:T(8,128)S(1)}, u32[]{:S(2)}, u32[]{:S(2)}) collective-permute-start(f32[400,128]{1,0:T(8,128)S(1)} %get-tuple-element.100), channel_id=1, source_target_pairs={{0,16},{1,17},{2,18},{3,19},{4,20},{5,21},{6,22},{7,23},{8,24},{9,... | collective-permute-start | bytes 614408 | tf_op jit(solution)/shard_map/ppermute | solution.py:825
  94.4 1.0 collective-permute-start.5
  95.4 0.7 broadcast_in_dim.54.refs_5_
  96.0 0.0 copy-done.20
  96.1 13.3 %phase_two_0.1 = (bf16[8,256,128]{2,1,0:T(8,128)(2,1)}, f32[8,320,128]{2,1,0:T(8,128)}, f32[4,24,128]{2,1,0:T(8,128)}, f32[32,128]{1,0:T(8,128)}) custom-call(s32[1]{0:T(128)} %bitcast.1.refs_0_, bf16[8,576,128]{2,1,0:T(8,128)(2,1)} %copy-done.2, bf16[8,576,128]{2,1,0:T(8,128)(2,1)} %copy-done.2, f32[5,128,128]{2,1,0:T(8,128)} %broadcast_in_dim.50.refs_1_.refs_3_, ...), custom_call_target="tpu_custom_call" | custom-call | flops 16000000000 | bytes 8000000 | tf_op jit(solution)/shard_map/phase_two_0/pallas_call | solution.py:666
  109.3 3.7 %all-to-all-start.1 = ((bf16[8,256,128]{2,1,0:T(8,128)(2,1)}), bf16[8,256,128]{2,1,0:T(8,128)(2,1)S(1)}, u32[]{:S(2)}, u32[]{:S(2)}) async-start(bf16[8,256,128]{2,1,0:T(8,128)(2,1)} %get-tuple-element.65), calls=%async_computation.1 | async-start | bytes 1048576 | tf_op jit(solution)/shard_map/all_to_all | solution.py:801
  113.1 0.6 copy-done.15
  113.7 0.1 copy-done.16
  113.8 0.1 copy-done.17
  113.9 16.9 %phase_two_1.1 = (bf16[8,384,128]{2,1,0:T(8,128)(2,1)}, f32[8,320,128]{2,1,0:T(8,128)}, f32[4,24,128]{2,1,0:T(8,128)}, f32[32,128]{1,0:T(8,128)}) custom-call(s32[1]{0:T(128)} %bitcast.1.refs_0_, bf16[8,576,128]{2,1,0:T(8,128)(2,1)} %copy-done.2, bf16[8,384,128]{2,1,0:T(8,128)(2,1)} %copy-done.3, f32[5,192,128]{2,1,0:T(8,128)} %broadcast_in_dim.55.refs_2_.refs_3_, ...), custom_call_target="tpu_custom_call" | custom-call | flops 24000000000 | bytes 8000000 | tf_op jit(solution)/shard_map/phase_two_1/pallas_call | solution.py:666
  130.8 6.9 %all-to-all-start.3 = ((bf16[8,384,128]{2,1,0:T(8,128)(2,1)}), bf16[8,384,128]{2,1,0:T(8,128)(2,1)S(1)}, u32[]{:S(2)}, u32[]{:S(2)}) async-start(bf16[8,384,128]{2,1,0:T(8,128)(2,1)} %get-tuple-element.80), calls=%async_computation.3 | async-start | bytes 1572864 | tf_op jit(solution)/shard_map/all_to_all | solution.py:801
  137.8 0.1 collective-permute-start.10
  137.9 1.2 collective-permute-done.10
  139.1 0.8 collective-permute-start.11
  139.9 2.9 %collective-permute-done.11 = f32[32,128]{1,0:T(8,128)S(1)} collective-permute-done((f32[32,128]{1,0:T(8,128)S(1)}, f32[32,128]{1,0:T(8,128)S(1)}, u32[]{:S(2)}, u32[]{:S(2)}) %collective-permute-start.11) | collective-permute-done | bytes 16416 | tf_op jit(solution)/shard_map/ppermute | solution.py:831
  142.8 1.4 collective-permute-start.12
  144.2 3.8 %collective-permute-done.12 = f32[32,128]{1,0:T(8,128)S(1)} collective-permute-done((f32[32,128]{1,0:T(8,128)S(1)}, f32[32,128]{1,0:T(8,128)S(1)}, u32[]{:S(2)}, u32[]{:S(2)}) %collective-permute-start.12) | collective-permute-done | bytes 16416 | tf_op jit(solution)/shard_map/ppermute | solution.py:831
  148.1 0.2 collective-permute-start.13
  148.3 3.5 %collective-permute-done.13 = f32[32,128]{1,0:T(8,128)S(1)} collective-permute-done((f32[32,128]{1,0:T(8,128)S(1)}, f32[32,128]{1,0:T(8,128)S(1)}, u32[]{:S(2)}, u32[]{:S(2)}) %collective-permute-start.13) | collective-permute-done | bytes 16416 | tf_op jit(solution)/shard_map/ppermute | solution.py:831
  151.8 1.7 collective-permute-start.14
  153.5 1.3 collective-permute-start.9
  154.8 4.5 %collective-permute-start.8 = (f32[24,128]{1,0:T(8,128)S(1)}, f32[24,128]{1,0:T(8,128)S(1)}, u32[]{:S(2)}, u32[]{:S(2)}) collective-permute-start(f32[24,128]{1,0:T(8,128)S(1)} %get-tuple-element.106), channel_id=1, source_target_pairs={{0,8},{1,9},{2,10},{3,11},{4,12},{5,13},{6,14},{7,15},{8,16},{9,17... | collective-permute-start | bytes 36872 | tf_op jit(solution)/shard_map/ppermute | solution.py:811
  159.4 0.6 add.51.sums
  160.0 0.8 collective-permute-done.8.from_prev
  160.8 0.6 copy-done.10
  161.4 1.6 finish.1
  162.9 37.9 %all_to_all.25.refs_2_ = f32[8,320,128]{2,1,0:T(8,128)} all-to-all(f32[8,320,128]{2,1,0:T(8,128)} %finish.1), channel_id=1, replica_groups={{0,1,2,3,4,5,6,7},{8,9,10,11,12,13,14,15},{16,17,18,19,20,21,22,23},{24..., dimensions={0} | all-to-all | bytes 2621440 | tf_op jit(solution)/shard_map/all_to_all | solution.py:801
  200.9 3.7 %unpack.1 = (bf16[128,2560]{1,0:T(8,128)(2,1)}, bf16[128,2560]{1,0:T(8,128)(2,1)}, f32[128,128]{1,0:T(8,128)}, f32[128,128]{1,0:T(8,128)}, f32[40,128]{1,0:T(8,1...) custom-call(s32[1]{0:T(128)} %bitcast.place_z, ...), custom_call_target="tpu_custom_call" | custom-call | tf_op jit(solution)/shard_map/unpack/pallas_call | solution.py:786
  204.5 1.3 reduce.2
  (57 shorter events, 0.2 us)
Async XLA Ops:
  1.5 9.5 %collective-permute-start.1 = (bf16[8,2560]{1,0:T(8,128)(2,1)S(1)}, bf16[8,2560]{1,0:T(8,128)(2,1)S(1)}, u32[]{:S(2)}, u32[]{:S(2)}) collective-permute-start(bf16[8,2560]{1,0:T(8,128)(2,1)S(1)} %get-tuple-element.97), channel_id=1, source_target_pairs={{1,0},{2,1},{3,2},{4,3},{5,4},{6,5},{7,6},{8,7},{9,8},{10,9},{11,1... | collective-permute-start | bytes 122888 | tf_op jit(solution)/shard_map/ppermute | solution.py:816
  2.7 8.2 %collective-permute-start = (bf16[8,2560]{1,0:T(8,128)(2,1)S(1)}, bf16[8,2560]{1,0:T(8,128)(2,1)S(1)}, u32[]{:S(2)}, u32[]{:S(2)}) collective-permute-start(bf16[8,2560]{1,0:T(8,128)(2,1)S(1)} %get-tuple-element.98), channel_id=1, source_target_pairs={{0,1},{1,2},{2,3},{3,4},{4,5},{5,6},{6,7},{7,8},{8,9},{9,10},{10,1... | collective-permute-start | bytes 122888 | tf_op jit(solution)/shard_map/ppermute | solution.py:816
  10.9 0.6 copy-start.6
  10.9 0.6 copy-start.7
  13.1 9.5 %copy-start.11 = (f32[2560]{0:T(1024)S(1)}, f32[2560]{0:T(1024)}, u32[]{:S(2)}) copy-start(f32[2560]{0:T(1024)} %param.24) | copy-start | bytes 30724
  13.1 9.6 %copy-start.5 = (f32[4,2560]{1,0:T(4,128)S(1)}, f32[4,2560]{1,0:T(4,128)}, u32[]{:S(2)}) copy-start(f32[4,2560]{1,0:T(4,128)} %param.23) | copy-start | bytes 122884
  13.1 9.7 %copy-start.12 = (f32[12,40]{1,0:T(8,128)S(1)}, f32[12,40]{1,0:T(8,128)}, u32[]{:S(2)}) copy-start(f32[12,40]{1,0:T(8,128)} %param.22) | copy-start | bytes 5764
  13.1 40.4 %all-to-all-start = ((bf16[8,576,128]{2,1,0:T(8,128)(2,1)}), bf16[8,576,128]{2,1,0:T(8,128)(2,1)S(1)}, u32[]{:S(2)}, u32[]{:S(2)}) async-start(bf16[8,576,128]{2,1,0:T(8,128)(2,1)} %rows_beside.1), calls=%async_computation | async-start | bytes 2359296 | tf_op jit(solution)/shard_map/all_to_all | solution.py:801
  22.5 34.5 %copy-start.21 = (f32[40]{0:T(128)S(1)}, f32[40]{0:T(128)}, u32[]{:S(2)}) copy-start(f32[40]{0:T(128)} %param.19) | copy-start | bytes 484
  22.5 34.7 %copy-start.13 = (f32[40]{0:T(128)S(1)}, f32[40]{0:T(128)}, u32[]{:S(2)}) copy-start(f32[40]{0:T(128)} %param.20) | copy-start | bytes 484
  22.5 34.8 %copy-start.14 = (f32[40]{0:T(128)S(1)}, f32[40]{0:T(128)}, u32[]{:S(2)}) copy-start(f32[40]{0:T(128)} %param.21) | copy-start | bytes 484
  53.5 6.5 %copy-start.2 = (bf16[8,576,128]{2,1,0:T(8,128)(2,1)}, bf16[8,576,128]{2,1,0:T(8,128)(2,1)S(1)}, u32[]{:S(2)}) copy-start(bf16[8,576,128]{2,1,0:T(8,128)(2,1)S(1)} %all-to-all-done.refs_0_.refs_1_.refs_2_) | copy-start | bytes 3538948
  53.5 27.1 %all-to-all-start.2 = ((bf16[8,384,128]{2,1,0:T(8,128)(2,1)}), bf16[8,384,128]{2,1,0:T(8,128)(2,1)S(1)}, u32[]{:S(2)}, u32[]{:S(2)}) async-start(bf16[8,384,128]{2,1,0:T(8,128)(2,1)} %get-tuple-element.66), calls=%async_computation.2 | async-start | bytes 1572864 | tf_op jit(solution)/shard_map/all_to_all | solution.py:801
  67.7 26.7 %collective-permute-start.4 = (f32[272,128]{1,0:T(8,128)S(1)}, f32[272,128]{1,0:T(8,128)S(1)}, u32[]{:S(2)}, u32[]{:S(2)}) collective-permute-start(f32[272,128]{1,0:T(8,128)S(1)} %get-tuple-element.102), channel_id=1, source_target_pairs={{0,24},{1,25},{2,26},{3,27},{4,28},{5,29},{6,30},{7,31},{8,0},{9,1... | collective-permute-start | bytes 417800 | tf_op jit(solution)/shard_map/ppermute | solution.py:825
  70.9 24.5 %collective-permute-start.3 = (f32[272,128]{1,0:T(8,128)S(1)}, f32[272,128]{1,0:T(8,128)S(1)}, u32[]{:S(2)}, u32[]{:S(2)}) collective-permute-start(f32[272,128]{1,0:T(8,128)S(1)} %get-tuple-element.103), channel_id=1, source_target_pairs={{0,16},{1,17},{2,18},{3,19},{4,20},{5,21},{6,22},{7,23},{8,24},{9,... | collective-permute-start | bytes 417800 | tf_op jit(solution)/shard_map/ppermute | solution.py:825
  71.4 23.9 %collective-permute-start.2 = (f32[272,128]{1,0:T(8,128)S(1)}, f32[272,128]{1,0:T(8,128)S(1)}, u32[]{:S(2)}, u32[]{:S(2)}) collective-permute-start(f32[272,128]{1,0:T(8,128)S(1)} %get-tuple-element.104), channel_id=1, source_target_pairs={{0,8},{1,9},{2,10},{3,11},{4,12},{5,13},{6,14},{7,15},{8,16},{9,17... | collective-permute-start | bytes 417800 | tf_op jit(solution)/shard_map/ppermute | solution.py:825
  80.6 1.1 copy-start.3
  90.6 22.4 %collective-permute-start.7 = (f32[400,128]{1,0:T(8,128)S(1)}, f32[400,128]{1,0:T(8,128)S(1)}, u32[]{:S(2)}, u32[]{:S(2)}) collective-permute-start(f32[400,128]{1,0:T(8,128)S(1)} %get-tuple-element.99), channel_id=1, source_target_pairs={{0,24},{1,25},{2,26},{3,27},{4,28},{5,29},{6,30},{7,31},{8,0},{9,1... | collective-permute-start | bytes 614408 | tf_op jit(solution)/shard_map/ppermute | solution.py:825
  92.1 21.0 %collective-permute-start.6 = (f32[400,128]{1,0:T(8,128)S(1)}, f32[400,128]{1,0:T(8,128)S(1)}, u32[]{:S(2)}, u32[]{:S(2)}) collective-permute-start(f32[400,128]{1,0:T(8,128)S(1)} %get-tuple-element.100), channel_id=1, source_target_pairs={{0,16},{1,17},{2,18},{3,19},{4,20},{5,21},{6,22},{7,23},{8,24},{9,... | collective-permute-start | bytes 614408 | tf_op jit(solution)/shard_map/ppermute | solution.py:825
  94.4 1.7 copy-start.18
  94.4 18.7 %collective-permute-start.5 = (f32[400,128]{1,0:T(8,128)S(1)}, f32[400,128]{1,0:T(8,128)S(1)}, u32[]{:S(2)}, u32[]{:S(2)}) collective-permute-start(f32[400,128]{1,0:T(8,128)S(1)} %get-tuple-element.101), channel_id=1, source_target_pairs={{0,8},{1,9},{2,10},{3,11},{4,12},{5,13},{6,14},{7,15},{8,16},{9,17... | collective-permute-start | bytes 614408 | tf_op jit(solution)/shard_map/ppermute | solution.py:825
  95.3 0.7 copy-start.19
  95.3 0.7 copy-start.20
  109.3 21.5 %all-to-all-start.1 = ((bf16[8,256,128]{2,1,0:T(8,128)(2,1)}), bf16[8,256,128]{2,1,0:T(8,128)(2,1)S(1)}, u32[]{:S(2)}, u32[]{:S(2)}) async-start(bf16[8,256,128]{2,1,0:T(8,128)(2,1)} %get-tuple-element.65), calls=%async_computation.1 | async-start | bytes 1048576 | tf_op jit(solution)/shard_map/all_to_all | solution.py:801
  113.0 0.7 copy-start.15
  113.1 0.7 copy-start.16
  113.1 0.8 copy-start.17
  130.8 7.0 %copy-start.8 = (f32[32,128]{1,0:T(8,128)S(1)}, f32[32,128]{1,0:T(8,128)}, u32[]{:S(2)}) copy-start(f32[32,128]{1,0:T(8,128)} %get-tuple-element.82) | copy-start | bytes 49156
  130.8 22.7 %copy-start.4 = (f32[4,24,128]{2,1,0:T(8,128)S(1)}, f32[4,24,128]{2,1,0:T(8,128)}, u32[]{:S(2)}) copy-start(f32[4,24,128]{2,1,0:T(8,128)} %get-tuple-element.81.edges) | copy-start | bytes 147460
  130.8 32.1 %copy-start.1 = (bf16[8,256,128]{2,1,0:T(8,128)(2,1)}, bf16[8,256,128]{2,1,0:T(8,128)(2,1)S(1)}, u32[]{:S(2)}) copy-start(bf16[8,256,128]{2,1,0:T(8,128)(2,1)S(1)} %all-to-all-done.1.refs_0_) | copy-start | bytes 1572868
  130.8 32.1 %all-to-all-start.3 = ((bf16[8,384,128]{2,1,0:T(8,128)(2,1)}), bf16[8,384,128]{2,1,0:T(8,128)(2,1)S(1)}, u32[]{:S(2)}, u32[]{:S(2)}) async-start(bf16[8,384,128]{2,1,0:T(8,128)(2,1)} %get-tuple-element.80), calls=%async_computation.3 | async-start | bytes 1572864 | tf_op jit(solution)/shard_map/all_to_all | solution.py:801
  137.8 1.3 collective-permute-start.10
  139.1 3.7 %collective-permute-start.11 = (f32[32,128]{1,0:T(8,128)S(1)}, f32[32,128]{1,0:T(8,128)S(1)}, u32[]{:S(2)}, u32[]{:S(2)}) collective-permute-start(f32[32,128]{1,0:T(8,128)S(1)} %add.47), channel_id=1, source_target_pairs={{0,64},{32,96},{64,0},{96,32},{128,192},{160,224},{192,128},{224,1... | collective-permute-start | bytes 49160 | tf_op jit(solution)/shard_map/ppermute | solution.py:831
  142.8 5.2 %collective-permute-start.12 = (f32[32,128]{1,0:T(8,128)S(1)}, f32[32,128]{1,0:T(8,128)S(1)}, u32[]{:S(2)}, u32[]{:S(2)}) collective-permute-start(f32[32,128]{1,0:T(8,128)S(1)} %add.48), channel_id=1, source_target_pairs={{0,128},{32,160},{64,192},{96,224},{128,0},{160,32},{192,64},{224,... | collective-permute-start | bytes 49160 | tf_op jit(solution)/shard_map/ppermute | solution.py:831
  148.1 3.7 %collective-permute-start.13 = (f32[32,128]{1,0:T(8,128)S(1)}, f32[32,128]{1,0:T(8,128)S(1)}, u32[]{:S(2)}, u32[]{:S(2)}) collective-permute-start(f32[32,128]{1,0:T(8,128)S(1)} %add.49), channel_id=1, source_target_pairs={{0,8},{1,9},{2,10},{3,11},{4,12},{5,13},{6,14},{7,15},{8,0},{9,1},... | collective-permute-start | bytes 49160 | tf_op jit(solution)/shard_map/ppermute | solution.py:831
  151.8 7.6 %collective-permute-start.14 = (f32[32,128]{1,0:T(8,128)S(1)}, f32[32,128]{1,0:T(8,128)S(1)}, u32[]{:S(2)}, u32[]{:S(2)}) collective-permute-start(f32[32,128]{1,0:T(8,128)S(1)} %add.50), channel_id=1, source_target_pairs={{0,16},{1,17},{2,18},{3,19},{4,20},{5,21},{6,22},{7,23},{8,24},{9,... | collective-permute-start | bytes 49160 | tf_op jit(solution)/shard_map/ppermute | solution.py:831
  153.5 6.5 %collective-permute-start.9 = (f32[24,128]{1,0:T(8,128)S(1)}, f32[24,128]{1,0:T(8,128)S(1)}, u32[]{:S(2)}, u32[]{:S(2)}) collective-permute-start(f32[24,128]{1,0:T(8,128)S(1)} %get-tuple-element.105), channel_id=1, source_target_pairs={{8,0},{9,1},{10,2},{11,3},{12,4},{13,5},{14,6},{15,7},{16,8},{17,9... | collective-permute-start | bytes 36872 | tf_op jit(solution)/shard_map/ppermute | solution.py:811
  154.8 5.9 %collective-permute-start.8 = (f32[24,128]{1,0:T(8,128)S(1)}, f32[24,128]{1,0:T(8,128)S(1)}, u32[]{:S(2)}, u32[]{:S(2)}) collective-permute-start(f32[24,128]{1,0:T(8,128)S(1)} %get-tuple-element.106), channel_id=1, source_target_pairs={{0,8},{1,9},{2,10},{3,11},{4,12},{5,13},{6,14},{7,15},{8,16},{9,17... | collective-permute-start | bytes 36872 | tf_op jit(solution)/shard_map/ppermute | solution.py:811
  160.0 0.8 copy-start.9
  160.8 0.6 copy-start.10
  162.9 37.9 %copy-start = (bf16[8,384,128]{2,1,0:T(8,128)(2,1)}, bf16[8,384,128]{2,1,0:T(8,128)(2,1)S(1)}, u32[]{:S(2)}) copy-start(bf16[8,384,128]{2,1,0:T(8,128)(2,1)S(1)} %all-to-all-done.3.refs_1_) | copy-start | bytes 2359300

commit v4 on v3

--- a/solution.py
+++ b/solution.py
@@ -19,7 +19,9 @@
 SETS = ((0, 2), (2, 5))
 SHARED = 2 * SETS[0][1] * WIDTH
 TAIL = SHARED + 2 * LANES
-PACK = TAIL + 64
+PACK = TAIL + 32
+SECOND = 2 * (SETS[1][1] - SETS[1][0]) * WIDTH
+PACK_2 = SECOND + 16
 EDGE = 2 * LANES + 8
 PARAMS = EDGE + 24
 WIDE = PARAMS + 32
@@ -107,7 +109,7 @@
         tail = jnp.concatenate(
             [part[target * 8 : target * 8 + 8] for part in parts] + [both], axis=0
         )
-        out_1[target, TAIL : TAIL + 32, :] = tail.astype(bf16)
+        out_1[target, TAIL:PACK, :] = tail.astype(bf16)
 
 
 def rows_beside_kernel(before_ref, after_ref, _, out, lines, sem):
@@ -115,12 +117,11 @@
         iota((8, GROUP * CH), 0) >= 5, before_ref[...].astype(f32), after_ref[...].astype(f32)
     )
     for target in range(GROUP):
-        mine = beside[:, target * CH : (target + 1) * CH]
-        mine = jnp.concatenate([mine, jnp.zeros((8, 4 * LANES - CH), f32)], axis=1)
-        lines[target] = jnp.concatenate(
-            [mine[:, j * LANES : (j + 1) * LANES] for j in range(4)], axis=0
-        ).astype(bf16)
-    copy = pltpu.make_async_copy(lines, out.at[:, TAIL + 32 : PACK, :], sem)
+        start = target * CH + SETS[1][0] * WIDTH
+        mine = beside[:, start : (target + 1) * CH]
+        mine = jnp.concatenate([mine, jnp.zeros((8, 2 * LANES - mine.shape[1]), f32)], axis=1)
+        lines[target] = jnp.concatenate([mine[:, :LANES], mine[:, LANES:]], axis=0).astype(bf16)
+    copy = pltpu.make_async_copy(lines, out.at[:, SECOND:PACK_2, :], sem)
     copy.start()
     copy.wait()
 
@@ -129,11 +130,10 @@
 
 
 def pack(complement, hidden, grad, b_rows, c_rows, dt_rows, ids):
-    rows = [PACK] + [2 * (last - first) * WIDTH for first, last in SETS[1:]]
     return pl.pallas_call(
         pack_kernel,
         name="pack",
-        out_shape=[jax.ShapeDtypeStruct((GROUP, count, LANES), bf16) for count in rows],
+        out_shape=[jax.ShapeDtypeStruct((GROUP, count, LANES), bf16) for count in (PACK, PACK_2)],
         in_specs=[pl.BlockSpec(memory_space=pltpu.SMEM)] + [WHOLE] * 6,
         out_specs=[WHOLE] * len(SETS),
         compiler_params=pltpu.CompilerParams(vmem_limit_bytes=VMEM),
@@ -149,7 +149,7 @@
         in_specs=[WHOLE, WHOLE, anywhere],
         out_specs=anywhere,
         scratch_shapes=[
-            pltpu.VMEM((GROUP, PACK - TAIL - 32, LANES), bf16),
+            pltpu.VMEM((GROUP, PACK_2 - SECOND, LANES), bf16),
             pltpu.SemaphoreType.DMA,
         ],
         input_output_aliases={2: 0},
@@ -190,29 +190,33 @@
     return slice(offset + head * WIDTH, offset + (head + 1) * WIDTH)
 
 
-def beside_chunk(pk1, which, place, block):
-    tail = pk1[which, TAIL:PACK, :].astype(f32)
-    lines = tail[32 + 8 * block : 40 + 8 * block]
+def beside_chunk(pk, which, place, block):
+    lines = pk[which, SECOND:PACK_2, :].astype(f32)[8 * block : 8 * block + 8]
     lines = jnp.concatenate([lines, jnp.zeros((8, LANES), f32)], axis=0).astype(bf16)
     return dot(lines, place, TN).astype(bf16)
 
 
-def fill_edges(ext, pk1, first):
+def fill_edges(ext, pk, beside):
+    if beside:
+        ext[0] = beside[0][...]
+        ext[GROUP + 1] = beside[1][...]
+        return
     token, place = iota((16, LANES), 0), iota((16, LANES), 1)
     before = zero_one((token >= 5) & (token < 8) & (place == token + LANES - 8))
     after = zero_one((token < 3) & (place == token))
     count = ext.shape[1]
     for start in range(0, count, LANES):
         size = min(LANES, count - start)
-        block = (first * WIDTH + start) // LANES
-        ext[0, start : start + size, :] = beside_chunk(pk1, 0, before, block)[:size]
-        ext[GROUP + 1, start : start + size, :] = beside_chunk(pk1, GROUP - 1, after, block)[:size]
+        block = start // LANES
+        ext[0, start : start + size, :] = beside_chunk(pk, 0, before, block)[:size]
+        ext[GROUP + 1, start : start + size, :] = beside_chunk(pk, GROUP - 1, after, block)[:size]
 
 
 def phase_one_kernel(first, heads, *refs):
+    beside = ()
     if first == 0:
-        pk1, cw, shift_table, rate = refs[:4]
-        pk, refs = pk1, refs[4:]
+        pk1, cw, shift_table, rate, *beside = refs[:6]
+        pk, refs = pk1, refs[6:]
         rows = refs[8]
         x_f, x_r, slope_f, slope_r, u_f, u_r, v_f, v_r = refs[:8]
         refs = refs[9:]
@@ -227,7 +231,7 @@
 
     @pl.when(pair == 0)
     def _():
-        fill_edges(ext, pk1, first)
+        fill_edges(ext, pk, beside)
         for chunk in range(GROUP):
             ext[chunk + 1] = pk[chunk, :width, :]
         if first == 0:
@@ -373,9 +377,12 @@
         x_f, x_r, slope_f, slope_r, u_f, u_r, v_f, v_r, rows, *ends,
     ) = refs[:18]
     refs = refs[18:]
+    beside = ()
     if first:
         wide_in, edges_in, params_in = refs[:3]
         refs = refs[3:]
+    else:
+        beside, refs = refs[:2], refs[2:]
     (
         rows_out, wide, edges, params,
         ext, entry, d_pre_f, d_pre_r, acc, lines, *of_chunk,
@@ -394,7 +401,7 @@
 
     @pl.when(pair == 0)
     def _():
-        fill_edges(ext, pk1, first)
+        fill_edges(ext, pk, beside)
         entry[...] = jnp.zeros_like(entry)
         here = place_y[0]
         for away in (3, 2, 1):
@@ -661,7 +668,9 @@
         + [chunked((width, LANES))] * 8
         + [kept(rows.shape)] + [kept(end.shape) for end in ends]
     )
-    if which:
+    if not which:
+        in_specs += [kept(block.shape) for block in carried]
+    else:
         in_specs += [chunked((WIDE, LANES)), kept((4, 24, LANES)), kept((32, LANES))]
     return pl.pallas_call(
         functools.partial(phase_two_kernel, first, heads),
@@ -831,10 +840,9 @@
     return lax.ppermute(array, axis, [(i, i ^ bit) for i in range(count)])
 
 
-def total_over_runs(array):
-    for axis, bit in (("dp", 1), ("dp", 2), ("dp", 4), ("seq", 8), ("seq", 16)):
-        array = array + flip_bit(array, axis, bit)
-    return array
+def total_over(array, axis, low, high):
+    near, far, both = (flip_bit(array, axis, bits) for bits in (low, high, low | high))
+    return (array + near) + (far + both)
 
 
 def per_device(
@@ -863,12 +871,18 @@
     packed = pack(
         complement, hidden[0], grad_out[0], b_proj[0], c_proj[0], dt_raw[0].T, base_ids
     )
-    packed = [add_rows_beside(before, after, packed[0]), *packed[1:]]
-    pk = [exchange(part) for part in packed]
-    saved, ends, sets, carried = [], [], [], ()
+    pk = [exchange(packed[0])]
+    second = add_rows_beside(before, after, packed[1])
+    second, taps, shift_table, rate, skip = lax.optimization_barrier(
+        (second, taps, shift_table, rate, skip)
+    )
+    pk.append(exchange(second))
+    cut = SETS[0][1] * WIDTH
+    edge_chunks = (along_y(pk[0][GROUP - 1, :cut], 1), along_y(pk[0][0, :cut], -1))
+    saved, ends, sets, carried = [], [], [], edge_chunks
     for which, tap in enumerate(taps):
         *blocks, up, down = phase_one(
-            which, pk[0], pk[which], tap, (rows,) if which else (shift_table, rate)
+            which, pk[0], pk[which], tap, (rows,) if which else (shift_table, rate, *edge_chunks)
         )
         if not which:
             rows = blocks.pop()
@@ -882,7 +896,11 @@
     wide, edges, sums = carried
     from_next = along_y(edges[2], -1)
     from_prev = along_y(edges[3], 1)
-    wide = exchange(finish(edges, from_prev, from_next, total_over_runs(sums), wide))
+    sums = total_over(sums, "dp", 1, 2)
+    sums, from_next, from_prev = lax.optimization_barrier((sums, from_next, from_prev))
+    sums = total_over(sums, "seq", GROUP, 2 * GROUP)
+    sums = sums + flip_bit(sums, "dp", 4)
+    wide = exchange(finish(edges, from_prev, from_next, sums, wide))
     layer_out, d_hidden, d_b, d_c, d_dt, taps, bias, rates, skips, shifts, codes = unpack(
         here_z, sets, wide
     )

time: 207 us -> 202 us (0.976)
  waiting for transfers between devices: 51 us -> 34.2 us
  starting transfers between devices: 48.9 us -> 59.5 us
    all_to_all x4, waiting for transfers between devices: 38.8 us -> 2.93 us  [exchange(): return lax.all_to_all(array, 'seq', 0, 0, axis_index_groups=Z_GROUPS)]
    ppermute x2, waiting for transfers between devices: 0.01 us -> 18.7 us  [beside(): lax.ppermute(array, 'seq', [(i, i + by) for i in range(count) if 0 <= i +...]
    ppermute x2 -> x4, waiting for transfers between devices: 0.76 us -> 5.77 us  [along_y(): return lax.ppermute(array, 'seq', pairs)]
    ppermute x5 -> x7, waiting for transfers between devices: 11.4 us -> 6.71 us  [flip_bit(): return lax.ppermute(array, axis, [(i, i ^ bit) for i in range(count)])]
    ppermute x2 -> x4, starting transfers between devices: 5.83 us -> 10.5 us  [along_y(): return lax.ppermute(array, 'seq', pairs)]
    ppermute x5 -> x7, starting transfers between devices: 4.29 us -> 7.52 us  [flip_bit(): return lax.ppermute(array, axis, [(i, i ^ bit) for i in range(count)])]
  transfers between devices with their start and end apart: 19 -> 23, of which waited for: 7 -> 8; matrix products, arithmetic and copies ran while one was open for 4% -> 4% of each run, Pallas kernels for 24% -> 24%
where the time goes in v4:
time: 202 us; the launch traced here: 201 us
  starting transfers between devices  59.5 us (29%)
  Pallas kernels  54.6 us (27%)
  blocking collectives  38.3 us (19%)
  waiting for transfers between devices  34.2 us (17%)
  local copies, waits for them, and re-layouts  9.14 us (5%)
  other arithmetic  4.13 us (2%)
    all_to_all x1, blocking collectives, exchange(): return lax.all_to_all(array, 'seq', 0, 0, axis_index_groups=Z_GROUPS)  38.3 us
    pallas_call x2, Pallas kernels, phase_two(): pl.pallas_call(functools.partial(phase_two_kernel, first, heads), name=f'...  30 us
    all_to_all x4, starting transfers between devices, exchange(): return lax.all_to_all(array, 'seq', 0, 0, axis_index_groups=Z_GROUPS)  25.6 us
    ppermute x2, waiting for transfers between devices, beside(): lax.ppermute(array, 'seq', [(i, i + by) for i in range(count) if 0 <= i +...  18.7 us
    pallas_call x2, Pallas kernels, phase_one(): pl.pallas_call(functools.partial(phase_one_kernel, first, heads), name=f'...  14.4 us
    ppermute x4, starting transfers between devices, along_y(): return lax.ppermute(array, 'seq', pairs)  10.5 us
    ppermute x6, starting transfers between devices, cross_y(): lax.ppermute(jnp.where(run + shift < ROWS, up, down), 'seq', pairs)  10.1 us
    ppermute x7, starting transfers between devices, flip_bit(): return lax.ppermute(array, axis, [(i, i ^ bit) for i in range(count)])  7.52 us
  transfers between devices with their start and end apart: 23, of which 8 were waited for; matrix products, arithmetic and copies ran while one was open for 4% of the time, Pallas kernels for 24%

profile of v4, /device:TPU:6, one launch (start us, length us, event | category | flops | bytes accessed | tf_op | source)
XLA Modules:
  0.0 201.1 jit_solution(12578166761157020002)
XLA Ops:
  0.6 3.6 %pack.1 = (bf16[8,544,128]{2,1,0:T(8,128)(2,1)}, bf16[8,400,128]{2,1,0:T(8,128)(2,1)}) custom-call(s32[12]{0:T(128)} %comp_ref.1, bf16[128,2560]{1,0:T(8,128)(2,1)} %bitcast.40, bf16[128,2560]{1,0:T(8,128)(2,1)} %bitcast.41, bf16[128,128]{1,0:T(8,128)(2,1)} %bitcast.44, bf16[128,128]{1,0:T(8,128)(2,1)} %bitcast.45, f32[40,128]{1,0:T(8,128)} %bitcast.46, ...), custom_call_target="tpu_custom_call" | custom-call | tf_op jit(solution)/shard_map/pack/pallas_call | solution.py:133
  4.3 8.6 %all-to-all-start = ((bf16[8,544,128]{2,1,0:T(8,128)(2,1)}), bf16[8,544,128]{2,1,0:T(8,128)(2,1)S(1)}, u32[]{:S(2)}, u32[]{:S(2)}) async-start(bf16[8,544,128]{2,1,0:T(8,128)(2,1)} %get-tuple-element.62), calls=%async_computation | async-start | bytes 2228224 | tf_op jit(solution)/shard_map/all_to_all | solution.py:810
  12.9 0.8 slice_bitcast_fusion
  13.7 1.3 collective-permute-start.1
  15.0 4.6 %collective-permute-start = (bf16[8,2560]{1,0:T(8,128)(2,1)S(1)}, bf16[8,2560]{1,0:T(8,128)(2,1)S(1)}, u32[]{:S(2)}, u32[]{:S(2)}) collective-permute-start(bf16[8,2560]{1,0:T(8,128)(2,1)S(1)} %get-tuple-element.118), channel_id=1, source_target_pairs={{0,1},{1,2},{2,3},{3,4},{4,5},{5,6},{6,7},{7,8},{8,9},{9,10},{10,1... | collective-permute-start | bytes 122888 | tf_op jit(solution)/shard_map/ppermute | solution.py:825
  19.6 0.1 concatenate.21
  19.7 0.1 copy.30
  19.8 0.1 concatenate.28
  19.9 0.1 concatenate.29
  20.0 0.1 concatenate.30
  20.1 0.1 concatenate.20
  20.2 0.1 fusion.4
  20.3 0.1 slice_bitcast_fusion.6
  20.4 0.7 pad.9.refs_2_
  21.1 0.2 slice_reduce_fusion
  21.3 18.7 %collective-permute-done.1.after_ref = bf16[8,2560]{1,0:T(8,128)(2,1)S(1)} collective-permute-done((bf16[8,2560]{1,0:T(8,128)(2,1)S(1)}, bf16[8,2560]{1,0:T(8,128)(2,1)S(1)}, u32[]{:S(2)}, u32[]{:S(2)}) %collective-permute-start.1) | collective-permute-done | bytes 40992 | tf_op jit(solution)/shard_map/ppermute | solution.py:825
  40.0 0.6 copy-done.6
  40.6 1.5 rows_beside.1
  42.1 0.7 broadcast_in_dim.55.refs_5_
  42.8 0.7 broadcast_in_dim.53.refs_3_.refs_4_
  43.5 0.9 broadcast_in_dim.50.refs_1_.refs_3_
  44.3 1.0 broadcast_in_dim.51.refs_2_.refs_3_
  45.3 5.8 %all-to-all-start.2 = ((bf16[8,400,128]{2,1,0:T(8,128)(2,1)}), bf16[8,400,128]{2,1,0:T(8,128)(2,1)S(1)}, u32[]{:S(2)}, u32[]{:S(2)}) async-start(bf16[8,400,128]{2,1,0:T(8,128)(2,1)} %rows_beside.1), calls=%async_computation.2 | async-start | bytes 1638400 | tf_op jit(solution)/shard_map/all_to_all | solution.py:810
  51.1 1.3 collective-permute-start.3
  52.4 4.5 %collective-permute-start.2 = (bf16[128,128]{1,0:T(8,128)(2,1)S(1)}, bf16[128,128]{1,0:T(8,128)(2,1)S(1)}, u32[]{:S(2)}, u32[]{:S(2)}) collective-permute-start(bf16[128,128]{1,0:T(8,128)(2,1)S(1)} %get-tuple-element.116), channel_id=1, source_target_pairs={{0,8},{1,9},{2,10},{3,11},{4,12},{5,13},{6,14},{7,15},{8,16},{9,17... | collective-permute-start | bytes 98312 | tf_op jit(solution)/shard_map/ppermute | solution.py:820
  57.0 1.5 collective-permute-done.2.refs_4_.refs_18_
  58.5 0.6 copy-done.22
  59.2 6.6 %phase_one_0.1 = (f32[8,128,128]{2,1,0:T(8,128)}, f32[8,128,128]{2,1,0:T(8,128)}, f32[8,128,128]{2,1,0:T(8,128)}, f32[8,128,128]{2,1,0:T(8,128)}, f32[8,128,128]...) custom-call(bf16[8,544,128]{2,1,0:T(8,128)(2,1)} %copy-done.2, ...), custom_call_target="tpu_custom_call" | custom-call | flops 8000000000 | bytes 8000000 | tf_op jit(solution)/shard_map/phase_one_0/pallas_call | solution.py:356
  65.7 1.0 broadcast_select_fusion.3
  66.7 4.1 %collective-permute-start.6 = (f32[272,128]{1,0:T(8,128)S(1)}, f32[272,128]{1,0:T(8,128)S(1)}, u32[]{:S(2)}, u32[]{:S(2)}) collective-permute-start(f32[272,128]{1,0:T(8,128)S(1)} %get-tuple-element.122), channel_id=1, source_target_pairs={{0,24},{1,25},{2,26},{3,27},{4,28},{5,29},{6,30},{7,31},{8,0},{9,1... | collective-permute-start | bytes 417800 | tf_op jit(solution)/shard_map/ppermute | solution.py:834
  70.8 0.3 collective-permute-start.5
  71.2 1.0 collective-permute-start.4
  72.2 2.9 %all-to-all-done.2.refs_1_.refs_2_ = bf16[8,400,128]{2,1,0:T(8,128)(2,1)S(1)} async-done(((bf16[8,400,128]{2,1,0:T(8,128)(2,1)}), bf16[8,400,128]{2,1,0:T(8,128)(2,1)S(1)}, u32[]{:S(2)}, u32[]{:S(2)}) %all-to-all-start.2) | async-done | bytes 819232 | tf_op jit(solution)/shard_map/all_to_all | solution.py:810
  75.1 0.9 copy-done.3
  76.0 7.8 %phase_one_1.1 = (f32[8,192,128]{2,1,0:T(8,128)}, f32[8,192,128]{2,1,0:T(8,128)}, f32[8,192,128]{2,1,0:T(8,128)}, f32[8,192,128]{2,1,0:T(8,128)}, f32[8,192,128]...) custom-call(bf16[8,544,128]{2,1,0:T(8,128)(2,1)} %copy-done.2, ...), custom_call_target="tpu_custom_call" | custom-call | flops 12000000000 | bytes 8000000 | tf_op jit(solution)/shard_map/phase_one_1/pallas_call | solution.py:356
  83.8 1.1 broadcast_select_fusion
  84.9 3.1 %collective-permute-start.9 = (f32[400,128]{1,0:T(8,128)S(1)}, f32[400,128]{1,0:T(8,128)S(1)}, u32[]{:S(2)}, u32[]{:S(2)}) collective-permute-start(f32[400,128]{1,0:T(8,128)S(1)} %get-tuple-element.119), channel_id=1, source_target_pairs={{0,24},{1,25},{2,26},{3,27},{4,28},{5,29},{6,30},{7,31},{8,0},{9,1... | collective-permute-start | bytes 614408 | tf_op jit(solution)/shard_map/ppermute | solution.py:834
  88.0 0.6 collective-permute-start.8
  88.6 1.0 collective-permute-start.7
  89.6 0.6 copy-done.19
  90.3 13.1 %phase_two_0.1 = (bf16[8,256,128]{2,1,0:T(8,128)(2,1)}, f32[8,320,128]{2,1,0:T(8,128)}, f32[4,24,128]{2,1,0:T(8,128)}, f32[32,128]{1,0:T(8,128)}) custom-call(s32[1]{0:T(128)} %bitcast.1.refs_0_, bf16[8,544,128]{2,1,0:T(8,128)(2,1)} %copy-done.2, bf16[8,544,128]{2,1,0:T(8,128)(2,1)} %copy-done.2, f32[5,128,128]{2,1,0:T(8,128)} %broadcast_in_dim.50.refs_1_.refs_3_, ...), custom_call_target="tpu_custom_call" | custom-call | flops 16000000000 | bytes 8000000 | tf_op jit(solution)/shard_map/phase_two_0/pallas_call | solution.py:675
  103.4 4.0 %all-to-all-start.1 = ((bf16[8,256,128]{2,1,0:T(8,128)(2,1)}), bf16[8,256,128]{2,1,0:T(8,128)(2,1)S(1)}, u32[]{:S(2)}, u32[]{:S(2)}) async-start(bf16[8,256,128]{2,1,0:T(8,128)(2,1)} %get-tuple-element.79), calls=%async_computation.1 | async-start | bytes 1048576 | tf_op jit(solution)/shard_map/all_to_all | solution.py:810
  107.4 0.6 copy-done.15
  108.2 16.9 %phase_two_1.1 = (bf16[8,384,128]{2,1,0:T(8,128)(2,1)}, f32[8,320,128]{2,1,0:T(8,128)}, f32[4,24,128]{2,1,0:T(8,128)}, f32[32,128]{1,0:T(8,128)}) custom-call(s32[1]{0:T(128)} %bitcast.1.refs_0_, bf16[8,544,128]{2,1,0:T(8,128)(2,1)} %copy-done.2, bf16[8,400,128]{2,1,0:T(8,128)(2,1)} %copy-done.3, f32[5,192,128]{2,1,0:T(8,128)} %broadcast_in_dim.51.refs_2_.refs_3_, ...), custom_call_target="tpu_custom_call" | custom-call | flops 24000000000 | bytes 8000000 | tf_op jit(solution)/shard_map/phase_two_1/pallas_call | solution.py:675
  125.1 7.2 %all-to-all-start.3 = ((bf16[8,384,128]{2,1,0:T(8,128)(2,1)}), bf16[8,384,128]{2,1,0:T(8,128)(2,1)S(1)}, u32[]{:S(2)}, u32[]{:S(2)}) async-start(bf16[8,384,128]{2,1,0:T(8,128)(2,1)} %get-tuple-element.95), calls=%async_computation.3 | async-start | bytes 1572864 | tf_op jit(solution)/shard_map/all_to_all | solution.py:810
  132.3 0.1 collective-permute-start.12
  132.4 0.9 collective-permute-start.11
  133.4 0.9 collective-permute-start.10
  134.3 3.3 %collective-permute-start.14 = (f32[24,128]{1,0:T(8,128)S(1)}, f32[24,128]{1,0:T(8,128)S(1)}, u32[]{:S(2)}, u32[]{:S(2)}) collective-permute-start(f32[24,128]{1,0:T(8,128)S(1)} %get-tuple-element.125), channel_id=1, source_target_pairs={{0,8},{1,9},{2,10},{3,11},{4,12},{5,13},{6,14},{7,15},{8,16},{9,17... | collective-permute-start | bytes 36872 | tf_op jit(solution)/shard_map/ppermute | solution.py:820
  137.7 1.3 collective-permute-start.13
  139.0 4.2 %collective-permute-done.13.from_next = f32[24,128]{1,0:T(8,128)S(1)} collective-permute-done((f32[24,128]{1,0:T(8,128)S(1)}, f32[24,128]{1,0:T(8,128)S(1)}, u32[]{:S(2)}, u32[]{:S(2)}) %collective-permute-start.13) | collective-permute-done | bytes 12320 | tf_op jit(solution)/shard_map/ppermute | solution.py:820
  143.2 1.5 collective-permute-start.17
  144.7 1.7 collective-permute-start.16
  146.5 0.9 collective-permute-start.15
  147.3 0.9 collective-permute-done.17
  148.2 1.8 collective-permute-done.16
  150.0 0.2 collective-permute-done.15
  150.2 1.5 collective-permute-start.18
  151.7 3.8 %collective-permute-done.18 = f32[32,128]{1,0:T(8,128)S(1)} collective-permute-done((f32[32,128]{1,0:T(8,128)S(1)}, f32[32,128]{1,0:T(8,128)S(1)}, u32[]{:S(2)}, u32[]{:S(2)}) %collective-permute-start.18) | collective-permute-done | bytes 16416 | tf_op jit(solution)/shard_map/ppermute | solution.py:840
  155.5 0.6 add.59.sums
  156.2 1.5 finish.1
  157.7 38.3 %all_to_all.25.refs_2_ = f32[8,320,128]{2,1,0:T(8,128)} all-to-all(f32[8,320,128]{2,1,0:T(8,128)} %finish.1), channel_id=1, replica_groups={{0,1,2,3,4,5,6,7},{8,9,10,11,12,13,14,15},{16,17,18,19,20,21,22,23},{24..., dimensions={0} | all-to-all | bytes 2621440 | tf_op jit(solution)/shard_map/all_to_all | solution.py:810
  196.1 3.7 %unpack.1 = (bf16[128,2560]{1,0:T(8,128)(2,1)}, bf16[128,2560]{1,0:T(8,128)(2,1)}, f32[128,128]{1,0:T(8,128)}, f32[128,128]{1,0:T(8,128)}, f32[40,128]{1,0:T(8,1...) custom-call(s32[1]{0:T(128)} %bitcast.place_z, ...), custom_call_target="tpu_custom_call" | custom-call | tf_op jit(solution)/shard_map/unpack/pallas_call | solution.py:795
  199.7 1.3 reduce.2
  (68 shorter events, 0.4 us)
Async XLA Ops:
  4.2 15.3 %copy-start.11 = (f32[2560]{0:T(1024)S(1)}, f32[2560]{0:T(1024)}, u32[]{:S(2)}) copy-start(f32[2560]{0:T(1024)} %param.24) | copy-start | bytes 30724
  4.2 15.4 %copy-start.12 = (f32[12,40]{1,0:T(8,128)S(1)}, f32[12,40]{1,0:T(8,128)}, u32[]{:S(2)}) copy-start(f32[12,40]{1,0:T(8,128)} %param.22) | copy-start | bytes 5764
  4.2 15.5 %copy-start.23 = (f32[40]{0:T(128)S(1)}, f32[40]{0:T(128)}, u32[]{:S(2)}) copy-start(f32[40]{0:T(128)} %param.19) | copy-start | bytes 484
  4.3 15.6 %copy-start.13 = (f32[40]{0:T(128)S(1)}, f32[40]{0:T(128)}, u32[]{:S(2)}) copy-start(f32[40]{0:T(128)} %param.20) | copy-start | bytes 484
  4.3 15.7 %copy-start.14 = (f32[40]{0:T(128)S(1)}, f32[40]{0:T(128)}, u32[]{:S(2)}) copy-start(f32[40]{0:T(128)} %param.21) | copy-start | bytes 484
  4.3 15.9 %copy-start.5 = (f32[4,2560]{1,0:T(4,128)S(1)}, f32[4,2560]{1,0:T(4,128)}, u32[]{:S(2)}) copy-start(f32[4,2560]{1,0:T(4,128)} %param.23) | copy-start | bytes 122884
  4.3 41.0 %all-to-all-start = ((bf16[8,544,128]{2,1,0:T(8,128)(2,1)}), bf16[8,544,128]{2,1,0:T(8,128)(2,1)S(1)}, u32[]{:S(2)}, u32[]{:S(2)}) async-start(bf16[8,544,128]{2,1,0:T(8,128)(2,1)} %get-tuple-element.62), calls=%async_computation | async-start | bytes 2228224 | tf_op jit(solution)/shard_map/all_to_all | solution.py:810
  13.7 26.3 %collective-permute-start.1 = (bf16[8,2560]{1,0:T(8,128)(2,1)S(1)}, bf16[8,2560]{1,0:T(8,128)(2,1)S(1)}, u32[]{:S(2)}, u32[]{:S(2)}) collective-permute-start(bf16[8,2560]{1,0:T(8,128)(2,1)S(1)} %get-tuple-element.117), channel_id=1, source_target_pairs={{1,0},{2,1},{3,2},{4,3},{5,4},{6,5},{7,6},{8,7},{9,8},{10,9},{11,1... | collective-permute-start | bytes 122888 | tf_op jit(solution)/shard_map/ppermute | solution.py:825
  15.0 25.0 %collective-permute-start = (bf16[8,2560]{1,0:T(8,128)(2,1)S(1)}, bf16[8,2560]{1,0:T(8,128)(2,1)S(1)}, u32[]{:S(2)}, u32[]{:S(2)}) collective-permute-start(bf16[8,2560]{1,0:T(8,128)(2,1)S(1)} %get-tuple-element.118), channel_id=1, source_target_pairs={{0,1},{1,2},{2,3},{3,4},{4,5},{5,6},{6,7},{7,8},{8,9},{9,10},{10,1... | collective-permute-start | bytes 122888 | tf_op jit(solution)/shard_map/ppermute | solution.py:825
  40.0 0.6 copy-start.6
  40.0 0.6 copy-start.7
  45.3 13.2 %copy-start.2 = (bf16[8,544,128]{2,1,0:T(8,128)(2,1)}, bf16[8,544,128]{2,1,0:T(8,128)(2,1)S(1)}, u32[]{:S(2)}) copy-start(bf16[8,544,128]{2,1,0:T(8,128)(2,1)S(1)} %all-to-all-done.refs_0_.refs_1_.refs_2_) | copy-start | bytes 3342340
  45.3 29.8 %all-to-all-start.2 = ((bf16[8,400,128]{2,1,0:T(8,128)(2,1)}), bf16[8,400,128]{2,1,0:T(8,128)(2,1)S(1)}, u32[]{:S(2)}, u32[]{:S(2)}) async-start(bf16[8,400,128]{2,1,0:T(8,128)(2,1)} %rows_beside.1), calls=%async_computation.2 | async-start | bytes 1638400 | tf_op jit(solution)/shard_map/all_to_all | solution.py:810
  51.1 5.9 %collective-permute-start.3 = (bf16[128,128]{1,0:T(8,128)(2,1)S(1)}, bf16[128,128]{1,0:T(8,128)(2,1)S(1)}, u32[]{:S(2)}, u32[]{:S(2)}) collective-permute-start(bf16[128,128]{1,0:T(8,128)(2,1)S(1)} %get-tuple-element.115), channel_id=1, source_target_pairs={{8,0},{9,1},{10,2},{11,3},{12,4},{13,5},{14,6},{15,7},{16,8},{17,9... | collective-permute-start | bytes 98312 | tf_op jit(solution)/shard_map/ppermute | solution.py:820
  52.4 6.1 %collective-permute-start.2 = (bf16[128,128]{1,0:T(8,128)(2,1)S(1)}, bf16[128,128]{1,0:T(8,128)(2,1)S(1)}, u32[]{:S(2)}, u32[]{:S(2)}) collective-permute-start(bf16[128,128]{1,0:T(8,128)(2,1)S(1)} %get-tuple-element.116), channel_id=1, source_target_pairs={{0,8},{1,9},{2,10},{3,11},{4,12},{5,13},{6,14},{7,15},{8,16},{9,17... | collective-permute-start | bytes 98312 | tf_op jit(solution)/shard_map/ppermute | solution.py:820
  57.0 1.6 copy-start.21
  58.5 0.6 copy-start.22
  66.7 21.9 %collective-permute-start.6 = (f32[272,128]{1,0:T(8,128)S(1)}, f32[272,128]{1,0:T(8,128)S(1)}, u32[]{:S(2)}, u32[]{:S(2)}) collective-permute-start(f32[272,128]{1,0:T(8,128)S(1)} %get-tuple-element.122), channel_id=1, source_target_pairs={{0,24},{1,25},{2,26},{3,27},{4,28},{5,29},{6,30},{7,31},{8,0},{9,1... | collective-permute-start | bytes 417800 | tf_op jit(solution)/shard_map/ppermute | solution.py:834
  70.8 18.7 %collective-permute-start.5 = (f32[272,128]{1,0:T(8,128)S(1)}, f32[272,128]{1,0:T(8,128)S(1)}, u32[]{:S(2)}, u32[]{:S(2)}) collective-permute-start(f32[272,128]{1,0:T(8,128)S(1)} %get-tuple-element.123), channel_id=1, source_target_pairs={{0,16},{1,17},{2,18},{3,19},{4,20},{5,21},{6,22},{7,23},{8,24},{9,... | collective-permute-start | bytes 417800 | tf_op jit(solution)/shard_map/ppermute | solution.py:834
  71.2 18.4 %collective-permute-start.4 = (f32[272,128]{1,0:T(8,128)S(1)}, f32[272,128]{1,0:T(8,128)S(1)}, u32[]{:S(2)}, u32[]{:S(2)}) collective-permute-start(f32[272,128]{1,0:T(8,128)S(1)} %get-tuple-element.124), channel_id=1, source_target_pairs={{0,8},{1,9},{2,10},{3,11},{4,12},{5,13},{6,14},{7,15},{8,16},{9,17... | collective-permute-start | bytes 417800 | tf_op jit(solution)/shard_map/ppermute | solution.py:834
  75.1 0.9 copy-start.3
  84.9 22.5 %collective-permute-start.9 = (f32[400,128]{1,0:T(8,128)S(1)}, f32[400,128]{1,0:T(8,128)S(1)}, u32[]{:S(2)}, u32[]{:S(2)}) collective-permute-start(f32[400,128]{1,0:T(8,128)S(1)} %get-tuple-element.119), channel_id=1, source_target_pairs={{0,24},{1,25},{2,26},{3,27},{4,28},{5,29},{6,30},{7,31},{8,0},{9,1... | collective-permute-start | bytes 614408 | tf_op jit(solution)/shard_map/ppermute | solution.py:834
  88.0 19.4 %collective-permute-start.8 = (f32[400,128]{1,0:T(8,128)S(1)}, f32[400,128]{1,0:T(8,128)S(1)}, u32[]{:S(2)}, u32[]{:S(2)}) collective-permute-start(f32[400,128]{1,0:T(8,128)S(1)} %get-tuple-element.120), channel_id=1, source_target_pairs={{0,16},{1,17},{2,18},{3,19},{4,20},{5,21},{6,22},{7,23},{8,24},{9,... | collective-permute-start | bytes 614408 | tf_op jit(solution)/shard_map/ppermute | solution.py:834
  88.6 1.0 copy-start.18
  88.6 18.8 %collective-permute-start.7 = (f32[400,128]{1,0:T(8,128)S(1)}, f32[400,128]{1,0:T(8,128)S(1)}, u32[]{:S(2)}, u32[]{:S(2)}) collective-permute-start(f32[400,128]{1,0:T(8,128)S(1)} %get-tuple-element.121), channel_id=1, source_target_pairs={{0,8},{1,9},{2,10},{3,11},{4,12},{5,13},{6,14},{7,15},{8,16},{9,17... | collective-permute-start | bytes 614408 | tf_op jit(solution)/shard_map/ppermute | solution.py:834
  89.6 0.7 copy-start.19
  89.6 0.7 copy-start.20
  103.4 21.7 %all-to-all-start.1 = ((bf16[8,256,128]{2,1,0:T(8,128)(2,1)}), bf16[8,256,128]{2,1,0:T(8,128)(2,1)S(1)}, u32[]{:S(2)}, u32[]{:S(2)}) async-start(bf16[8,256,128]{2,1,0:T(8,128)(2,1)} %get-tuple-element.79), calls=%async_computation.1 | async-start | bytes 1048576 | tf_op jit(solution)/shard_map/all_to_all | solution.py:810
  107.4 0.7 copy-start.15
  107.4 0.7 copy-start.16
  107.4 0.8 copy-start.17
  125.1 7.3 %copy-start.8 = (f32[32,128]{1,0:T(8,128)S(1)}, f32[32,128]{1,0:T(8,128)}, u32[]{:S(2)}) copy-start(f32[32,128]{1,0:T(8,128)} %get-tuple-element.97) | copy-start | bytes 49156
  125.1 9.2 %copy-start.4 = (f32[4,24,128]{2,1,0:T(8,128)S(1)}, f32[4,24,128]{2,1,0:T(8,128)}, u32[]{:S(2)}) copy-start(f32[4,24,128]{2,1,0:T(8,128)} %get-tuple-element.96.edges) | copy-start | bytes 147460
  125.1 32.6 %copy-start.1 = (bf16[8,256,128]{2,1,0:T(8,128)(2,1)}, bf16[8,256,128]{2,1,0:T(8,128)(2,1)S(1)}, u32[]{:S(2)}) copy-start(bf16[8,256,128]{2,1,0:T(8,128)(2,1)S(1)} %all-to-all-done.1.refs_0_) | copy-start | bytes 1572868
  125.1 32.6 %all-to-all-start.3 = ((bf16[8,384,128]{2,1,0:T(8,128)(2,1)}), bf16[8,384,128]{2,1,0:T(8,128)(2,1)S(1)}, u32[]{:S(2)}, u32[]{:S(2)}) async-start(bf16[8,384,128]{2,1,0:T(8,128)(2,1)} %get-tuple-element.95), calls=%async_computation.3 | async-start | bytes 1572864 | tf_op jit(solution)/shard_map/all_to_all | solution.py:810
  132.3 6.6 %collective-permute-start.12 = (f32[32,128]{1,0:T(8,128)S(1)}, f32[32,128]{1,0:T(8,128)S(1)}, u32[]{:S(2)}, u32[]{:S(2)}) collective-permute-start(f32[32,128]{1,0:T(8,128)S(1)} %copy-done.8), channel_id=1, source_target_pairs={{0,96},{32,64},{64,32},{96,0},{128,224},{160,192},{192,160},{224,1... | collective-permute-start | bytes 49160 | tf_op jit(solution)/shard_map/ppermute | solution.py:840
  132.4 6.5 %collective-permute-start.11 = (f32[32,128]{1,0:T(8,128)S(1)}, f32[32,128]{1,0:T(8,128)S(1)}, u32[]{:S(2)}, u32[]{:S(2)}) collective-permute-start(f32[32,128]{1,0:T(8,128)S(1)} %copy-done.8), channel_id=1, source_target_pairs={{0,64},{32,96},{64,0},{96,32},{128,192},{160,224},{192,128},{224,1... | collective-permute-start | bytes 49160 | tf_op jit(solution)/shard_map/ppermute | solution.py:840
  133.4 5.6 %collective-permute-start.10 = (f32[32,128]{1,0:T(8,128)S(1)}, f32[32,128]{1,0:T(8,128)S(1)}, u32[]{:S(2)}, u32[]{:S(2)}) collective-permute-start(f32[32,128]{1,0:T(8,128)S(1)} %copy-done.8), channel_id=1, source_target_pairs={{0,32},{32,0},{64,96},{96,64},{128,160},{160,128},{192,224},{224,1... | collective-permute-start | bytes 49160 | tf_op jit(solution)/shard_map/ppermute | solution.py:840
  134.3 4.7 %collective-permute-start.14 = (f32[24,128]{1,0:T(8,128)S(1)}, f32[24,128]{1,0:T(8,128)S(1)}, u32[]{:S(2)}, u32[]{:S(2)}) collective-permute-start(f32[24,128]{1,0:T(8,128)S(1)} %get-tuple-element.125), channel_id=1, source_target_pairs={{0,8},{1,9},{2,10},{3,11},{4,12},{5,13},{6,14},{7,15},{8,16},{9,17... | collective-permute-start | bytes 36872 | tf_op jit(solution)/shard_map/ppermute | solution.py:820
  137.7 5.6 %collective-permute-start.13 = (f32[24,128]{1,0:T(8,128)S(1)}, f32[24,128]{1,0:T(8,128)S(1)}, u32[]{:S(2)}, u32[]{:S(2)}) collective-permute-start(f32[24,128]{1,0:T(8,128)S(1)} %get-tuple-element.126), channel_id=1, source_target_pairs={{8,0},{9,1},{10,2},{11,3},{12,4},{13,5},{14,6},{15,7},{16,8},{17,9... | collective-permute-start | bytes 36872 | tf_op jit(solution)/shard_map/ppermute | solution.py:820
  139.0 17.1 %copy-start.9 = (f32[24,128]{1,0:T(8,128)}, f32[24,128]{1,0:T(8,128)S(1)}, u32[]{:S(2)}) copy-start(f32[24,128]{1,0:T(8,128)S(1)} %collective-permute-done.14.from_prev) | copy-start | bytes 36868
  143.2 12.9 %copy-start.10 = (f32[24,128]{1,0:T(8,128)}, f32[24,128]{1,0:T(8,128)S(1)}, u32[]{:S(2)}) copy-start(f32[24,128]{1,0:T(8,128)S(1)} %collective-permute-done.13.from_next) | copy-start | bytes 36868
  143.2 4.9 %collective-permute-start.17 = (f32[32,128]{1,0:T(8,128)S(1)}, f32[32,128]{1,0:T(8,128)S(1)}, u32[]{:S(2)}, u32[]{:S(2)}) collective-permute-start(f32[32,128]{1,0:T(8,128)S(1)} %add_add_fusion.1), channel_id=1, source_target_pairs={{0,24},{1,25},{2,26},{3,27},{4,28},{5,29},{6,30},{7,31},{8,16},{9,... | collective-permute-start | bytes 49160 | tf_op jit(solution)/shard_map/ppermute | solution.py:840
  144.7 5.2 %collective-permute-start.16 = (f32[32,128]{1,0:T(8,128)S(1)}, f32[32,128]{1,0:T(8,128)S(1)}, u32[]{:S(2)}, u32[]{:S(2)}) collective-permute-start(f32[32,128]{1,0:T(8,128)S(1)} %add_add_fusion.1), channel_id=1, source_target_pairs={{0,16},{1,17},{2,18},{3,19},{4,20},{5,21},{6,22},{7,23},{8,24},{9,... | collective-permute-start | bytes 49160 | tf_op jit(solution)/shard_map/ppermute | solution.py:840
  146.5 3.7 %collective-permute-start.15 = (f32[32,128]{1,0:T(8,128)S(1)}, f32[32,128]{1,0:T(8,128)S(1)}, u32[]{:S(2)}, u32[]{:S(2)}) collective-permute-start(f32[32,128]{1,0:T(8,128)S(1)} %add_add_fusion.1), channel_id=1, source_target_pairs={{0,8},{1,9},{2,10},{3,11},{4,12},{5,13},{6,14},{7,15},{8,0},{9,1},... | collective-permute-start | bytes 49160 | tf_op jit(solution)/shard_map/ppermute | solution.py:840
  150.2 5.3 %collective-permute-start.18 = (f32[32,128]{1,0:T(8,128)S(1)}, f32[32,128]{1,0:T(8,128)S(1)}, u32[]{:S(2)}, u32[]{:S(2)}) collective-permute-start(f32[32,128]{1,0:T(8,128)S(1)} %add_add_fusion), channel_id=1, source_target_pairs={{0,128},{32,160},{64,192},{96,224},{128,0},{160,32},{192,64},{224,... | collective-permute-start | bytes 49160 | tf_op jit(solution)/shard_map/ppermute | solution.py:840
  157.7 38.4 %copy-start = (bf16[8,384,128]{2,1,0:T(8,128)(2,1)}, bf16[8,384,128]{2,1,0:T(8,128)(2,1)S(1)}, u32[]{:S(2)}) copy-start(bf16[8,384,128]{2,1,0:T(8,128)(2,1)S(1)} %all-to-all-done.3.refs_1_) | copy-start | bytes 2359300

commit v5 on v4

--- a/solution.py
+++ b/solution.py
@@ -852,8 +852,6 @@
     place = lax.axis_index("seq")
     group, run = place % GROUP, place // GROUP
     here_z, here_y = group[None].astype(jnp.int32), run[None].astype(jnp.int32)
-    before = beside(hidden[0, -8:], 1)
-    after = beside(hidden[0, :8], -1)
     taps = jnp.concatenate([conv_w, conv_b[None]], axis=0).reshape(5, GROUP, CH)
     taps = lax.dynamic_index_in_dim(taps, group, 1, keepdims=False)
     cw = jnp.broadcast_to(taps[:, :, None], (5, CH, LANES))
@@ -872,10 +870,10 @@
         complement, hidden[0], grad_out[0], b_proj[0], c_proj[0], dt_raw[0].T, base_ids
     )
     pk = [exchange(packed[0])]
-    second = add_rows_beside(before, after, packed[1])
-    second, taps, shift_table, rate, skip = lax.optimization_barrier(
-        (second, taps, shift_table, rate, skip)
-    )
+    last, leading, taps, shift_table, rate, skip = lax.optimization_barrier(
+        (hidden[0, -8:], hidden[0, :8], taps, shift_table, rate, skip)
+    )
+    second = add_rows_beside(beside(last, 1), beside(leading, -1), packed[1])
     pk.append(exchange(second))
     cut = SETS[0][1] * WIDTH
     edge_chunks = (along_y(pk[0][GROUP - 1, :cut], 1), along_y(pk[0][0, :cut], -1))
@@ -894,11 +892,16 @@
         )
         sets.append(exchange(out))
     wide, edges, sums = carried
-    from_next = along_y(edges[2], -1)
-    from_prev = along_y(edges[3], 1)
+    lines = jnp.concatenate([sums, edges[2], edges[3]], axis=0)
+    near, both = flip_bit(lines, "seq", GROUP), flip_bit(lines, "seq", 3 * GROUP)
+    far = flip_bit(sums, "seq", 2 * GROUP)
+    odd = run % 2 == 1
+    from_next = jnp.where(odd, both[32:56], near[32:56])
+    from_next = jnp.where(run == ROWS - 1, 0.0, from_next)
+    from_prev = jnp.where(odd, near[56:], both[56:])
+    from_prev = jnp.where(run == 0, 0.0, from_prev)
+    sums = (sums + near[:32]) + (far + both[:32])
     sums = total_over(sums, "dp", 1, 2)
-    sums, from_next, from_prev = lax.optimization_barrier((sums, from_next, from_prev))
-    sums = total_over(sums, "seq", GROUP, 2 * GROUP)
     sums = sums + flip_bit(sums, "dp", 4)
     wide = exchange(finish(edges, from_prev, from_next, sums, wide))
     layer_out, d_hidden, d_b, d_c, d_dt, taps, bias, rates, skips, shifts, codes = unpack(

time: 202 us -> 198 us (0.980)
  starting transfers between devices: 59.5 us -> 53.6 us
    ppermute x4 -> x2, starting transfers between devices: 10.5 us -> 4.78 us  [along_y(): return lax.ppermute(array, 'seq', pairs)]
    ppermute x7, waiting for transfers between devices: 6.71 us -> 9.93 us  [flip_bit(): return lax.ppermute(array, axis, [(i, i ^ bit) for i in range(count)])]
    ppermute x2, waiting for transfers between devices: 18.7 us -> 16.2 us  [beside(): lax.ppermute(array, 'seq', [(i, i + by) for i in range(count) if 0 <= i +...]
    ppermute x4 -> x2, waiting for transfers between devices: 5.77 us -> 4.48 us  [along_y(): return lax.ppermute(array, 'seq', pairs)]
  transfers between devices with their start and end apart: 23 -> 21, of which waited for: 8 -> 11; matrix products, arithmetic and copies ran while one was open for 4% -> 5% of each run, Pallas kernels for 24% -> 24%
where the time goes in v5:
time: 198 us; the launch traced here: 197 us
  Pallas kernels  54.7 us (28%)
  starting transfers between devices  53.6 us (27%)
  blocking collectives  39.4 us (20%)
  waiting for transfers between devices  33.8 us (17%)
  local copies, waits for them, and re-layouts  9.15 us (5%)
  other arithmetic  4.74 us (2%)
    all_to_all x1, blocking collectives, exchange(): return lax.all_to_all(array, 'seq', 0, 0, axis_index_groups=Z_GROUPS)  39.4 us
    pallas_call x2, Pallas kernels, phase_two(): pl.pallas_call(functools.partial(phase_two_kernel, first, heads), name=f'...  30 us
    all_to_all x4, starting transfers between devices, exchange(): return lax.all_to_all(array, 'seq', 0, 0, axis_index_groups=Z_GROUPS)  24.5 us
    ppermute x2, waiting for transfers between devices, beside(): lax.ppermute(array, 'seq', [(i, i + by) for i in range(count) if 0 <= i +...  16.2 us
    pallas_call x2, Pallas kernels, phase_one(): pl.pallas_call(functools.partial(phase_one_kernel, first, heads), name=f'...  14.4 us
    ppermute x6, starting transfers between devices, cross_y(): lax.ppermute(jnp.where(run + shift < ROWS, up, down), 'seq', pairs)  11.5 us
    ppermute x7, waiting for transfers between devices, flip_bit(): return lax.ppermute(array, axis, [(i, i ^ bit) for i in range(count)])  9.93 us
    ppermute x7, starting transfers between devices, flip_bit(): return lax.ppermute(array, axis, [(i, i ^ bit) for i in range(count)])  7.7 us
  transfers between devices with their start and end apart: 21, of which 11 were waited for; matrix products, arithmetic and copies ran while one was open for 5% of the time, Pallas kernels for 24%

profile of v5, /device:TPU:6, one launch (start us, length us, event | category | flops | bytes accessed | tf_op | source)
XLA Modules:
  0.0 196.5 jit_solution(957305100338350990)
XLA Ops:
  0.6 3.6 %pack.1 = (bf16[8,544,128]{2,1,0:T(8,128)(2,1)}, bf16[8,400,128]{2,1,0:T(8,128)(2,1)}) custom-call(s32[12]{0:T(128)} %comp_ref.1, bf16[128,2560]{1,0:T(8,128)(2,1)} %bitcast.40, bf16[128,2560]{1,0:T(8,128)(2,1)} %bitcast.41, bf16[128,128]{1,0:T(8,128)(2,1)} %bitcast.44, bf16[128,128]{1,0:T(8,128)(2,1)} %bitcast.45, f32[40,128]{1,0:T(8,128)} %bitcast.46, ...), custom_call_target="tpu_custom_call" | custom-call | tf_op jit(solution)/shard_map/pack/pallas_call | solution.py:133
  4.3 8.6 %all-to-all-start = ((bf16[8,544,128]{2,1,0:T(8,128)(2,1)}), bf16[8,544,128]{2,1,0:T(8,128)(2,1)S(1)}, u32[]{:S(2)}, u32[]{:S(2)}) async-start(bf16[8,544,128]{2,1,0:T(8,128)(2,1)} %get-tuple-element.60), calls=%async_computation | async-start | bytes 2228224 | tf_op jit(solution)/shard_map/all_to_all | solution.py:810
  13.0 0.1 concatenate.23
  13.2 0.1 concatenate.32
  13.3 0.1 concatenate.33
  13.4 0.1 concatenate.34
  13.5 0.1 copy.30
  13.6 0.1 fusion.7
  13.7 0.1 slice_bitcast_fusion.6
  13.8 0.7 pad.9.refs_2_
  14.5 0.2 slice_reduce_fusion
  14.7 0.8 slice_bitcast_fusion
  15.5 0.9 broadcast_in_dim.55.refs_1_.refs_3_
  16.3 1.0 broadcast_in_dim.56.refs_2_.refs_3_
  17.3 0.7 broadcast_in_dim.58.refs_3_.refs_4_
  18.0 0.7 broadcast_in_dim.60.refs_5_
  18.7 3.9 %collective-permute-start.5 = (bf16[8,2560]{1,0:T(8,128)(2,1)S(1)}, bf16[8,2560]{1,0:T(8,128)(2,1)S(1)}, u32[]{:S(2)}, u32[]{:S(2)}) collective-permute-start(bf16[8,2560]{1,0:T(8,128)(2,1)S(1)} %get-tuple-element.77), channel_id=1, source_target_pairs={{0,1},{1,2},{2,3},{3,4},{4,5},{5,6},{6,7},{7,8},{8,9},{9,10},{10,1... | collective-permute-start | bytes 122888 | tf_op jit(solution)/shard_map/ppermute | solution.py:825
  22.6 1.3 collective-permute-start.6
  23.9 13.0 %collective-permute-done.5.before_ref = bf16[8,2560]{1,0:T(8,128)(2,1)S(1)} collective-permute-done((bf16[8,2560]{1,0:T(8,128)(2,1)S(1)}, bf16[8,2560]{1,0:T(8,128)(2,1)S(1)}, u32[]{:S(2)}, u32[]{:S(2)}) %collective-permute-start.5) | collective-permute-done | bytes 40992 | tf_op jit(solution)/shard_map/ppermute | solution.py:825
  36.9 3.2 %collective-permute-done.6.after_ref = bf16[8,2560]{1,0:T(8,128)(2,1)S(1)} collective-permute-done((bf16[8,2560]{1,0:T(8,128)(2,1)S(1)}, bf16[8,2560]{1,0:T(8,128)(2,1)S(1)}, u32[]{:S(2)}, u32[]{:S(2)}) %collective-permute-start.6) | collective-permute-done | bytes 40992 | tf_op jit(solution)/shard_map/ppermute | solution.py:825
  40.0 0.6 copy-done.8
  40.7 1.5 rows_beside.1
  42.2 1.0 all-to-all-done.refs_0_.refs_1_.refs_2_
  43.2 4.8 %all-to-all-start.2 = ((bf16[8,400,128]{2,1,0:T(8,128)(2,1)}), bf16[8,400,128]{2,1,0:T(8,128)(2,1)S(1)}, u32[]{:S(2)}, u32[]{:S(2)}) async-start(bf16[8,400,128]{2,1,0:T(8,128)(2,1)} %rows_beside.1), calls=%async_computation.2 | async-start | bytes 1638400 | tf_op jit(solution)/shard_map/all_to_all | solution.py:810
  48.0 3.5 %collective-permute-start = (bf16[128,128]{1,0:T(8,128)(2,1)S(1)}, bf16[128,128]{1,0:T(8,128)(2,1)S(1)}, u32[]{:S(2)}, u32[]{:S(2)}) collective-permute-start(bf16[128,128]{1,0:T(8,128)(2,1)S(1)} %get-tuple-element.112), channel_id=1, source_target_pairs={{0,8},{1,9},{2,10},{3,11},{4,12},{5,13},{6,14},{7,15},{8,16},{9,17... | collective-permute-start | bytes 98312 | tf_op jit(solution)/shard_map/ppermute | solution.py:820
  51.5 1.3 collective-permute-start.1
  52.8 0.3 collective-permute-done.refs_4_.refs_18_
  53.1 4.2 %collective-permute-done.1.refs_5_.refs_19_ = bf16[128,128]{1,0:T(8,128)(2,1)S(1)} collective-permute-done((bf16[128,128]{1,0:T(8,128)(2,1)S(1)}, bf16[128,128]{1,0:T(8,128)(2,1)S(1)}, u32[]{:S(2)}, u32[]{:S(2)}) %collective-permute-start.1) | collective-permute-done | bytes 32800 | tf_op jit(solution)/shard_map/ppermute | solution.py:820
  57.3 0.6 copy-done.20
  57.9 6.5 %phase_one_0.1 = (f32[8,128,128]{2,1,0:T(8,128)}, f32[8,128,128]{2,1,0:T(8,128)}, f32[8,128,128]{2,1,0:T(8,128)}, f32[8,128,128]{2,1,0:T(8,128)}, f32[8,128,128]...) custom-call(bf16[8,544,128]{2,1,0:T(8,128)(2,1)} %copy-done.2, ...), custom_call_target="tpu_custom_call" | custom-call | flops 8000000000 | bytes 8000000 | tf_op jit(solution)/shard_map/phase_one_0/pallas_call | solution.py:356
  64.5 1.0 broadcast_select_fusion.3
  65.5 1.7 collective-permute-start.2
  67.2 1.4 collective-permute-start.3
  68.6 2.5 %collective-permute-start.4 = (f32[272,128]{1,0:T(8,128)S(1)}, f32[272,128]{1,0:T(8,128)S(1)}, u32[]{:S(2)}, u32[]{:S(2)}) collective-permute-start(f32[272,128]{1,0:T(8,128)S(1)} %get-tuple-element.118), channel_id=1, source_target_pairs={{0,24},{1,25},{2,26},{3,27},{4,28},{5,29},{6,30},{7,31},{8,0},{9,1... | collective-permute-start | bytes 417800 | tf_op jit(solution)/shard_map/ppermute | solution.py:834
  71.1 0.9 all-to-all-done.2.refs_1_.refs_2_
  72.0 0.9 copy-done.3
  72.9 7.8 %phase_one_1.1 = (f32[8,192,128]{2,1,0:T(8,128)}, f32[8,192,128]{2,1,0:T(8,128)}, f32[8,192,128]{2,1,0:T(8,128)}, f32[8,192,128]{2,1,0:T(8,128)}, f32[8,192,128]...) custom-call(bf16[8,544,128]{2,1,0:T(8,128)(2,1)} %copy-done.2, ...), custom_call_target="tpu_custom_call" | custom-call | flops 12000000000 | bytes 8000000 | tf_op jit(solution)/shard_map/phase_one_1/pallas_call | solution.py:356
  80.7 1.1 broadcast_select_fusion
  81.8 1.7 collective-permute-start.7
  83.5 2.9 %collective-permute-start.8 = (f32[400,128]{1,0:T(8,128)S(1)}, f32[400,128]{1,0:T(8,128)S(1)}, u32[]{:S(2)}, u32[]{:S(2)}) collective-permute-start(f32[400,128]{1,0:T(8,128)S(1)} %get-tuple-element.116), channel_id=1, source_target_pairs={{0,16},{1,17},{2,18},{3,19},{4,20},{5,21},{6,22},{7,23},{8,24},{9,... | collective-permute-start | bytes 614408 | tf_op jit(solution)/shard_map/ppermute | solution.py:834
  86.4 1.3 collective-permute-start.9
  87.7 0.6 copy-done.17
  88.4 13.1 %phase_two_0.1 = (bf16[8,256,128]{2,1,0:T(8,128)(2,1)}, f32[8,320,128]{2,1,0:T(8,128)}, f32[4,24,128]{2,1,0:T(8,128)}, f32[32,128]{1,0:T(8,128)}) custom-call(s32[1]{0:T(128)} %bitcast.1.refs_0_, bf16[8,544,128]{2,1,0:T(8,128)(2,1)} %copy-done.2, bf16[8,544,128]{2,1,0:T(8,128)(2,1)} %copy-done.2, f32[5,128,128]{2,1,0:T(8,128)} %broadcast_in_dim.55.refs_1_.refs_3_, ...), custom_call_target="tpu_custom_call" | custom-call | flops 16000000000 | bytes 8000000 | tf_op jit(solution)/shard_map/phase_two_0/pallas_call | solution.py:675
  101.5 3.8 %all-to-all-start.1 = ((bf16[8,256,128]{2,1,0:T(8,128)(2,1)}), bf16[8,256,128]{2,1,0:T(8,128)(2,1)S(1)}, u32[]{:S(2)}, u32[]{:S(2)}) async-start(bf16[8,256,128]{2,1,0:T(8,128)(2,1)} %get-tuple-element.76), calls=%async_computation.1 | async-start | bytes 1048576 | tf_op jit(solution)/shard_map/all_to_all | solution.py:810
  105.4 0.6 copy-done.13
  106.2 16.9 %phase_two_1.1 = (bf16[8,384,128]{2,1,0:T(8,128)(2,1)}, f32[8,320,128]{2,1,0:T(8,128)}, f32[4,24,128]{2,1,0:T(8,128)}, f32[32,128]{1,0:T(8,128)}) custom-call(s32[1]{0:T(128)} %bitcast.1.refs_0_, bf16[8,544,128]{2,1,0:T(8,128)(2,1)} %copy-done.2, bf16[8,400,128]{2,1,0:T(8,128)(2,1)} %copy-done.3, f32[5,192,128]{2,1,0:T(8,128)} %broadcast_in_dim.56.refs_2_.refs_3_, ...), custom_call_target="tpu_custom_call" | custom-call | flops 24000000000 | bytes 8000000 | tf_op jit(solution)/shard_map/phase_two_1/pallas_call | solution.py:675
  123.1 7.2 %all-to-all-start.3 = ((bf16[8,384,128]{2,1,0:T(8,128)(2,1)}), bf16[8,384,128]{2,1,0:T(8,128)(2,1)S(1)}, u32[]{:S(2)}, u32[]{:S(2)}) async-start(bf16[8,384,128]{2,1,0:T(8,128)(2,1)} %get-tuple-element.94), calls=%async_computation.3 | async-start | bytes 1572864 | tf_op jit(solution)/shard_map/all_to_all | solution.py:810
  130.4 0.9 collective-permute-start.10
  131.3 2.6 %collective-permute-start.11 = (f32[80,128]{1,0:T(8,128)S(1)}, f32[80,128]{1,0:T(8,128)S(1)}, u32[]{:S(2)}, u32[]{:S(2)}) collective-permute-start(f32[80,128]{1,0:T(8,128)S(1)} %pad_maximum_fusion), channel_id=1, source_target_pairs={{0,24},{1,25},{2,26},{3,27},{4,28},{5,29},{6,30},{7,31},{8,16},{9,... | collective-permute-start | bytes 122888 | tf_op jit(solution)/shard_map/ppermute | solution.py:840
  133.9 0.7 collective-permute-start.12
  134.6 4.5 %collective-permute-done.12 = f32[32,128]{1,0:T(8,128)S(1)} collective-permute-done((f32[32,128]{1,0:T(8,128)S(1)}, f32[32,128]{1,0:T(8,128)S(1)}, u32[]{:S(2)}, u32[]{:S(2)}) %collective-permute-start.12) | collective-permute-done | bytes 16416 | tf_op jit(solution)/shard_map/ppermute | solution.py:840
  139.1 0.9 collective-permute-start.14
  140.1 1.3 collective-permute-start.13
  141.4 1.6 collective-permute-done.14
  143.0 0.4 collective-permute-done.15
  143.3 1.3 collective-permute-start.16
  144.6 0.6 fusion.1
  145.2 3.4 %collective-permute-done.16 = f32[32,128]{1,0:T(8,128)S(1)} collective-permute-done((f32[32,128]{1,0:T(8,128)S(1)}, f32[32,128]{1,0:T(8,128)S(1)}, u32[]{:S(2)}, u32[]{:S(2)}) %collective-permute-start.16) | collective-permute-done | bytes 16416 | tf_op jit(solution)/shard_map/ppermute | solution.py:840
  148.6 0.6 add.63.sums
  149.3 1.5 finish.1
  150.8 1.3 all-to-all-done.3.refs_1_
  152.1 39.4 %all_to_all.25.refs_2_ = f32[8,320,128]{2,1,0:T(8,128)} all-to-all(f32[8,320,128]{2,1,0:T(8,128)} %finish.1), channel_id=1, replica_groups={{0,1,2,3,4,5,6,7},{8,9,10,11,12,13,14,15},{16,17,18,19,20,21,22,23},{24..., dimensions={0} | all-to-all | bytes 2621440 | tf_op jit(solution)/shard_map/all_to_all | solution.py:810
  191.5 3.7 %unpack.1 = (bf16[128,2560]{1,0:T(8,128)(2,1)}, bf16[128,2560]{1,0:T(8,128)(2,1)}, f32[128,128]{1,0:T(8,128)}, f32[128,128]{1,0:T(8,128)}, f32[40,128]{1,0:T(8,1...) custom-call(s32[1]{0:T(128)} %bitcast.place_z, ...), custom_call_target="tpu_custom_call" | custom-call | tf_op jit(solution)/shard_map/unpack/pallas_call | solution.py:795
  195.2 1.3 reduce.2
  (62 shorter events, 0.4 us)
Async XLA Ops:
  4.3 8.7 %copy-start.6 = (f32[4,2560]{1,0:T(4,128)S(1)}, f32[4,2560]{1,0:T(4,128)}, u32[]{:S(2)}) copy-start(f32[4,2560]{1,0:T(4,128)} %param.23) | copy-start | bytes 122884
  4.3 8.8 %copy-start.9 = (f32[2560]{0:T(1024)S(1)}, f32[2560]{0:T(1024)}, u32[]{:S(2)}) copy-start(f32[2560]{0:T(1024)} %param.24) | copy-start | bytes 30724
  4.3 8.9 %copy-start.21 = (f32[40]{0:T(128)S(1)}, f32[40]{0:T(128)}, u32[]{:S(2)}) copy-start(f32[40]{0:T(128)} %param.19) | copy-start | bytes 484
  4.3 9.0 %copy-start.11 = (f32[40]{0:T(128)S(1)}, f32[40]{0:T(128)}, u32[]{:S(2)}) copy-start(f32[40]{0:T(128)} %param.20) | copy-start | bytes 484
  4.3 9.1 %copy-start.12 = (f32[40]{0:T(128)S(1)}, f32[40]{0:T(128)}, u32[]{:S(2)}) copy-start(f32[40]{0:T(128)} %param.21) | copy-start | bytes 484
  4.3 9.2 %copy-start.10 = (f32[12,40]{1,0:T(8,128)S(1)}, f32[12,40]{1,0:T(8,128)}, u32[]{:S(2)}) copy-start(f32[12,40]{1,0:T(8,128)} %param.22) | copy-start | bytes 5764
  4.3 38.9 %all-to-all-start = ((bf16[8,544,128]{2,1,0:T(8,128)(2,1)}), bf16[8,544,128]{2,1,0:T(8,128)(2,1)S(1)}, u32[]{:S(2)}, u32[]{:S(2)}) async-start(bf16[8,544,128]{2,1,0:T(8,128)(2,1)} %get-tuple-element.60), calls=%async_computation | async-start | bytes 2228224 | tf_op jit(solution)/shard_map/all_to_all | solution.py:810
  18.7 18.2 %collective-permute-start.5 = (bf16[8,2560]{1,0:T(8,128)(2,1)S(1)}, bf16[8,2560]{1,0:T(8,128)(2,1)S(1)}, u32[]{:S(2)}, u32[]{:S(2)}) collective-permute-start(bf16[8,2560]{1,0:T(8,128)(2,1)S(1)} %get-tuple-element.77), channel_id=1, source_target_pairs={{0,1},{1,2},{2,3},{3,4},{4,5},{5,6},{6,7},{7,8},{8,9},{9,10},{10,1... | collective-permute-start | bytes 122888 | tf_op jit(solution)/shard_map/ppermute | solution.py:825
  22.6 17.5 %collective-permute-start.6 = (bf16[8,2560]{1,0:T(8,128)(2,1)S(1)}, bf16[8,2560]{1,0:T(8,128)(2,1)S(1)}, u32[]{:S(2)}, u32[]{:S(2)}) collective-permute-start(bf16[8,2560]{1,0:T(8,128)(2,1)S(1)} %get-tuple-element.78), channel_id=1, source_target_pairs={{1,0},{2,1},{3,2},{4,3},{5,4},{6,5},{7,6},{8,7},{9,8},{10,9},{11,1... | collective-permute-start | bytes 122888 | tf_op jit(solution)/shard_map/ppermute | solution.py:825
  36.8 3.2 %copy-start.7 = (bf16[8,2560]{1,0:T(8,128)(2,1)}, bf16[8,2560]{1,0:T(8,128)(2,1)S(1)}, u32[]{:S(2)}) copy-start(bf16[8,2560]{1,0:T(8,128)(2,1)S(1)} %collective-permute-done.5.before_ref) | copy-start | bytes 122884
  40.0 0.6 copy-start.8
  43.2 14.1 %copy-start.2 = (bf16[8,544,128]{2,1,0:T(8,128)(2,1)}, bf16[8,544,128]{2,1,0:T(8,128)(2,1)S(1)}, u32[]{:S(2)}) copy-start(bf16[8,544,128]{2,1,0:T(8,128)(2,1)S(1)} %all-to-all-done.refs_0_.refs_1_.refs_2_) | copy-start | bytes 3342340
  43.2 28.8 %all-to-all-start.2 = ((bf16[8,400,128]{2,1,0:T(8,128)(2,1)}), bf16[8,400,128]{2,1,0:T(8,128)(2,1)S(1)}, u32[]{:S(2)}, u32[]{:S(2)}) async-start(bf16[8,400,128]{2,1,0:T(8,128)(2,1)} %rows_beside.1), calls=%async_computation.2 | async-start | bytes 1638400 | tf_op jit(solution)/shard_map/all_to_all | solution.py:810
  48.0 5.1 %collective-permute-start = (bf16[128,128]{1,0:T(8,128)(2,1)S(1)}, bf16[128,128]{1,0:T(8,128)(2,1)S(1)}, u32[]{:S(2)}, u32[]{:S(2)}) collective-permute-start(bf16[128,128]{1,0:T(8,128)(2,1)S(1)} %get-tuple-element.112), channel_id=1, source_target_pairs={{0,8},{1,9},{2,10},{3,11},{4,12},{5,13},{6,14},{7,15},{8,16},{9,17... | collective-permute-start | bytes 98312 | tf_op jit(solution)/shard_map/ppermute | solution.py:820
  51.5 5.8 %collective-permute-start.1 = (bf16[128,128]{1,0:T(8,128)(2,1)S(1)}, bf16[128,128]{1,0:T(8,128)(2,1)S(1)}, u32[]{:S(2)}, u32[]{:S(2)}) collective-permute-start(bf16[128,128]{1,0:T(8,128)(2,1)S(1)} %get-tuple-element.111), channel_id=1, source_target_pairs={{8,0},{9,1},{10,2},{11,3},{12,4},{13,5},{14,6},{15,7},{16,8},{17,9... | collective-permute-start | bytes 98312 | tf_op jit(solution)/shard_map/ppermute | solution.py:820
  53.1 4.2 %copy-start.19 = (bf16[128,128]{1,0:T(8,128)(2,1)}, bf16[128,128]{1,0:T(8,128)(2,1)S(1)}, u32[]{:S(2)}) copy-start(bf16[128,128]{1,0:T(8,128)(2,1)S(1)} %collective-permute-done.refs_4_.refs_18_) | copy-start | bytes 98308
  57.3 0.6 copy-start.20
  65.5 20.9 %collective-permute-start.2 = (f32[272,128]{1,0:T(8,128)S(1)}, f32[272,128]{1,0:T(8,128)S(1)}, u32[]{:S(2)}, u32[]{:S(2)}) collective-permute-start(f32[272,128]{1,0:T(8,128)S(1)} %get-tuple-element.120), channel_id=1, source_target_pairs={{0,8},{1,9},{2,10},{3,11},{4,12},{5,13},{6,14},{7,15},{8,16},{9,17... | collective-permute-start | bytes 417800 | tf_op jit(solution)/shard_map/ppermute | solution.py:834
  67.2 20.6 %collective-permute-start.3 = (f32[272,128]{1,0:T(8,128)S(1)}, f32[272,128]{1,0:T(8,128)S(1)}, u32[]{:S(2)}, u32[]{:S(2)}) collective-permute-start(f32[272,128]{1,0:T(8,128)S(1)} %get-tuple-element.119), channel_id=1, source_target_pairs={{0,16},{1,17},{2,18},{3,19},{4,20},{5,21},{6,22},{7,23},{8,24},{9,... | collective-permute-start | bytes 417800 | tf_op jit(solution)/shard_map/ppermute | solution.py:834
  68.6 19.1 %collective-permute-start.4 = (f32[272,128]{1,0:T(8,128)S(1)}, f32[272,128]{1,0:T(8,128)S(1)}, u32[]{:S(2)}, u32[]{:S(2)}) collective-permute-start(f32[272,128]{1,0:T(8,128)S(1)} %get-tuple-element.118), channel_id=1, source_target_pairs={{0,24},{1,25},{2,26},{3,27},{4,28},{5,29},{6,30},{7,31},{8,0},{9,1... | collective-permute-start | bytes 417800 | tf_op jit(solution)/shard_map/ppermute | solution.py:834
  72.0 0.9 copy-start.3
  81.8 23.6 %collective-permute-start.7 = (f32[400,128]{1,0:T(8,128)S(1)}, f32[400,128]{1,0:T(8,128)S(1)}, u32[]{:S(2)}, u32[]{:S(2)}) collective-permute-start(f32[400,128]{1,0:T(8,128)S(1)} %get-tuple-element.117), channel_id=1, source_target_pairs={{0,8},{1,9},{2,10},{3,11},{4,12},{5,13},{6,14},{7,15},{8,16},{9,17... | collective-permute-start | bytes 614408 | tf_op jit(solution)/shard_map/ppermute | solution.py:834
  83.5 21.9 %collective-permute-start.8 = (f32[400,128]{1,0:T(8,128)S(1)}, f32[400,128]{1,0:T(8,128)S(1)}, u32[]{:S(2)}, u32[]{:S(2)}) collective-permute-start(f32[400,128]{1,0:T(8,128)S(1)} %get-tuple-element.116), channel_id=1, source_target_pairs={{0,16},{1,17},{2,18},{3,19},{4,20},{5,21},{6,22},{7,23},{8,24},{9,... | collective-permute-start | bytes 614408 | tf_op jit(solution)/shard_map/ppermute | solution.py:834
  86.4 1.4 copy-start.16
  86.4 19.0 %collective-permute-start.9 = (f32[400,128]{1,0:T(8,128)S(1)}, f32[400,128]{1,0:T(8,128)S(1)}, u32[]{:S(2)}, u32[]{:S(2)}) collective-permute-start(f32[400,128]{1,0:T(8,128)S(1)} %get-tuple-element.115), channel_id=1, source_target_pairs={{0,24},{1,25},{2,26},{3,27},{4,28},{5,29},{6,30},{7,31},{8,0},{9,1... | collective-permute-start | bytes 614408 | tf_op jit(solution)/shard_map/ppermute | solution.py:834
  87.7 0.7 copy-start.17
  87.7 0.7 copy-start.18
  101.5 21.6 %all-to-all-start.1 = ((bf16[8,256,128]{2,1,0:T(8,128)(2,1)}), bf16[8,256,128]{2,1,0:T(8,128)(2,1)S(1)}, u32[]{:S(2)}, u32[]{:S(2)}) async-start(bf16[8,256,128]{2,1,0:T(8,128)(2,1)} %get-tuple-element.76), calls=%async_computation.1 | async-start | bytes 1048576 | tf_op jit(solution)/shard_map/all_to_all | solution.py:810
  105.4 0.7 copy-start.13
  105.4 0.7 copy-start.14
  105.4 0.8 copy-start.15
  123.1 7.3 %copy-start.4 = (f32[4,24,128]{2,1,0:T(8,128)S(1)}, f32[4,24,128]{2,1,0:T(8,128)}, u32[]{:S(2)}) copy-start(f32[4,24,128]{2,1,0:T(8,128)} %get-tuple-element.95.edges) | copy-start | bytes 147460
  123.1 7.3 %copy-start.5 = (f32[32,128]{1,0:T(8,128)S(1)}, f32[32,128]{1,0:T(8,128)}, u32[]{:S(2)}) copy-start(f32[32,128]{1,0:T(8,128)} %get-tuple-element.96) | copy-start | bytes 49156
  123.1 27.7 %copy-start.1 = (bf16[8,256,128]{2,1,0:T(8,128)(2,1)}, bf16[8,256,128]{2,1,0:T(8,128)(2,1)S(1)}, u32[]{:S(2)}) copy-start(bf16[8,256,128]{2,1,0:T(8,128)(2,1)S(1)} %all-to-all-done.1.refs_0_) | copy-start | bytes 1572868
  123.1 29.0 %all-to-all-start.3 = ((bf16[8,384,128]{2,1,0:T(8,128)(2,1)}), bf16[8,384,128]{2,1,0:T(8,128)(2,1)S(1)}, u32[]{:S(2)}, u32[]{:S(2)}) async-start(bf16[8,384,128]{2,1,0:T(8,128)(2,1)} %get-tuple-element.94), calls=%async_computation.3 | async-start | bytes 1572864 | tf_op jit(solution)/shard_map/all_to_all | solution.py:810
  130.4 8.7 %collective-permute-start.10 = (f32[80,128]{1,0:T(8,128)S(1)}, f32[80,128]{1,0:T(8,128)S(1)}, u32[]{:S(2)}, u32[]{:S(2)}) collective-permute-start(f32[80,128]{1,0:T(8,128)S(1)} %pad_maximum_fusion), channel_id=1, source_target_pairs={{0,8},{1,9},{2,10},{3,11},{4,12},{5,13},{6,14},{7,15},{8,0},{9,1},... | collective-permute-start | bytes 122888 | tf_op jit(solution)/shard_map/ppermute | solution.py:840
  131.3 7.8 %collective-permute-start.11 = (f32[80,128]{1,0:T(8,128)S(1)}, f32[80,128]{1,0:T(8,128)S(1)}, u32[]{:S(2)}, u32[]{:S(2)}) collective-permute-start(f32[80,128]{1,0:T(8,128)S(1)} %pad_maximum_fusion), channel_id=1, source_target_pairs={{0,24},{1,25},{2,26},{3,27},{4,28},{5,29},{6,30},{7,31},{8,16},{9,... | collective-permute-start | bytes 122888 | tf_op jit(solution)/shard_map/ppermute | solution.py:840
  133.9 5.2 %collective-permute-start.12 = (f32[32,128]{1,0:T(8,128)S(1)}, f32[32,128]{1,0:T(8,128)S(1)}, u32[]{:S(2)}, u32[]{:S(2)}) collective-permute-start(f32[32,128]{1,0:T(8,128)S(1)} %copy-done.5), channel_id=1, source_target_pairs={{0,16},{1,17},{2,18},{3,19},{4,20},{5,21},{6,22},{7,23},{8,24},{9,... | collective-permute-start | bytes 49160 | tf_op jit(solution)/shard_map/ppermute | solution.py:840
  139.1 3.8 %collective-permute-start.14 = (f32[32,128]{1,0:T(8,128)S(1)}, f32[32,128]{1,0:T(8,128)S(1)}, u32[]{:S(2)}, u32[]{:S(2)}) collective-permute-start(f32[32,128]{1,0:T(8,128)S(1)} %fusion), channel_id=1, source_target_pairs={{0,64},{32,96},{64,0},{96,32},{128,192},{160,224},{192,128},{224,1... | collective-permute-start | bytes 49160 | tf_op jit(solution)/shard_map/ppermute | solution.py:840
  140.1 3.2 %collective-permute-start.15 = (f32[32,128]{1,0:T(8,128)S(1)}, f32[32,128]{1,0:T(8,128)S(1)}, u32[]{:S(2)}, u32[]{:S(2)}) collective-permute-start(f32[32,128]{1,0:T(8,128)S(1)} %fusion), channel_id=1, source_target_pairs={{0,96},{32,64},{64,32},{96,0},{128,224},{160,192},{192,160},{224,1... | collective-permute-start | bytes 49160 | tf_op jit(solution)/shard_map/ppermute | solution.py:840
  140.1 3.2 %collective-permute-start.13 = (f32[32,128]{1,0:T(8,128)S(1)}, f32[32,128]{1,0:T(8,128)S(1)}, u32[]{:S(2)}, u32[]{:S(2)}) collective-permute-start(f32[32,128]{1,0:T(8,128)S(1)} %fusion), channel_id=1, source_target_pairs={{0,32},{32,0},{64,96},{96,64},{128,160},{160,128},{192,224},{224,1... | collective-permute-start | bytes 49160 | tf_op jit(solution)/shard_map/ppermute | solution.py:840
  143.3 5.3 %collective-permute-start.16 = (f32[32,128]{1,0:T(8,128)S(1)}, f32[32,128]{1,0:T(8,128)S(1)}, u32[]{:S(2)}, u32[]{:S(2)}) collective-permute-start(f32[32,128]{1,0:T(8,128)S(1)} %add_add_fusion), channel_id=1, source_target_pairs={{0,128},{32,160},{64,192},{96,224},{128,0},{160,32},{192,64},{224,... | collective-permute-start | bytes 49160 | tf_op jit(solution)/shard_map/ppermute | solution.py:840
  152.1 39.4 %copy-start = (bf16[8,384,128]{2,1,0:T(8,128)(2,1)}, bf16[8,384,128]{2,1,0:T(8,128)(2,1)S(1)}, u32[]{:S(2)}) copy-start(bf16[8,384,128]{2,1,0:T(8,128)(2,1)S(1)} %all-to-all-done.3.refs_1_) | copy-start | bytes 2359300

commit v6 on v5

--- a/solution.py
+++ b/solution.py
@@ -23,8 +23,7 @@
 SECOND = 2 * (SETS[1][1] - SETS[1][0]) * WIDTH
 PACK_2 = SECOND + 16
 EDGE = 2 * LANES + 8
-PARAMS = EDGE + 24
-WIDE = PARAMS + 32
+WIDE = EDGE + 32
 UNROLL = 2
 VMEM = 58 * 1024 * 1024
 
@@ -561,7 +560,7 @@
     def _():
         edges[...] = edges_in[...] if first else jnp.zeros_like(edges)
         token, place = iota((8, LANES), 0), iota((8, LANES), 1)
-        first_rows = zero_one((token < 3) & (place == token))
+        first_rows = zero_one((token >= 5) & (place == token - 5))
         last_rows = zero_one((token >= 5) & (place == token + LANES - 8))
 
         def lines_of(marker, tile):
@@ -705,10 +704,9 @@
 
 def finish_kernel(edges, from_prev, from_next, sums, _, out, lines, sem):
     for target in range(GROUP):
-        lines[target, :24, :] = jnp.zeros((24, LANES), f32)
-        lines[target, 24:, :] = sums[...]
-    lines[0, :24, :] = edges[0] + from_prev[...]
-    lines[GROUP - 1, :24, :] = edges[1] + from_next[...]
+        lines[target] = sums[...]
+    lines[0, :24, :] = sums[:24, :] + (edges[0] + from_prev[...])
+    lines[GROUP - 1, :24, :] = sums[:24, :] + (edges[1] + from_next[...])
     copy = pltpu.make_async_copy(lines, out.at[:, EDGE:WIDE, :], sem)
     copy.start()
     copy.wait()
@@ -747,7 +745,7 @@
                 group, at = channel // CH, channel % CH
                 offset = at % LANES
                 start = EDGE + at // LANES * 8
-                taps.append(wide[group, start + 24 : start + 32, offset : offset + WIDTH])
+                taps.append(wide[group, start : start + 8, offset : offset + WIDTH])
                 edge.append(wide[group, start : start + 8, offset : offset + WIDTH])
                 which, at = set_row(at, order)
                 pieces.append(sets[which][group, at : at + WIDTH, :])
@@ -758,7 +756,8 @@
                 taps_out[:, lanes] = taps[:4]
                 bias_out[:, lanes] = taps[4:5]
                 edge = jnp.concatenate(edge, axis=1)
-                head = jnp.where(at_start, jnp.concatenate([edge, blank], axis=0), flipped[:16])
+                first = jnp.concatenate([pltpu.roll(edge, 3, 0), blank], axis=0)
+                head = jnp.where(at_start, first, flipped[:16])
                 tail = jnp.where(
                     at_end, jnp.concatenate([blank, edge], axis=0), flipped[LANES - 16 :]
                 )

time: 198 us -> 195 us (0.985)
  blocking collectives: 39.4 us -> 37.3 us
    all_to_all x1, blocking collectives: 39.4 us -> 37.3 us  [exchange(): return lax.all_to_all(array, 'seq', 0, 0, axis_index_groups=Z_GROUPS)]
where the time goes in v6:
time: 195 us; the launch traced here: 194 us
  Pallas kernels  54.7 us (28%)
  starting transfers between devices  53.6 us (27%)
  blocking collectives  37.3 us (19%)
  waiting for transfers between devices  33.9 us (17%)
  local copies, waits for them, and re-layouts  9.16 us (5%)
  other arithmetic  4.74 us (2%)
    all_to_all x1, blocking collectives, exchange(): return lax.all_to_all(array, 'seq', 0, 0, axis_index_groups=Z_GROUPS)  37.3 us
    pallas_call x2, Pallas kernels, phase_two(): pl.pallas_call(functools.partial(phase_two_kernel, first, heads), name=f'...  29.9 us
    all_to_all x4, starting transfers between devices, exchange(): return lax.all_to_all(array, 'seq', 0, 0, axis_index_groups=Z_GROUPS)  24.4 us
    ppermute x2, waiting for transfers between devices, beside(): lax.ppermute(array, 'seq', [(i, i + by) for i in range(count) if 0 <= i +...  16.2 us
    pallas_call x2, Pallas kernels, phase_one(): pl.pallas_call(functools.partial(phase_one_kernel, first, heads), name=f'...  14.4 us
    ppermute x6, starting transfers between devices, cross_y(): lax.ppermute(jnp.where(run + shift < ROWS, up, down), 'seq', pairs)  11.5 us
    ppermute x7, waiting for transfers between devices, flip_bit(): return lax.ppermute(array, axis, [(i, i ^ bit) for i in range(count)])  9.96 us
    ppermute x7, starting transfers between devices, flip_bit(): return lax.ppermute(array, axis, [(i, i ^ bit) for i in range(count)])  7.68 us
  transfers between devices with their start and end apart: 21, of which 11 were waited for; matrix products, arithmetic and copies ran while one was open for 5% of the time, Pallas kernels for 24%

profile of v6, /device:TPU:6, one launch (start us, length us, event | category | flops | bytes accessed | tf_op | source)
XLA Modules:
  0.0 194.4 jit_solution(16912810297997706536)
XLA Ops:
  0.6 3.6 %pack.1 = (bf16[8,544,128]{2,1,0:T(8,128)(2,1)}, bf16[8,400,128]{2,1,0:T(8,128)(2,1)}) custom-call(s32[12]{0:T(128)} %comp_ref.1, bf16[128,2560]{1,0:T(8,128)(2,1)} %bitcast.40, bf16[128,2560]{1,0:T(8,128)(2,1)} %bitcast.41, bf16[128,128]{1,0:T(8,128)(2,1)} %bitcast.44, bf16[128,128]{1,0:T(8,128)(2,1)} %bitcast.45, f32[40,128]{1,0:T(8,128)} %bitcast.46, ...), custom_call_target="tpu_custom_call" | custom-call | tf_op jit(solution)/shard_map/pack/pallas_call | solution.py:132
  4.3 8.6 %all-to-all-start = ((bf16[8,544,128]{2,1,0:T(8,128)(2,1)}), bf16[8,544,128]{2,1,0:T(8,128)(2,1)S(1)}, u32[]{:S(2)}, u32[]{:S(2)}) async-start(bf16[8,544,128]{2,1,0:T(8,128)(2,1)} %get-tuple-element.60), calls=%async_computation | async-start | bytes 2228224 | tf_op jit(solution)/shard_map/all_to_all | solution.py:809
  13.0 0.1 concatenate.23
  13.2 0.1 concatenate.32
  13.3 0.1 concatenate.33
  13.4 0.1 concatenate.34
  13.5 0.1 copy.30
  13.6 0.1 fusion.7
  13.7 0.1 slice_bitcast_fusion.6
  13.8 0.7 pad.9.refs_2_
  14.5 0.2 slice_reduce_fusion
  14.7 0.8 slice_bitcast_fusion
  15.5 0.9 broadcast_in_dim.55.refs_1_.refs_3_
  16.3 1.0 broadcast_in_dim.56.refs_2_.refs_3_
  17.3 0.7 broadcast_in_dim.58.refs_3_.refs_4_
  18.0 0.7 broadcast_in_dim.60.refs_5_
  18.7 3.9 %collective-permute-start.5 = (bf16[8,2560]{1,0:T(8,128)(2,1)S(1)}, bf16[8,2560]{1,0:T(8,128)(2,1)S(1)}, u32[]{:S(2)}, u32[]{:S(2)}) collective-permute-start(bf16[8,2560]{1,0:T(8,128)(2,1)S(1)} %get-tuple-element.77), channel_id=1, source_target_pairs={{0,1},{1,2},{2,3},{3,4},{4,5},{5,6},{6,7},{7,8},{8,9},{9,10},{10,1... | collective-permute-start | bytes 122888 | tf_op jit(solution)/shard_map/ppermute | solution.py:824
  22.6 1.3 collective-permute-start.6
  23.9 13.0 %collective-permute-done.5.before_ref = bf16[8,2560]{1,0:T(8,128)(2,1)S(1)} collective-permute-done((bf16[8,2560]{1,0:T(8,128)(2,1)S(1)}, bf16[8,2560]{1,0:T(8,128)(2,1)S(1)}, u32[]{:S(2)}, u32[]{:S(2)}) %collective-permute-start.5) | collective-permute-done | bytes 40992 | tf_op jit(solution)/shard_map/ppermute | solution.py:824
  36.9 3.2 %collective-permute-done.6.after_ref = bf16[8,2560]{1,0:T(8,128)(2,1)S(1)} collective-permute-done((bf16[8,2560]{1,0:T(8,128)(2,1)S(1)}, bf16[8,2560]{1,0:T(8,128)(2,1)S(1)}, u32[]{:S(2)}, u32[]{:S(2)}) %collective-permute-start.6) | collective-permute-done | bytes 40992 | tf_op jit(solution)/shard_map/ppermute | solution.py:824
  40.0 0.6 copy-done.8
  40.7 1.5 rows_beside.1
  42.2 1.0 all-to-all-done.refs_0_.refs_1_.refs_2_
  43.2 4.8 %all-to-all-start.2 = ((bf16[8,400,128]{2,1,0:T(8,128)(2,1)}), bf16[8,400,128]{2,1,0:T(8,128)(2,1)S(1)}, u32[]{:S(2)}, u32[]{:S(2)}) async-start(bf16[8,400,128]{2,1,0:T(8,128)(2,1)} %rows_beside.1), calls=%async_computation.2 | async-start | bytes 1638400 | tf_op jit(solution)/shard_map/all_to_all | solution.py:809
  48.0 3.5 %collective-permute-start = (bf16[128,128]{1,0:T(8,128)(2,1)S(1)}, bf16[128,128]{1,0:T(8,128)(2,1)S(1)}, u32[]{:S(2)}, u32[]{:S(2)}) collective-permute-start(bf16[128,128]{1,0:T(8,128)(2,1)S(1)} %get-tuple-element.112), channel_id=1, source_target_pairs={{0,8},{1,9},{2,10},{3,11},{4,12},{5,13},{6,14},{7,15},{8,16},{9,17... | collective-permute-start | bytes 98312 | tf_op jit(solution)/shard_map/ppermute | solution.py:819
  51.5 1.3 collective-permute-start.1
  52.8 0.3 collective-permute-done.refs_4_.refs_18_
  53.1 4.2 %collective-permute-done.1.refs_5_.refs_19_ = bf16[128,128]{1,0:T(8,128)(2,1)S(1)} collective-permute-done((bf16[128,128]{1,0:T(8,128)(2,1)S(1)}, bf16[128,128]{1,0:T(8,128)(2,1)S(1)}, u32[]{:S(2)}, u32[]{:S(2)}) %collective-permute-start.1) | collective-permute-done | bytes 32800 | tf_op jit(solution)/shard_map/ppermute | solution.py:819
  57.3 0.6 copy-done.20
  57.9 6.5 %phase_one_0.1 = (f32[8,128,128]{2,1,0:T(8,128)}, f32[8,128,128]{2,1,0:T(8,128)}, f32[8,128,128]{2,1,0:T(8,128)}, f32[8,128,128]{2,1,0:T(8,128)}, f32[8,128,128]...) custom-call(bf16[8,544,128]{2,1,0:T(8,128)(2,1)} %copy-done.2, ...), custom_call_target="tpu_custom_call" | custom-call | flops 8000000000 | bytes 8000000 | tf_op jit(solution)/shard_map/phase_one_0/pallas_call | solution.py:355
  64.5 1.0 broadcast_select_fusion.3
  65.5 1.7 collective-permute-start.2
  67.2 1.4 collective-permute-start.3
  68.6 2.5 %collective-permute-start.4 = (f32[272,128]{1,0:T(8,128)S(1)}, f32[272,128]{1,0:T(8,128)S(1)}, u32[]{:S(2)}, u32[]{:S(2)}) collective-permute-start(f32[272,128]{1,0:T(8,128)S(1)} %get-tuple-element.118), channel_id=1, source_target_pairs={{0,24},{1,25},{2,26},{3,27},{4,28},{5,29},{6,30},{7,31},{8,0},{9,1... | collective-permute-start | bytes 417800 | tf_op jit(solution)/shard_map/ppermute | solution.py:833
  71.1 0.9 all-to-all-done.2.refs_1_.refs_2_
  72.0 0.9 copy-done.3
  72.9 7.8 %phase_one_1.1 = (f32[8,192,128]{2,1,0:T(8,128)}, f32[8,192,128]{2,1,0:T(8,128)}, f32[8,192,128]{2,1,0:T(8,128)}, f32[8,192,128]{2,1,0:T(8,128)}, f32[8,192,128]...) custom-call(bf16[8,544,128]{2,1,0:T(8,128)(2,1)} %copy-done.2, ...), custom_call_target="tpu_custom_call" | custom-call | flops 12000000000 | bytes 8000000 | tf_op jit(solution)/shard_map/phase_one_1/pallas_call | solution.py:355
  80.7 1.1 broadcast_select_fusion
  81.8 1.7 collective-permute-start.7
  83.5 2.9 %collective-permute-start.8 = (f32[400,128]{1,0:T(8,128)S(1)}, f32[400,128]{1,0:T(8,128)S(1)}, u32[]{:S(2)}, u32[]{:S(2)}) collective-permute-start(f32[400,128]{1,0:T(8,128)S(1)} %get-tuple-element.116), channel_id=1, source_target_pairs={{0,16},{1,17},{2,18},{3,19},{4,20},{5,21},{6,22},{7,23},{8,24},{9,... | collective-permute-start | bytes 614408 | tf_op jit(solution)/shard_map/ppermute | solution.py:833
  86.4 1.3 collective-permute-start.9
  87.7 0.6 copy-done.17
  88.4 13.1 %phase_two_0.1 = (bf16[8,256,128]{2,1,0:T(8,128)(2,1)}, f32[8,296,128]{2,1,0:T(8,128)}, f32[4,24,128]{2,1,0:T(8,128)}, f32[32,128]{1,0:T(8,128)}) custom-call(s32[1]{0:T(128)} %bitcast.1.refs_0_, bf16[8,544,128]{2,1,0:T(8,128)(2,1)} %copy-done.2, bf16[8,544,128]{2,1,0:T(8,128)(2,1)} %copy-done.2, f32[5,128,128]{2,1,0:T(8,128)} %broadcast_in_dim.55.refs_1_.refs_3_, ...), custom_call_target="tpu_custom_call" | custom-call | flops 16000000000 | bytes 8000000 | tf_op jit(solution)/shard_map/phase_two_0/pallas_call | solution.py:674
  101.5 3.8 %all-to-all-start.1 = ((bf16[8,256,128]{2,1,0:T(8,128)(2,1)}), bf16[8,256,128]{2,1,0:T(8,128)(2,1)S(1)}, u32[]{:S(2)}, u32[]{:S(2)}) async-start(bf16[8,256,128]{2,1,0:T(8,128)(2,1)} %get-tuple-element.76), calls=%async_computation.1 | async-start | bytes 1048576 | tf_op jit(solution)/shard_map/all_to_all | solution.py:809
  105.4 0.6 copy-done.13
  106.2 16.8 %phase_two_1.1 = (bf16[8,384,128]{2,1,0:T(8,128)(2,1)}, f32[8,296,128]{2,1,0:T(8,128)}, f32[4,24,128]{2,1,0:T(8,128)}, f32[32,128]{1,0:T(8,128)}) custom-call(s32[1]{0:T(128)} %bitcast.1.refs_0_, bf16[8,544,128]{2,1,0:T(8,128)(2,1)} %copy-done.2, bf16[8,400,128]{2,1,0:T(8,128)(2,1)} %copy-done.3, f32[5,192,128]{2,1,0:T(8,128)} %broadcast_in_dim.56.refs_2_.refs_3_, ...), custom_call_target="tpu_custom_call" | custom-call | flops 24000000000 | bytes 8000000 | tf_op jit(solution)/shard_map/phase_two_1/pallas_call | solution.py:674
  123.1 7.2 %all-to-all-start.3 = ((bf16[8,384,128]{2,1,0:T(8,128)(2,1)}), bf16[8,384,128]{2,1,0:T(8,128)(2,1)S(1)}, u32[]{:S(2)}, u32[]{:S(2)}) async-start(bf16[8,384,128]{2,1,0:T(8,128)(2,1)} %get-tuple-element.94), calls=%async_computation.3 | async-start | bytes 1572864 | tf_op jit(solution)/shard_map/all_to_all | solution.py:809
  130.3 0.9 collective-permute-start.10
  131.2 2.6 %collective-permute-start.11 = (f32[80,128]{1,0:T(8,128)S(1)}, f32[80,128]{1,0:T(8,128)S(1)}, u32[]{:S(2)}, u32[]{:S(2)}) collective-permute-start(f32[80,128]{1,0:T(8,128)S(1)} %pad_maximum_fusion), channel_id=1, source_target_pairs={{0,24},{1,25},{2,26},{3,27},{4,28},{5,29},{6,30},{7,31},{8,16},{9,... | collective-permute-start | bytes 122888 | tf_op jit(solution)/shard_map/ppermute | solution.py:839
  133.8 0.7 collective-permute-start.12
  134.5 4.6 %collective-permute-done.12 = f32[32,128]{1,0:T(8,128)S(1)} collective-permute-done((f32[32,128]{1,0:T(8,128)S(1)}, f32[32,128]{1,0:T(8,128)S(1)}, u32[]{:S(2)}, u32[]{:S(2)}) %collective-permute-start.12) | collective-permute-done | bytes 16416 | tf_op jit(solution)/shard_map/ppermute | solution.py:839
  139.1 0.9 collective-permute-start.14
  140.0 1.3 collective-permute-start.13
  141.3 1.6 collective-permute-done.14
  142.9 0.4 collective-permute-done.15
  143.3 1.3 collective-permute-start.16
  144.5 0.6 fusion.1
  145.1 3.4 %collective-permute-done.16 = f32[32,128]{1,0:T(8,128)S(1)} collective-permute-done((f32[32,128]{1,0:T(8,128)S(1)}, f32[32,128]{1,0:T(8,128)S(1)}, u32[]{:S(2)}, u32[]{:S(2)}) %collective-permute-start.16) | collective-permute-done | bytes 16416 | tf_op jit(solution)/shard_map/ppermute | solution.py:839
  148.6 0.6 add.63.sums
  149.2 1.5 finish.1
  150.7 1.3 all-to-all-done.3.refs_1_
  152.0 37.3 %all_to_all.25.refs_2_ = f32[8,296,128]{2,1,0:T(8,128)} all-to-all(f32[8,296,128]{2,1,0:T(8,128)} %finish.1), channel_id=1, replica_groups={{0,1,2,3,4,5,6,7},{8,9,10,11,12,13,14,15},{16,17,18,19,20,21,22,23},{24..., dimensions={0} | all-to-all | bytes 2424832 | tf_op jit(solution)/shard_map/all_to_all | solution.py:809
  189.3 3.7 %unpack.1 = (bf16[128,2560]{1,0:T(8,128)(2,1)}, bf16[128,2560]{1,0:T(8,128)(2,1)}, f32[128,128]{1,0:T(8,128)}, f32[128,128]{1,0:T(8,128)}, f32[40,128]{1,0:T(8,1...) custom-call(s32[1]{0:T(128)} %bitcast.place_z, ...), custom_call_target="tpu_custom_call" | custom-call | tf_op jit(solution)/shard_map/unpack/pallas_call | solution.py:794
  193.1 1.3 reduce.2
  (62 shorter events, 0.5 us)
Async XLA Ops:
  4.3 8.7 %copy-start.6 = (f32[4,2560]{1,0:T(4,128)S(1)}, f32[4,2560]{1,0:T(4,128)}, u32[]{:S(2)}) copy-start(f32[4,2560]{1,0:T(4,128)} %param.23) | copy-start | bytes 122884
  4.3 8.8 %copy-start.9 = (f32[2560]{0:T(1024)S(1)}, f32[2560]{0:T(1024)}, u32[]{:S(2)}) copy-start(f32[2560]{0:T(1024)} %param.24) | copy-start | bytes 30724
  4.3 8.9 %copy-start.21 = (f32[40]{0:T(128)S(1)}, f32[40]{0:T(128)}, u32[]{:S(2)}) copy-start(f32[40]{0:T(128)} %param.19) | copy-start | bytes 484
  4.3 9.0 %copy-start.11 = (f32[40]{0:T(128)S(1)}, f32[40]{0:T(128)}, u32[]{:S(2)}) copy-start(f32[40]{0:T(128)} %param.20) | copy-start | bytes 484
  4.3 9.1 %copy-start.12 = (f32[40]{0:T(128)S(1)}, f32[40]{0:T(128)}, u32[]{:S(2)}) copy-start(f32[40]{0:T(128)} %param.21) | copy-start | bytes 484
  4.3 9.2 %copy-start.10 = (f32[12,40]{1,0:T(8,128)S(1)}, f32[12,40]{1,0:T(8,128)}, u32[]{:S(2)}) copy-start(f32[12,40]{1,0:T(8,128)} %param.22) | copy-start | bytes 5764
  4.3 38.9 %all-to-all-start = ((bf16[8,544,128]{2,1,0:T(8,128)(2,1)}), bf16[8,544,128]{2,1,0:T(8,128)(2,1)S(1)}, u32[]{:S(2)}, u32[]{:S(2)}) async-start(bf16[8,544,128]{2,1,0:T(8,128)(2,1)} %get-tuple-element.60), calls=%async_computation | async-start | bytes 2228224 | tf_op jit(solution)/shard_map/all_to_all | solution.py:809
  18.7 18.2 %collective-permute-start.5 = (bf16[8,2560]{1,0:T(8,128)(2,1)S(1)}, bf16[8,2560]{1,0:T(8,128)(2,1)S(1)}, u32[]{:S(2)}, u32[]{:S(2)}) collective-permute-start(bf16[8,2560]{1,0:T(8,128)(2,1)S(1)} %get-tuple-element.77), channel_id=1, source_target_pairs={{0,1},{1,2},{2,3},{3,4},{4,5},{5,6},{6,7},{7,8},{8,9},{9,10},{10,1... | collective-permute-start | bytes 122888 | tf_op jit(solution)/shard_map/ppermute | solution.py:824
  22.6 17.5 %collective-permute-start.6 = (bf16[8,2560]{1,0:T(8,128)(2,1)S(1)}, bf16[8,2560]{1,0:T(8,128)(2,1)S(1)}, u32[]{:S(2)}, u32[]{:S(2)}) collective-permute-start(bf16[8,2560]{1,0:T(8,128)(2,1)S(1)} %get-tuple-element.78), channel_id=1, source_target_pairs={{1,0},{2,1},{3,2},{4,3},{5,4},{6,5},{7,6},{8,7},{9,8},{10,9},{11,1... | collective-permute-start | bytes 122888 | tf_op jit(solution)/shard_map/ppermute | solution.py:824
  36.8 3.2 %copy-start.7 = (bf16[8,2560]{1,0:T(8,128)(2,1)}, bf16[8,2560]{1,0:T(8,128)(2,1)S(1)}, u32[]{:S(2)}) copy-start(bf16[8,2560]{1,0:T(8,128)(2,1)S(1)} %collective-permute-done.5.before_ref) | copy-start | bytes 122884
  40.0 0.6 copy-start.8
  43.2 14.1 %copy-start.2 = (bf16[8,544,128]{2,1,0:T(8,128)(2,1)}, bf16[8,544,128]{2,1,0:T(8,128)(2,1)S(1)}, u32[]{:S(2)}) copy-start(bf16[8,544,128]{2,1,0:T(8,128)(2,1)S(1)} %all-to-all-done.refs_0_.refs_1_.refs_2_) | copy-start | bytes 3342340
  43.2 28.8 %all-to-all-start.2 = ((bf16[8,400,128]{2,1,0:T(8,128)(2,1)}), bf16[8,400,128]{2,1,0:T(8,128)(2,1)S(1)}, u32[]{:S(2)}, u32[]{:S(2)}) async-start(bf16[8,400,128]{2,1,0:T(8,128)(2,1)} %rows_beside.1), calls=%async_computation.2 | async-start | bytes 1638400 | tf_op jit(solution)/shard_map/all_to_all | solution.py:809
  48.0 5.1 %collective-permute-start = (bf16[128,128]{1,0:T(8,128)(2,1)S(1)}, bf16[128,128]{1,0:T(8,128)(2,1)S(1)}, u32[]{:S(2)}, u32[]{:S(2)}) collective-permute-start(bf16[128,128]{1,0:T(8,128)(2,1)S(1)} %get-tuple-element.112), channel_id=1, source_target_pairs={{0,8},{1,9},{2,10},{3,11},{4,12},{5,13},{6,14},{7,15},{8,16},{9,17... | collective-permute-start | bytes 98312 | tf_op jit(solution)/shard_map/ppermute | solution.py:819
  51.5 5.8 %collective-permute-start.1 = (bf16[128,128]{1,0:T(8,128)(2,1)S(1)}, bf16[128,128]{1,0:T(8,128)(2,1)S(1)}, u32[]{:S(2)}, u32[]{:S(2)}) collective-permute-start(bf16[128,128]{1,0:T(8,128)(2,1)S(1)} %get-tuple-element.111), channel_id=1, source_target_pairs={{8,0},{9,1},{10,2},{11,3},{12,4},{13,5},{14,6},{15,7},{16,8},{17,9... | collective-permute-start | bytes 98312 | tf_op jit(solution)/shard_map/ppermute | solution.py:819
  53.1 4.2 %copy-start.19 = (bf16[128,128]{1,0:T(8,128)(2,1)}, bf16[128,128]{1,0:T(8,128)(2,1)S(1)}, u32[]{:S(2)}) copy-start(bf16[128,128]{1,0:T(8,128)(2,1)S(1)} %collective-permute-done.refs_4_.refs_18_) | copy-start | bytes 98308
  57.3 0.6 copy-start.20
  65.5 20.9 %collective-permute-start.2 = (f32[272,128]{1,0:T(8,128)S(1)}, f32[272,128]{1,0:T(8,128)S(1)}, u32[]{:S(2)}, u32[]{:S(2)}) collective-permute-start(f32[272,128]{1,0:T(8,128)S(1)} %get-tuple-element.120), channel_id=1, source_target_pairs={{0,8},{1,9},{2,10},{3,11},{4,12},{5,13},{6,14},{7,15},{8,16},{9,17... | collective-permute-start | bytes 417800 | tf_op jit(solution)/shard_map/ppermute | solution.py:833
  67.2 20.6 %collective-permute-start.3 = (f32[272,128]{1,0:T(8,128)S(1)}, f32[272,128]{1,0:T(8,128)S(1)}, u32[]{:S(2)}, u32[]{:S(2)}) collective-permute-start(f32[272,128]{1,0:T(8,128)S(1)} %get-tuple-element.119), channel_id=1, source_target_pairs={{0,16},{1,17},{2,18},{3,19},{4,20},{5,21},{6,22},{7,23},{8,24},{9,... | collective-permute-start | bytes 417800 | tf_op jit(solution)/shard_map/ppermute | solution.py:833
  68.6 19.1 %collective-permute-start.4 = (f32[272,128]{1,0:T(8,128)S(1)}, f32[272,128]{1,0:T(8,128)S(1)}, u32[]{:S(2)}, u32[]{:S(2)}) collective-permute-start(f32[272,128]{1,0:T(8,128)S(1)} %get-tuple-element.118), channel_id=1, source_target_pairs={{0,24},{1,25},{2,26},{3,27},{4,28},{5,29},{6,30},{7,31},{8,0},{9,1... | collective-permute-start | bytes 417800 | tf_op jit(solution)/shard_map/ppermute | solution.py:833
  72.0 0.9 copy-start.3
  81.8 23.5 %collective-permute-start.7 = (f32[400,128]{1,0:T(8,128)S(1)}, f32[400,128]{1,0:T(8,128)S(1)}, u32[]{:S(2)}, u32[]{:S(2)}) collective-permute-start(f32[400,128]{1,0:T(8,128)S(1)} %get-tuple-element.117), channel_id=1, source_target_pairs={{0,8},{1,9},{2,10},{3,11},{4,12},{5,13},{6,14},{7,15},{8,16},{9,17... | collective-permute-start | bytes 614408 | tf_op jit(solution)/shard_map/ppermute | solution.py:833
  83.5 21.9 %collective-permute-start.8 = (f32[400,128]{1,0:T(8,128)S(1)}, f32[400,128]{1,0:T(8,128)S(1)}, u32[]{:S(2)}, u32[]{:S(2)}) collective-permute-start(f32[400,128]{1,0:T(8,128)S(1)} %get-tuple-element.116), channel_id=1, source_target_pairs={{0,16},{1,17},{2,18},{3,19},{4,20},{5,21},{6,22},{7,23},{8,24},{9,... | collective-permute-start | bytes 614408 | tf_op jit(solution)/shard_map/ppermute | solution.py:833
  86.4 1.4 copy-start.16
  86.4 19.0 %collective-permute-start.9 = (f32[400,128]{1,0:T(8,128)S(1)}, f32[400,128]{1,0:T(8,128)S(1)}, u32[]{:S(2)}, u32[]{:S(2)}) collective-permute-start(f32[400,128]{1,0:T(8,128)S(1)} %get-tuple-element.115), channel_id=1, source_target_pairs={{0,24},{1,25},{2,26},{3,27},{4,28},{5,29},{6,30},{7,31},{8,0},{9,1... | collective-permute-start | bytes 614408 | tf_op jit(solution)/shard_map/ppermute | solution.py:833
  87.7 0.7 copy-start.17
  87.7 0.7 copy-start.18
  101.5 21.5 %all-to-all-start.1 = ((bf16[8,256,128]{2,1,0:T(8,128)(2,1)}), bf16[8,256,128]{2,1,0:T(8,128)(2,1)S(1)}, u32[]{:S(2)}, u32[]{:S(2)}) async-start(bf16[8,256,128]{2,1,0:T(8,128)(2,1)} %get-tuple-element.76), calls=%async_computation.1 | async-start | bytes 1048576 | tf_op jit(solution)/shard_map/all_to_all | solution.py:809
  105.3 0.7 copy-start.13
  105.4 0.7 copy-start.14
  105.4 0.8 copy-start.15
  123.0 7.3 %copy-start.4 = (f32[4,24,128]{2,1,0:T(8,128)S(1)}, f32[4,24,128]{2,1,0:T(8,128)}, u32[]{:S(2)}) copy-start(f32[4,24,128]{2,1,0:T(8,128)} %get-tuple-element.95.edges) | copy-start | bytes 147460
  123.0 7.3 %copy-start.5 = (f32[32,128]{1,0:T(8,128)S(1)}, f32[32,128]{1,0:T(8,128)}, u32[]{:S(2)}) copy-start(f32[32,128]{1,0:T(8,128)} %get-tuple-element.96) | copy-start | bytes 49156
  123.0 27.7 %copy-start.1 = (bf16[8,256,128]{2,1,0:T(8,128)(2,1)}, bf16[8,256,128]{2,1,0:T(8,128)(2,1)S(1)}, u32[]{:S(2)}) copy-start(bf16[8,256,128]{2,1,0:T(8,128)(2,1)S(1)} %all-to-all-done.1.refs_0_) | copy-start | bytes 1572868
  123.1 29.0 %all-to-all-start.3 = ((bf16[8,384,128]{2,1,0:T(8,128)(2,1)}), bf16[8,384,128]{2,1,0:T(8,128)(2,1)S(1)}, u32[]{:S(2)}, u32[]{:S(2)}) async-start(bf16[8,384,128]{2,1,0:T(8,128)(2,1)} %get-tuple-element.94), calls=%async_computation.3 | async-start | bytes 1572864 | tf_op jit(solution)/shard_map/all_to_all | solution.py:809
  130.3 8.7 %collective-permute-start.10 = (f32[80,128]{1,0:T(8,128)S(1)}, f32[80,128]{1,0:T(8,128)S(1)}, u32[]{:S(2)}, u32[]{:S(2)}) collective-permute-start(f32[80,128]{1,0:T(8,128)S(1)} %pad_maximum_fusion), channel_id=1, source_target_pairs={{0,8},{1,9},{2,10},{3,11},{4,12},{5,13},{6,14},{7,15},{8,0},{9,1},... | collective-permute-start | bytes 122888 | tf_op jit(solution)/shard_map/ppermute | solution.py:839
  131.2 7.8 %collective-permute-start.11 = (f32[80,128]{1,0:T(8,128)S(1)}, f32[80,128]{1,0:T(8,128)S(1)}, u32[]{:S(2)}, u32[]{:S(2)}) collective-permute-start(f32[80,128]{1,0:T(8,128)S(1)} %pad_maximum_fusion), channel_id=1, source_target_pairs={{0,24},{1,25},{2,26},{3,27},{4,28},{5,29},{6,30},{7,31},{8,16},{9,... | collective-permute-start | bytes 122888 | tf_op jit(solution)/shard_map/ppermute | solution.py:839
  133.8 5.2 %collective-permute-start.12 = (f32[32,128]{1,0:T(8,128)S(1)}, f32[32,128]{1,0:T(8,128)S(1)}, u32[]{:S(2)}, u32[]{:S(2)}) collective-permute-start(f32[32,128]{1,0:T(8,128)S(1)} %copy-done.5), channel_id=1, source_target_pairs={{0,16},{1,17},{2,18},{3,19},{4,20},{5,21},{6,22},{7,23},{8,24},{9,... | collective-permute-start | bytes 49160 | tf_op jit(solution)/shard_map/ppermute | solution.py:839
  139.1 3.8 %collective-permute-start.14 = (f32[32,128]{1,0:T(8,128)S(1)}, f32[32,128]{1,0:T(8,128)S(1)}, u32[]{:S(2)}, u32[]{:S(2)}) collective-permute-start(f32[32,128]{1,0:T(8,128)S(1)} %fusion), channel_id=1, source_target_pairs={{0,64},{32,96},{64,0},{96,32},{128,192},{160,224},{192,128},{224,1... | collective-permute-start | bytes 49160 | tf_op jit(solution)/shard_map/ppermute | solution.py:839
  140.0 3.2 %collective-permute-start.15 = (f32[32,128]{1,0:T(8,128)S(1)}, f32[32,128]{1,0:T(8,128)S(1)}, u32[]{:S(2)}, u32[]{:S(2)}) collective-permute-start(f32[32,128]{1,0:T(8,128)S(1)} %fusion), channel_id=1, source_target_pairs={{0,96},{32,64},{64,32},{96,0},{128,224},{160,192},{192,160},{224,1... | collective-permute-start | bytes 49160 | tf_op jit(solution)/shard_map/ppermute | solution.py:839
  140.0 3.2 %collective-permute-start.13 = (f32[32,128]{1,0:T(8,128)S(1)}, f32[32,128]{1,0:T(8,128)S(1)}, u32[]{:S(2)}, u32[]{:S(2)}) collective-permute-start(f32[32,128]{1,0:T(8,128)S(1)} %fusion), channel_id=1, source_target_pairs={{0,32},{32,0},{64,96},{96,64},{128,160},{160,128},{192,224},{224,1... | collective-permute-start | bytes 49160 | tf_op jit(solution)/shard_map/ppermute | solution.py:839
  143.3 5.3 %collective-permute-start.16 = (f32[32,128]{1,0:T(8,128)S(1)}, f32[32,128]{1,0:T(8,128)S(1)}, u32[]{:S(2)}, u32[]{:S(2)}) collective-permute-start(f32[32,128]{1,0:T(8,128)S(1)} %add_add_fusion), channel_id=1, source_target_pairs={{0,128},{32,160},{64,192},{96,224},{128,0},{160,32},{192,64},{224,... | collective-permute-start | bytes 49160 | tf_op jit(solution)/shard_map/ppermute | solution.py:839
  152.0 37.3 %copy-start = (bf16[8,384,128]{2,1,0:T(8,128)(2,1)}, bf16[8,384,128]{2,1,0:T(8,128)(2,1)S(1)}, u32[]{:S(2)}) copy-start(bf16[8,384,128]{2,1,0:T(8,128)(2,1)S(1)} %all-to-all-done.3.refs_1_) | copy-start | bytes 2359300
